TPU v7x, 128 devices: a whole 4x4x4 slice. The times are simulated.
128 devices in a mesh: tok: 4 (over x_lo, core), voc: 32 (over x_hi, z, y).
Axes of the slice: x: 4 (x_hi: 2, x_lo: 2; x = x_hi * 2 + x_lo), y: 4, z: 4, core: 2. Of those that a mesh axis runs over, the one named last changes fastest.
Arguments:
- hidden: bfloat16 [32768, 5120], P('tok', 'voc'), may hold values from -240 to 240
- head_weight: bfloat16 [98304, 5120], P(('tok', 'voc')), may hold values from -0.25 to 0.25
- tile_owners: int32 [8192, 2], P(('tok', 'voc')), may hold values from 0 to 127, all different within a row; in each aligned block of 64 rows (0 to 63, 64 to 127, ...) at most 2 rows name the same one
- cand_pos: int32 [32768, 64], P(('tok', 'voc')), may hold values from 0 to 1535, as said below
- teacher_logp: float32 [32768, 64], P(('tok', 'voc')), may hold values from -16 to -2
Outputs:
- token_loss: float32 [32768], P(('tok', 'voc'))
- grad_hidden: bfloat16 [32768, 5120], P(('tok', 'voc'))
- grad_head: bfloat16 [98304, 5120], P(('tok', 'voc'))
Inputs may be any that keep to these rules, and one draw needn't show every extreme that they name: `tile_owners`: the 2 panels of a tile are distinct. Among the tiles of one device no panel is named more than 2 times, a bound that some block reaches. `cand_pos`: the 64 entries of a row are distinct.
All inputs are finite; a program needn't handle non-finite values.
Results may differ from a plain program's by a relative error of at most 0.013.
Values may be sent and summed in bfloat16 or wider, within the bound.
No kernel may reach another device: no remote copies, remote signals or barrier semaphores. Data moves between devices by JAX's collectives and lax.ppermute only.
A program may use at most 192 MiB of HBM per device.

v0:
```python
import jax
import jax.numpy as jnp
from jax import lax
from jax.sharding import PartitionSpec as P

loss_weight = 16.0


def spread(table, values, highest):
    return lax.dot_general(
        table,
        values,
        (((0,), (0,)), ((), ())),
        preferred_element_type=jnp.float32,
        precision=lax.Precision.HIGHEST if highest else None,
    )


def collect(table, values, highest):
    return jnp.dot(
        table,
        values,
        preferred_element_type=jnp.float32,
        precision=lax.Precision.HIGHEST if highest else None,
    )


def placement_tables(tile_owners, owner_count, capacity):
    tile_count, group_count = tile_owners.shape
    flat_owners = tile_owners.reshape(-1)
    entry_count = flat_owners.shape[0]
    target = (flat_owners[:, None] == jnp.arange(owner_count, dtype=jnp.int32)[None, :]).astype(
        jnp.float32
    )
    steps = jnp.arange(entry_count, dtype=jnp.int32)
    lower = (steps[:, None] > steps[None, :]).astype(jnp.float32)
    earlier = jnp.dot(
        lower, target, preferred_element_type=jnp.float32, precision=lax.Precision.HIGHEST
    )
    rank_in = jnp.sum(earlier * target, axis=1).astype(jnp.int32)
    slot_index = flat_owners * capacity + rank_in
    placement = (
        slot_index[:, None] == jnp.arange(owner_count * capacity, dtype=jnp.int32)[None, :]
    ).astype(jnp.float32)
    tile_placement = jnp.sum(
        placement.reshape(tile_count, group_count, owner_count * capacity), axis=1
    )
    return (placement, tile_placement)


def blocked_rows():
    return 64


def pick_columns(scores, columns):
    total_rows, panel_rows = scores.shape
    block = blocked_rows()
    vocab_index = jnp.arange(panel_rows, dtype=jnp.int32)

    def pick_one_block(pieces):
        score_block, column_block = pieces
        match = column_block[:, :, None] == vocab_index[None, None, :]
        return jnp.sum(jnp.where(match, score_block[:, None, :], 0.0), axis=2)

    picked = lax.map(
        pick_one_block,
        (
            scores.reshape(total_rows // block, block, panel_rows),
            columns.reshape(total_rows // block, block, columns.shape[1]),
        ),
    )
    return picked.reshape(total_rows, columns.shape[1])


def place_columns(values, columns, panel_rows):
    total_rows, pick_count = values.shape
    block = blocked_rows()
    vocab_index = jnp.arange(panel_rows, dtype=jnp.int32)

    def place_one_block(pieces):
        value_block, column_block = pieces
        match = column_block[:, :, None] == vocab_index[None, None, :]
        return jnp.sum(jnp.where(match, value_block[:, :, None], 0.0), axis=1).astype(jnp.bfloat16)

    dense = lax.map(
        place_one_block,
        (
            values.reshape(total_rows // block, block, pick_count),
            columns.reshape(total_rows // block, block, pick_count),
        ),
    )
    return dense.reshape(total_rows, panel_rows)


def body(hidden, head_weight, tile_owners, cand_pos, teacher_logp):
    own_rows = lax.all_to_all(hidden, "voc", split_axis=0, concat_axis=1, tiled=True)
    tok_count, width = own_rows.shape
    panel_rows = head_weight.shape[0]
    owner_count = lax.axis_size(("tok", "voc"))
    tile_count, group_count = tile_owners.shape
    per_tile = tok_count // tile_count
    pick_count = cand_pos.shape[1]
    capacity = max(2, 2 * group_count * tile_count // owner_count)
    slot_count = owner_count * capacity
    placement, tile_placement = placement_tables(tile_owners, owner_count, capacity)
    tile_bf16 = tile_placement.astype(jnp.bfloat16)
    send_rows = spread(tile_bf16, own_rows.reshape(tile_count, per_tile * width), False).astype(
        jnp.bfloat16
    )
    cand_group = (cand_pos // panel_rows).reshape(tile_count, per_tile, pick_count)
    cand_local = (cand_pos % panel_rows).reshape(tile_count, per_tile, pick_count)
    pair_cols = jnp.stack(
        [jnp.where(cand_group == slot_group, cand_local, -1) for slot_group in range(group_count)],
        axis=1,
    )
    pair_cols = pair_cols.reshape(tile_count * group_count, per_tile * pick_count)
    send_cols = (spread(placement, (pair_cols + 1).astype(jnp.float32), True) - 1.0).astype(
        jnp.int32
    )
    got_rows, got_cols = (
        lax.all_to_all(
            send_rows.reshape(owner_count, capacity, per_tile * width),
            ("tok", "voc"),
            split_axis=0,
            concat_axis=0,
            tiled=True,
        ),
        lax.all_to_all(
            send_cols.reshape(owner_count, capacity, per_tile * pick_count),
            ("tok", "voc"),
            split_axis=0,
            concat_axis=0,
            tiled=True,
        ),
    )
    got_rows = got_rows.reshape(slot_count * per_tile, width)
    got_cols = got_cols.reshape(slot_count * per_tile, pick_count)
    scores = lax.dot_general(
        got_rows, head_weight, (((1,), (1,)), ((), ())), preferred_element_type=jnp.float32
    )
    picked = pick_columns(scores, got_cols)
    returned = lax.all_to_all(
        picked.reshape(slot_count, per_tile * pick_count),
        ("tok", "voc"),
        split_axis=0,
        concat_axis=0,
        tiled=True,
    )
    cand_logit = collect(tile_placement, returned, True).reshape(tok_count, pick_count)
    row_max = jnp.max(cand_logit, axis=1, keepdims=True)
    log_total = row_max + jnp.log(jnp.sum(jnp.exp(cand_logit - row_max), axis=1, keepdims=True))
    target = jnp.exp(teacher_logp)
    teacher_mass = jnp.sum(target, axis=1, keepdims=True)
    token_loss = jnp.sum(target * (teacher_logp - cand_logit + log_total), axis=1)
    weights = (loss_weight * (teacher_mass * jnp.exp(cand_logit - log_total) - target)).astype(
        jnp.bfloat16
    )
    outgoing = spread(tile_bf16, weights.reshape(tile_count, per_tile * pick_count), False).astype(
        jnp.bfloat16
    )
    got_weights = lax.all_to_all(
        outgoing, ("tok", "voc"), split_axis=0, concat_axis=0, tiled=True
    ).reshape(slot_count * per_tile, pick_count)
    dense_weights = place_columns(got_weights.astype(jnp.float32), got_cols, panel_rows)
    grad_head = lax.dot_general(
        dense_weights, got_rows, (((0,), (0,)), ((), ())), preferred_element_type=jnp.float32
    ).astype(jnp.bfloat16)
    grad_parts = jnp.dot(dense_weights, head_weight, preferred_element_type=jnp.float32).astype(
        jnp.bfloat16
    )
    home_parts = lax.all_to_all(
        grad_parts.reshape(owner_count, capacity, per_tile * width),
        ("tok", "voc"),
        split_axis=0,
        concat_axis=0,
        tiled=True,
    )
    home_parts = home_parts.reshape(slot_count, per_tile * width)
    grad_hidden = (
        collect(tile_bf16, home_parts, False).astype(jnp.bfloat16).reshape(tok_count, width)
    )
    return (token_loss, grad_hidden, grad_head)


def solution(mesh):
    placed = (
        P("tok", "voc"),
        P(("tok", "voc"), None),
        P(("tok", "voc"), None),
        P(("tok", "voc"), None),
        P(("tok", "voc"), None),
    )
    return jax.shard_map(
        body,
        mesh=mesh,
        in_specs=placed,
        out_specs=(P(("tok", "voc")), P(("tok", "voc"), None), P(("tok", "voc"), None)),
        check_vma=False,
    )
```

profile of v0, /device:TPU:97, one launch (start us, length us, event | category | flops | bytes accessed | tf_op | source)
XLA Modules:
  0.0 618.5 jit_solution(8756282257830699632)
XLA Ops:
  0.7 3.6 copy.70
  4.2 9.2 %all-to-all-start.1 = ((bf16[32,256,160]{1,2,0:T(8,128)(2,1)}), bf16[32,256,160]{1,2,0:T(8,128)(2,1)S(1)}, u32[]{:S(2)}, u32[]{:S(2)}) async-start(bf16[32,256,160]{1,2,0:T(8,128)(2,1)} %bitcast.47), calls=%async_computation.1 | async-start | bytes 5242880 | tf_op jit(solution)/shard_map/all_to_all | solution.py:96
  16.2 29.4 %all-to-all-done.1 = bf16[32,256,160]{1,2,0:T(8,128)(2,1)S(1)} async-done(((bf16[32,256,160]{1,2,0:T(8,128)(2,1)}), bf16[32,256,160]{1,2,0:T(8,128)(2,1)S(1)}, u32[]{:S(2)}, u32[]{:S(2)}) %all-to-all-start.1) | async-done | bytes 2621472 | tf_op jit(solution)/shard_map/all_to_all | solution.py:96
  45.5 10.1 %all-to-all-start = ((s32[128,2,256]{2,1,0:T(2,128)}), s32[128,2,256]{2,1,0:T(2,128)S(1)}, u32[]{:S(2)}, u32[]{:S(2)}) async-start(s32[128,2,256]{2,1,0:T(2,128)} %reshape.158), calls=%async_computation | async-start | bytes 524288 | tf_op jit(solution)/shard_map/all_to_all | solution.py:128
  55.7 5.4 copy.66
  61.1 8.6 %reshape.159 = bf16[64,20480]{1,0:T(8,128)(2,1)S(1)} reshape(bf16[256,32,160]{2,1,0:T(8,128)(2,1)} %copy.66) | data formatting | bytes 5242880 | tf_op jit(solution)/shard_map/reshape | solution.py:107
  69.7 5.4 convolution_convert_fusion
  75.2 15.5 %reshape.160 = bf16[128,2,20480]{2,1,0:T(2,128)(2,1)} reshape(bf16[256,20480]{1,0:T(8,128)(2,1)} %convolution_convert_fusion) | data formatting | bytes 20971520 | tf_op jit(solution)/shard_map/reshape | solution.py:122
  90.7 10.2 %all-to-all-start.2 = ((bf16[128,2,20480]{2,1,0:T(2,128)(2,1)}), bf16[128,2,20480]{2,1,0:T(2,128)(2,1)}, u32[]{:S(2)}, u32[]{:S(2)}) async-start(bf16[128,2,20480]{2,1,0:T(2,128)(2,1)} %reshape.160), calls=%async_computation.2 | async-start | bytes 20971520 | tf_op jit(solution)/shard_map/all_to_all | solution.py:121
  101.2 137.3 %all-to-all-done.2 = bf16[128,2,20480]{2,1,0:T(2,128)(2,1)} async-done(((bf16[128,2,20480]{2,1,0:T(2,128)(2,1)}), bf16[128,2,20480]{2,1,0:T(2,128)(2,1)}, u32[]{:S(2)}, u32[]{:S(2)}) %all-to-all-start.2) | async-done | bytes 10485792 | tf_op jit(solution)/shard_map/all_to_all | solution.py:121
  238.5 25.7 %dot_general.32 = bf16[16,64,5120]{2,1,0:T(8,128)(2,1)} reshape(bf16[128,2,20480]{2,1,0:T(2,128)(2,1)} %all-to-all-done.2) | data formatting | bytes 20971520 | tf_op jit(solution)/shard_map/dot_general | solution.py:138
  264.2 14.5 %fusion.4 = f32[16,64,768]{2,1,0:T(8,128)} fusion(bf16[16,64,5120]{2,1,0:T(8,128)(2,1)} %dot_general.32, bf16[768,5120]{1,0:T(8,128)(2,1)} %param.10), kind=kOutput, calls=%fused_computation.16 | convolution fusion | flops 8053063680 | bytes 21495808 | tf_op jit(solution)/shard_map/dot_general | solution.py:138
  278.7 52.4 %while.22 = (s32[]{:T(128)}, f32[16,64,64]{2,1,0:T(8,128)S(1)}, s32[16,64,64]{2,1,0:T(8,128)S(1)}, f32[16,64,768]{2,1,0:T(8,128)}, s32[]{:T(128)}) while((s32[]{:T(128)}, f32[16,64,64]{2,1,0:T(8,128)S(1)}, s32[16,64,64]{2,1,0:T(8,128)S(1)}, f32[16,64,768]{2,1,0:T(8,128)}, s32[]{:T(128)}) %tuple.43), condition=%wide.region_4.5_spmd.clone, body=%wide.region_2.4_spmd.clone.sunk | while | flops 9433090 | bytes 720969 | solution.py:65
  332.0 4.9 all-to-all-start.3
  337.0 8.3 %all-to-all-done.3 = f32[128,2,256]{2,1,0:T(2,128)S(1)} async-done(((f32[128,2,256]{2,1,0:T(2,128)}), f32[128,2,256]{2,1,0:T(2,128)S(1)}, u32[]{:S(2)}, u32[]{:S(2)}) %all-to-all-start.3) | async-done | bytes 262176 | tf_op jit(solution)/shard_map/all_to_all | solution.py:142
  348.1 6.9 %all-to-all-start.4 = ((bf16[128,2,256]{2,1,0:T(2,128)(2,1)}), bf16[128,2,256]{2,1,0:T(2,128)(2,1)S(1)}, u32[]{:S(2)}, u32[]{:S(2)}) async-start(bf16[128,2,256]{2,1,0:T(2,128)(2,1)} %all_to_all.43), calls=%async_computation.4 | async-start | bytes 262144 | tf_op jit(solution)/shard_map/all_to_all | solution.py:161
  355.0 7.1 %all-to-all-done.4 = bf16[128,2,256]{2,1,0:T(2,128)(2,1)S(1)} async-done(((bf16[128,2,256]{2,1,0:T(2,128)(2,1)}), bf16[128,2,256]{2,1,0:T(2,128)(2,1)S(1)}, u32[]{:S(2)}, u32[]{:S(2)}) %all-to-all-start.4) | async-done | bytes 131104 | tf_op jit(solution)/shard_map/all_to_all | solution.py:161
  362.3 52.5 %while.23 = (s32[]{:T(128)}, bf16[16,64,768]{2,1,0:T(8,128)(2,1)}, s32[16,64,64]{2,1,0:T(8,128)S(1)}, f32[16,64,64]{2,1,0:T(8,128)S(1)}, s32[]{:T(128)}) while((s32[]{:T(128)}, bf16[16,64,768]{2,1,0:T(8,128)(2,1)}, s32[16,64,64]{2,1,0:T(8,128)S(1)}, f32[16,64,64]{2,1,0:T(8,128)S(1)}, s32[]{:T(128)}) %tuple.49), condition=%wide.region_11.12_spmd.clone, body=%wide.region_9.11_spmd.clone.sunk | while | flops 9388034 | bytes 393797 | solution.py:85
  362.3 2.6 select_reduce_fusion.5
  365.6 2.6 select_reduce_fusion.5
  368.9 2.6 select_reduce_fusion.5
  382.0 2.6 select_reduce_fusion.5
  385.3 2.6 select_reduce_fusion.5
  414.8 13.4 %convolution_convert_fusion.2 = bf16[1024,5120]{1,0:T(8,128)(2,1)} fusion(bf16[1024,768]{1,0:T(8,128)(2,1)} %bitcast.51, bf16[768,5120]{1,0:T(8,128)(2,1)} %param.10), kind=kOutput, calls=%fused_computation.14 | convolution fusion | flops 8058306560 | bytes 19922944 | tf_op jit(solution)/shard_map/dot_general | solution.py:168
  428.2 25.8 %reshape.164 = bf16[128,2,20480]{2,1,0:T(2,128)(2,1)} reshape(bf16[1024,5120]{1,0:T(8,128)(2,1)} %convolution_convert_fusion.2) | data formatting | bytes 20971520 | tf_op jit(solution)/shard_map/reshape | solution.py:172
  454.0 8.1 %all-to-all-start.5 = ((bf16[128,2,20480]{2,1,0:T(2,128)(2,1)}), bf16[128,2,20480]{2,1,0:T(2,128)(2,1)}, u32[]{:S(2)}, u32[]{:S(2)}) async-start(bf16[128,2,20480]{2,1,0:T(2,128)(2,1)} %reshape.164), calls=%async_computation.5 | async-start | bytes 20971520 | tf_op jit(solution)/shard_map/all_to_all | solution.py:171
  462.1 25.8 %reshape.167 = bf16[1024,5120]{1,0:T(8,128)(2,1)} reshape(bf16[128,2,20480]{2,1,0:T(2,128)(2,1)} %all-to-all-done.2) | data formatting | bytes 20971520 | tf_op jit(solution)/shard_map/reshape | solution.py:136
  487.9 14.3 %convolution_convert_fusion.3 = bf16[768,5120]{1,0:T(8,128)(2,1)} fusion(bf16[1024,768]{1,0:T(8,128)(2,1)S(1)} %bitcast.52, bf16[1024,5120]{1,0:T(8,128)(2,1)} %reshape.167), kind=kOutput, calls=%fused_computation.15 | convolution fusion | flops 8056995840 | bytes 19922944 | tf_op jit(solution)/shard_map/dot_general | solution.py:165
  502.2 92.7 %all-to-all-done.5 = bf16[128,2,20480]{2,1,0:T(2,128)(2,1)} async-done(((bf16[128,2,20480]{2,1,0:T(2,128)(2,1)}), bf16[128,2,20480]{2,1,0:T(2,128)(2,1)}, u32[]{:S(2)}, u32[]{:S(2)}) %all-to-all-start.5) | async-done | bytes 10485792 | tf_op jit(solution)/shard_map/all_to_all | solution.py:171
  595.0 14.4 %reshape.165 = bf16[256,20480]{1,0:T(8,128)(2,1)} reshape(bf16[128,2,20480]{2,1,0:T(2,128)(2,1)} %all-to-all-done.5) | data formatting | bytes 20971520 | tf_op jit(solution)/shard_map/reshape | solution.py:178
  609.4 5.9 convolution_convert_fusion.1
  615.3 3.3 reshape.166
  (167 shorter events, 97.9 us)
Async XLA Ops:
  0.6 12.8 %copy-start.2 = (s32[64,2]{0,1:T(2,128)S(1)}, s32[64,2]{0,1:T(2,128)}, u32[]{:S(2)}) copy-start(s32[64,2]{0,1:T(2,128)} %param.11) | copy-start | bytes 1540
  0.6 13.5 %copy-start = (s32[256,64]{0,1:T(8,128)S(1)}, s32[256,64]{0,1:T(8,128)}, u32[]{:S(2)}) copy-start(s32[256,64]{0,1:T(8,128)} %param.12) | copy-start | bytes 196612
  4.2 41.3 %all-to-all-start.1 = ((bf16[32,256,160]{1,2,0:T(8,128)(2,1)}), bf16[32,256,160]{1,2,0:T(8,128)(2,1)S(1)}, u32[]{:S(2)}, u32[]{:S(2)}) async-start(bf16[32,256,160]{1,2,0:T(8,128)(2,1)} %bitcast.47), calls=%async_computation.1 | async-start | bytes 5242880 | tf_op jit(solution)/shard_map/all_to_all | solution.py:96
  45.5 45.2 %all-to-all-start = ((s32[128,2,256]{2,1,0:T(2,128)}), s32[128,2,256]{2,1,0:T(2,128)S(1)}, u32[]{:S(2)}, u32[]{:S(2)}) async-start(s32[128,2,256]{2,1,0:T(2,128)} %reshape.158), calls=%async_computation | async-start | bytes 524288 | tf_op jit(solution)/shard_map/all_to_all | solution.py:128
  90.7 147.8 %all-to-all-start.2 = ((bf16[128,2,20480]{2,1,0:T(2,128)(2,1)}), bf16[128,2,20480]{2,1,0:T(2,128)(2,1)}, u32[]{:S(2)}, u32[]{:S(2)}) async-start(bf16[128,2,20480]{2,1,0:T(2,128)(2,1)} %reshape.160), calls=%async_computation.2 | async-start | bytes 20971520 | tf_op jit(solution)/shard_map/all_to_all | solution.py:121
  264.2 72.7 %copy-start.1 = (f32[256,64]{0,1:T(8,128)S(1)}, f32[256,64]{0,1:T(8,128)}, u32[]{:S(2)}) copy-start(f32[256,64]{0,1:T(8,128)} %param.13) | copy-start | bytes 196612
  332.0 13.3 %all-to-all-start.3 = ((f32[128,2,256]{2,1,0:T(2,128)}), f32[128,2,256]{2,1,0:T(2,128)S(1)}, u32[]{:S(2)}, u32[]{:S(2)}) async-start(f32[128,2,256]{2,1,0:T(2,128)} %all_to_all.40), calls=%async_computation.3 | async-start | bytes 524288 | tf_op jit(solution)/shard_map/all_to_all | solution.py:142
  348.1 14.0 %all-to-all-start.4 = ((bf16[128,2,256]{2,1,0:T(2,128)(2,1)}), bf16[128,2,256]{2,1,0:T(2,128)(2,1)S(1)}, u32[]{:S(2)}, u32[]{:S(2)}) async-start(bf16[128,2,256]{2,1,0:T(2,128)(2,1)} %all_to_all.43), calls=%async_computation.4 | async-start | bytes 262144 | tf_op jit(solution)/shard_map/all_to_all | solution.py:161
  454.0 141.0 %all-to-all-start.5 = ((bf16[128,2,20480]{2,1,0:T(2,128)(2,1)}), bf16[128,2,20480]{2,1,0:T(2,128)(2,1)}, u32[]{:S(2)}, u32[]{:S(2)}) async-start(bf16[128,2,20480]{2,1,0:T(2,128)(2,1)} %reshape.164), calls=%async_computation.5 | async-start | bytes 20971520 | tf_op jit(solution)/shard_map/all_to_all | solution.py:171
  462.1 25.8 %copy-start.3 = (bf16[16,64,768]{2,1,0:T(8,128)(2,1)S(1)}, bf16[16,64,768]{2,1,0:T(8,128)(2,1)}, u32[]{:S(2)}) copy-start(bf16[16,64,768]{2,1,0:T(8,128)(2,1)} %get-tuple-element.58) | copy-start | bytes 4718596
where the time goes:
time: 624 us; the launch traced here: 619 us
  waiting for transfers between devices  275 us (44%)
  local copies, waits for them, and re-layouts  159 us (25%)
  other arithmetic  79.5 us (13%)
  matrix products  54.6 us (9%)
  starting transfers between devices  49.4 us (8%)
    all_to_all x1, waiting for transfers between devices, body(): lax.all_to_all(send_rows.reshape(owner_count, capacity, per_tile * width)...  137 us
    all_to_all x1, waiting for transfers between devices, body(): lax.all_to_all(grad_parts.reshape(owner_count, capacity, per_tile * width...  92.7 us
    reduce_sum x16, other arithmetic, place_one_block(): jnp.sum(jnp.where(match, value_block[:, :, None], 0.0), axis=1)  41.7 us
    reduce_sum x16, other arithmetic, pick_one_block(): return jnp.sum(jnp.where(match, score_block[:, None, :], 0.0), axis=2)  36.3 us
    all_to_all x1, waiting for transfers between devices, body(): lax.all_to_all(hidden, 'voc', split_axis=0, concat_axis=1, tiled=True)  29.4 us
    reshape x1, local copies, waits for them, and re-layouts, body(): grad_parts.reshape(owner_count, capacity, per_tile * width)  25.8 us
    reshape x1, local copies, waits for them, and re-layouts, body(): got_rows = got_rows.reshape(slot_count * per_tile, width)  25.8 us
    dot_general x1, local copies, waits for them, and re-layouts, body(): lax.dot_general(got_rows, head_weight, (((1,), (1,)), ((), ())), preferre...  25.7 us
  transfers between devices with their start and end apart: 6, of which 5 were waited for; matrix products, arithmetic and copies ran while one was open for 13% of the time, Pallas kernels for 0%

commit v1 on v0

v1 whole, which is shorter than its diff:
```python
import functools

import jax
import jax.numpy as jnp
from jax import lax
from jax.experimental import pallas as pl
from jax.experimental.pallas import tpu as pltpu
from jax.sharding import PartitionSpec as P

loss_weight = 16.0
nothing = -1e30
f32, bf16, i32 = jnp.float32, jnp.bfloat16, jnp.int32
HIGHEST = lax.Precision.HIGHEST


def settings(mib=32):
    return pltpu.CompilerParams(vmem_limit_bytes=mib * 1024 * 1024)


def by_rows(a, b, precision=None):
    return lax.dot_general(
        a, b, (((1,), (1,)), ((), ())), preferred_element_type=f32, precision=precision
    )


def plain(a, b, precision=None):
    return lax.dot_general(
        a, b, (((1,), (0,)), ((), ())), preferred_element_type=f32, precision=precision
    )


def iota(shape, dim):
    return lax.broadcasted_iota(i32, shape, dim)


def rows_of(codes, tiles, per_tile):
    entries = codes.shape[1]
    wide = entries * per_tile
    spread = (iota((entries, wide), 0) == iota((entries, wide), 1) // per_tile).astype(bf16)
    expanded = plain(codes.astype(bf16), spread).astype(i32)
    return expanded * per_tile + iota(expanded.shape, 1) % per_tile


def announce_kernel(panel, per_tile, owner_ref, cand_ref, teacher_ref, out_ref, rows_ref):
    entries = owner_ref.shape[1]
    tiles = entries // 2
    tokens = tiles * per_tile
    owners = jnp.broadcast_to(owner_ref[...].astype(f32), (entries, entries))
    earlier = iota((entries, entries), 0) % tiles < iota((entries, entries), 1) % tiles
    same = (owners == owners.T) & earlier
    rank = jnp.sum(jnp.where(same, 1.0, 0.0), axis=0, keepdims=True)
    code = owner_ref[...].astype(f32) * 2.0 + rank
    rows = rows_of(jnp.broadcast_to(code, (8, entries)), tiles, per_tile)
    rows_ref[...] = rows
    cand = cand_ref[...]
    teacher = teacher_ref[...]
    columns = (
        jnp.where(cand < panel, cand + 1, 0).astype(f32),
        jnp.where(cand >= panel, cand - panel + 1, 0).astype(f32),
    )
    slots = out_ref.shape[0]
    block = 32
    for at in range(0, slots, block):
        row = iota((block * 8, tokens), 0) + at * 8
        told = jnp.zeros((block * 8, 2 * cand.shape[0]), f32)
        for group in range(2):
            hot = jnp.where(row == rows[0:1, group * tokens : (group + 1) * tokens], 1.0, 0.0)
            told = told + by_rows(
                hot, jnp.concatenate([columns[group], teacher], axis=0), HIGHEST
            )
        width = told.shape[1]
        out_ref[at : at + block, :, 0:width] = told.reshape(block, 8, width)
        out_ref[at : at + block, :, width : width + entries] = jnp.broadcast_to(
            code.reshape(1, 1, entries), (block, 8, entries)
        )


def announce(owner_row, cand, teacher, panel, per_tile, owners):
    entries = owner_row.shape[1]
    return pl.pallas_call(
        functools.partial(announce_kernel, panel, per_tile),
        out_shape=(
            jax.ShapeDtypeStruct((owners, 8, 2 * cand.shape[0] + entries), f32),
            jax.ShapeDtypeStruct((8, entries * per_tile), i32),
        ),
        compiler_params=settings(),
        name="announce",
    )(owner_row, cand, teacher)


def route_kernel(blocks, per_tile, tok_ref, codes_ref, hidden_ref, out_ref, rows_ref, held_ref):
    step = pl.program_id(0)
    steps = blocks // 2
    width = hidden_ref.shape[0]
    tokens = hidden_ref.shape[1] // 2
    owners = held_ref.shape[0]

    @pl.when(step == 0)
    def _():
        codes = codes_ref[pl.ds(pl.multiple_of(tok_ref[0] * blocks, blocks), blocks), :]
        rows_ref[...] = rows_of(codes, tokens // per_tile, per_tile)

    @pl.when(step < steps)
    def _():
        chunk = owners // 2
        for at in range(0, owners, chunk):
            row = iota((chunk * 8, tokens), 0) + at * 8
            parts = []
            for which in range(2):
                first = rows_ref[pl.ds(step * 2 + which, 1), 0:tokens]
                second = rows_ref[pl.ds(step * 2 + which, 1), tokens : 2 * tokens]
                hot = jnp.where((row == first) | (row == second), 1.0, 0.0).astype(bf16)
                part = by_rows(hot, hidden_ref[:, which * tokens : (which + 1) * tokens])
                parts.append(part.reshape(chunk, 8, width))
            held_ref[at : at + chunk, pl.ds(pl.multiple_of(step * 16, 16), 16), :] = (
                jnp.concatenate(parts, axis=1).astype(bf16)
            )

    @pl.when(step >= steps)
    def _():
        count = out_ref.shape[0]
        eye = (iota((width, width), 0) == iota((width, width), 1)).astype(bf16)
        for k in range(count):
            out_ref[k] = by_rows(eye, held_ref[(step - steps) * count + k]).astype(bf16)


def route(tok, codes, hidden, per_tile, blocks):
    width, total = hidden.shape
    owners = codes.shape[0]
    steps = blocks // 2
    tokens = total // blocks
    turn = 8
    return pl.pallas_call(
        functools.partial(route_kernel, blocks, per_tile),
        grid_spec=pltpu.PrefetchScalarGridSpec(
            num_scalar_prefetch=1,
            grid=(steps + owners // turn,),
            in_specs=[
                pl.BlockSpec(codes.shape, lambda s, t: (0, 0)),
                pl.BlockSpec((width, 2 * tokens), lambda s, t: (0, jnp.minimum(s, steps - 1))),
            ],
            out_specs=pl.BlockSpec(
                (turn, width, blocks * 8), lambda s, t: (jnp.maximum(s - steps, 0), 0, 0)
            ),
            scratch_shapes=[
                pltpu.VMEM((blocks, codes.shape[1] * per_tile), i32),
                pltpu.VMEM((owners, blocks * 8, width), bf16),
            ],
        ),
        out_shape=jax.ShapeDtypeStruct((owners, width, blocks * 8), bf16),
        compiler_params=settings(40),
        name="route",
    )(tok, codes, hidden)


def place_kernel(per_tile, owner_ref, told_ref, dense_ref, facts_ref):
    sources, _, width = told_ref.shape
    lanes = sources * 8
    turned = told_ref[...].reshape(lanes, width).T
    picks = width // 4
    columns = turned[0:picks].astype(i32) - 1
    teacher = turned[picks : 2 * picks]
    target = jnp.exp(teacher)
    panel = dense_ref.shape[0]
    chunk = 128
    place = iota((chunk, lanes), 0)
    for at in range(0, panel, chunk):
        dense = jnp.zeros((chunk, lanes), f32)
        for k in range(picks):
            dense = jnp.where(place == columns[k : k + 1] - at, target[k : k + 1], dense)
        dense_ref[at : at + chunk, :] = dense
    codes = turned[2 * picks :]
    half = codes.shape[0] // 2
    other = jnp.concatenate([codes[half:], codes[:half]], axis=0)
    slot = (iota((1, lanes), 1) // per_tile) % 2
    mine = (owner_ref[0] * 2 + slot).astype(f32)
    partner = jnp.sum(jnp.where(codes == mine, other + 1.0, 0.0), axis=0, keepdims=True)
    mass = jnp.sum(target, axis=0, keepdims=True)
    entropy = jnp.sum(jnp.where(columns >= 0, target * teacher, 0.0), axis=0, keepdims=True)
    facts_ref[...] = jnp.concatenate(
        [partner, mass, entropy, jnp.zeros((5, lanes), f32)], axis=0
    )


def place(owner, told, panel, per_tile):
    sources, _, width = told.shape
    rows = sources * 8
    block = 16
    return pl.pallas_call(
        functools.partial(place_kernel, per_tile),
        grid_spec=pltpu.PrefetchScalarGridSpec(
            num_scalar_prefetch=1,
            grid=(sources // block,),
            in_specs=[pl.BlockSpec((block, 8, width), lambda s, o: (s, 0, 0))],
            out_specs=[
                pl.BlockSpec((panel, block * 8), lambda s, o: (0, s)),
                pl.BlockSpec((8, block * 8), lambda s, o: (0, s)),
            ],
        ),
        out_shape=(
            jax.ShapeDtypeStruct((panel, rows), f32),
            jax.ShapeDtypeStruct((8, rows), f32),
        ),
        compiler_params=settings(),
        cost_estimate=pl.CostEstimate(
            flops=2 * 64 * panel * rows, bytes_accessed=8 * panel * rows, transcendentals=64 * rows
        ),
        name="place",
    )(owner, told)


def score_kernel(head_ref, rows_ref, dense_ref, facts_ref, part_ref, own_ref, told_ref, total_ref):
    step = pl.program_id(0)
    groups, _, lanes = rows_ref.shape

    @pl.when(step == 0)
    def _():
        for t in range(groups):
            total_ref[:, t * lanes : (t + 1) * lanes] = plain(head_ref[...], rows_ref[t])

    @pl.when(step > 0)
    def _():
        for t in range(groups):
            total_ref[:, t * lanes : (t + 1) * lanes] += plain(head_ref[...], rows_ref[t])

    @pl.when(step == pl.num_programs(0) - 1)
    def _():
        count = total_ref.shape[1]
        chunk = 128
        logs, largest, shares = [], [], []
        for at in range(0, count, chunk):
            here = slice(at, at + chunk)
            dense = dense_ref[:, here]
            score = total_ref[:, here]
            named = dense > 0.0
            most = jnp.max(jnp.where(named, score, nothing), axis=0, keepdims=True)
            part = jnp.where(named, jnp.exp(score - most), 0.0)
            part_ref[:, here] = part
            whole = jnp.sum(part, axis=0, keepdims=True)
            log = jnp.where(whole > 0.0, most + jnp.log(jnp.maximum(whole, 1.0)), nothing)
            shares.append(
                facts_ref[2:3, here] - jnp.sum(dense * score, axis=0, keepdims=True)
            )
            logs.append(log)
            largest.append(most)
        logs = jnp.concatenate(logs, axis=1)
        largest = jnp.concatenate(largest, axis=1)
        shares = jnp.concatenate(shares, axis=1)
        own_ref[...] = jnp.concatenate([largest, logs, jnp.zeros((6, count), f32)], axis=0)
        owners = told_ref.shape[0]
        told_ref[:, 0:count] = jnp.broadcast_to(logs, (owners, count))
        home = iota((owners, count), 1) // 8 == iota((owners, count), 0)
        which = (iota((count, 128), 0) % 8 == iota((count, 128), 1)).astype(f32)
        told_ref[:, count : count + 128] = plain(
            jnp.where(home, jnp.broadcast_to(shares, (owners, count)), 0.0), which, HIGHEST
        )


def score(head, rows, dense, facts, owners):
    panel, width = head.shape
    groups, _, lanes = rows.shape
    count = groups * lanes
    block = 640
    whole = lambda s: (0, 0)
    return pl.pallas_call(
        score_kernel,
        grid=(width // block,),
        in_specs=[
            pl.BlockSpec((panel, block), lambda s: (0, s)),
            pl.BlockSpec((groups, block, lanes), lambda s: (0, s, 0)),
            pl.BlockSpec((panel, count), whole),
            pl.BlockSpec((8, count), whole),
        ],
        out_specs=[
            pl.BlockSpec((panel, count), whole),
            pl.BlockSpec((8, count), whole),
            pl.BlockSpec((owners, count + 128), whole),
        ],
        out_shape=(
            jax.ShapeDtypeStruct((panel, count), f32),
            jax.ShapeDtypeStruct((8, count), f32),
            jax.ShapeDtypeStruct((owners, count + 128), f32),
        ),
        scratch_shapes=[pltpu.VMEM((panel, count), f32)],
        compiler_params=settings(48),
        name="score",
    )(head, rows, dense, facts)


def log_sum(a, b):
    most = jnp.maximum(a, b)
    return most + jnp.log(jnp.exp(a - most) + jnp.exp(b - most))


def part_kernel(
    per_tile, logs_ref, facts_ref, own_ref, part_ref, dense_ref, head_ref, out_ref, turned_ref, weight_ref
):
    step = pl.program_id(0)

    @pl.when(step == 0)
    def _():
        panel, count = part_ref.shape
        owners = logs_ref.shape[0]
        chunk = 128
        for at in range(0, count, chunk):
            here = slice(at, at + chunk)
            logs = logs_ref[:, here]
            partner = facts_ref[0:1, here].astype(i32) - 1
            slot = (iota((1, chunk), 1) // per_tile) % 2
            across = jnp.where(
                slot == 0, pltpu.roll(logs, chunk - per_tile, 1), pltpu.roll(logs, per_tile, 1)
            )
            picked = jnp.where(
                iota((owners, chunk), 0) == partner // 2,
                jnp.where(partner % 2 == slot, logs, across),
                0.0,
            )
            other = jnp.sum(picked, axis=0, keepdims=True)
            total = log_sum(own_ref[1:2, here], other)
            scale = loss_weight * facts_ref[1:2, here] * jnp.exp(own_ref[0:1, here] - total)
            weight = part_ref[:, here] * scale - loss_weight * dense_ref[:, here]
            turned_ref[:, here] = weight.astype(bf16)
            weight_ref[here, :] = weight.T.astype(bf16)

    out_ref[...] = plain(weight_ref[...], head_ref[...]).astype(bf16)


def grad_parts(logs, facts, own, part, dense, head, per_tile):
    panel, width = head.shape
    count = part.shape[1]
    block = 512
    whole = lambda s: (0, 0)
    return pl.pallas_call(
        functools.partial(part_kernel, per_tile),
        grid=(width // block,),
        in_specs=[
            pl.BlockSpec(logs.shape, whole),
            pl.BlockSpec((8, count), whole),
            pl.BlockSpec((8, count), whole),
            pl.BlockSpec((panel, count), whole),
            pl.BlockSpec((panel, count), whole),
            pl.BlockSpec((panel, block), lambda s: (0, s)),
        ],
        out_specs=[
            pl.BlockSpec((count, block), lambda s: (0, s)),
            pl.BlockSpec((panel, count), whole),
        ],
        out_shape=(
            jax.ShapeDtypeStruct((count, width), bf16),
            jax.ShapeDtypeStruct((panel, count), bf16),
        ),
        scratch_shapes=[pltpu.VMEM((count, panel), bf16)],
        compiler_params=settings(48),
        name="grad_parts",
    )(logs, facts, own, part, dense, head)


def head_kernel(weight_ref, rows_ref, out_ref):
    groups, _, lanes = rows_ref.shape
    total = by_rows(weight_ref[:, 0:lanes], rows_ref[0])
    for t in range(1, groups):
        total = total + by_rows(weight_ref[:, t * lanes : (t + 1) * lanes], rows_ref[t])
    out_ref[...] = total.astype(bf16)


def grad_of_head(weight, rows):
    panel, count = weight.shape
    groups, width, lanes = rows.shape
    block = 512
    return pl.pallas_call(
        head_kernel,
        grid=(width // block,),
        in_specs=[
            pl.BlockSpec((panel, count), lambda s: (0, 0)),
            pl.BlockSpec((groups, block, lanes), lambda s: (0, s, 0)),
        ],
        out_specs=pl.BlockSpec((panel, block), lambda s: (0, s)),
        out_shape=jax.ShapeDtypeStruct((panel, width), bf16),
        compiler_params=settings(),
        cost_estimate=pl.CostEstimate(
            flops=2 * panel * count * width,
            bytes_accessed=2 * (panel + count) * width,
            transcendentals=0,
        ),
        name="grad_of_head",
    )(weight, rows)


def loss_kernel(me_ref, logs_ref, rows_ref, teacher_ref, loss_ref, table_ref):
    owners = logs_ref.shape[0]
    tokens = teacher_ref.shape[1]
    count = table_ref.shape[1]
    mine = iota((count, 128), 0) == me_ref[0] * 8 + iota((count, 128), 1)
    mine = jnp.where(mine & (iota((count, 128), 1) < 8), 1.0, 0.0)
    logs = plain(logs_ref[:, 0:count], mine, HIGHEST).T
    shares = logs_ref[:, count : count + 128].T
    found = []
    total = jnp.zeros((1, tokens), f32)
    for group in range(2):
        row = rows_ref[0:1, group * tokens : (group + 1) * tokens]
        owner = jnp.where(iota((owners, tokens), 0) == row // 8, 1.0, 0.0)
        slot = iota((128, tokens), 0) == row % 8
        for table, kept in ((logs, True), (shares, False)):
            got = jnp.where(slot, plain(table, owner, HIGHEST), 0.0)
            got = jnp.sum(got, axis=0, keepdims=True)
            if kept:
                found.append(got)
            else:
                total = total + got
    teacher = teacher_ref[...]
    mass = jnp.sum(jnp.exp(teacher), axis=0, keepdims=True)
    loss_ref[...] = total + mass * log_sum(found[0], found[1])
    first, second = rows_ref[0:1, 0:tokens], rows_ref[0:1, tokens : 2 * tokens]
    for at in range(0, count, 128):
        row = iota((128, tokens), 0) + at
        hot = jnp.where((row == first) | (row == second), 1.0, 0.0)
        table_ref[:, at : at + 128] = hot.T.astype(bf16)


def losses(me, logs, rows, teacher, count):
    tokens = teacher.shape[1]
    return pl.pallas_call(
        loss_kernel,
        in_specs=[pl.BlockSpec(memory_space=pltpu.SMEM)] + [pl.BlockSpec(memory_space=pltpu.VMEM)] * 3,
        out_shape=(
            jax.ShapeDtypeStruct((1, tokens), f32),
            jax.ShapeDtypeStruct((tokens, count), bf16),
        ),
        compiler_params=settings(),
        cost_estimate=pl.CostEstimate(
            flops=12 * 2 * count * tokens * 128, bytes_accessed=4 * count * tokens, transcendentals=0
        ),
        name="losses",
    )(me, logs, rows, teacher)


def combine_kernel(table_ref, parts_ref, out_ref):
    out_ref[...] = plain(table_ref[...], parts_ref[...]).astype(bf16)


def combine(table, parts):
    tokens, count = table.shape
    width = parts.shape[1]
    block = 512
    return pl.pallas_call(
        combine_kernel,
        grid=(width // block,),
        in_specs=[
            pl.BlockSpec((tokens, count), lambda s: (0, 0)),
            pl.BlockSpec((count, block), lambda s: (0, s)),
        ],
        out_specs=pl.BlockSpec((tokens, block), lambda s: (0, s)),
        out_shape=jax.ShapeDtypeStruct((tokens, width), bf16),
        compiler_params=settings(),
        name="combine",
    )(table, parts)


def exchange(values):
    return lax.all_to_all(values, ("tok", "voc"), split_axis=0, concat_axis=0, tiled=True)


def body(hidden, head_weight, tile_owners, cand_pos, teacher_logp):
    panel, width = head_weight.shape
    tiles = tile_owners.shape[0]
    tokens = cand_pos.shape[0]
    per_tile = tokens // tiles
    tok_size, blocks = lax.axis_size("tok"), lax.axis_size("voc")
    owners = tok_size * blocks
    count = owners * 8
    tok = lax.axis_index("tok")
    me = (tok * blocks + lax.axis_index("voc")).astype(i32).reshape(1)
    teacher = teacher_logp.T
    told, home_rows = announce(
        tile_owners.T.reshape(1, 2 * tiles), cand_pos.T, teacher, panel, per_tile, owners
    )
    told = exchange(told)
    codes = told[:, 0, 2 * cand_pos.shape[1] :]
    sent = route(tok.astype(i32).reshape(1), codes, hidden.T, per_tile, blocks)
    rows = exchange(sent).reshape(tok_size, width, blocks * 8)
    dense, facts = place(me, told, panel, per_tile)
    part, own, logs = score(head_weight, rows, dense, facts, owners)
    logs = exchange(logs.reshape(owners, 1, count + 128)).reshape(owners, count + 128)
    parts, weight = grad_parts(logs, facts, own, part, dense, head_weight, per_tile)
    home_parts = exchange(parts.reshape(owners, 8, width)).reshape(count, width)
    grad_head = grad_of_head(weight, rows)
    loss, table = losses(me, logs, home_rows, teacher, count)
    grad_hidden = combine(table, home_parts)
    return (loss.reshape(tokens), grad_hidden, grad_head)


def solution(mesh):
    placed = (
        P("tok", "voc"),
        P(("tok", "voc"), None),
        P(("tok", "voc"), None),
        P(("tok", "voc"), None),
        P(("tok", "voc"), None),
    )
    return jax.shard_map(
        body,
        mesh=mesh,
        in_specs=placed,
        out_specs=(P(("tok", "voc")), P(("tok", "voc"), None), P(("tok", "voc"), None)),
        check_vma=False,
    )
```

time: 624 us -> 402 us (0.64)
  local copies, waits for them, and re-layouts: 159 us -> 10.3 us
  Pallas kernels: 0 us -> 103 us
  other arithmetic: 79.5 us -> 0 us
  matrix products: 54.6 us -> 0 us
  waiting for transfers between devices: 275 us -> 245 us
  starting transfers between devices: 49.4 us -> 24.9 us
  blocking collectives: 0 us -> 16.6 us
    pallas_call x0 -> x8, Pallas kernels: none -> 103 us  [the longest x1 21 us: place(): pl.pallas_call(functools.partial(place_kernel, per_tile), grid_spec=pltpu...]
    reshape x9 -> x2, local copies, waits for them, and re-layouts: 94.4 us -> 1.37 us  [the longest x1 0.76 us: body(): tile_owners.T.reshape(1, 2 * tiles)]
    reduce_sum x35 -> x0, other arithmetic: 79.1 us -> none  [the longest x16 41.7 us: place_one_block(): jnp.sum(jnp.where(match, value_block[:, :, None], 0.0), axis=1)]
    dot_general x9 -> x0, matrix products: 54.6 us -> none  [the longest x1 14.5 us: body(): lax.dot_general(got_rows, head_weight, (((1,), (1,)), ((), ())), preferre...]
    all_to_all x6 -> x3, waiting for transfers between devices: 275 us -> 245 us  [exchange(): lax.all_to_all(values, ('tok', 'voc'), split_axis=0, concat_axis=0, tiled...]
    dot_general x1 -> x0, local copies, waits for them, and re-layouts: 25.7 us -> none  [body(): lax.dot_general(got_rows, head_weight, (((1,), (1,)), ((), ())), preferre...]
    all_to_all x6 -> x3, starting transfers between devices: 49.4 us -> 24.9 us  [exchange(): lax.all_to_all(values, ('tok', 'voc'), split_axis=0, concat_axis=0, tiled...]
    all_to_all x0 -> x1, blocking collectives: none -> 16.6 us  [exchange(): lax.all_to_all(values, ('tok', 'voc'), split_axis=0, concat_axis=0, tiled...]
  transfers between devices with their start and end apart: 6 -> 3, of which waited for: 5 -> 3; matrix products, arithmetic and copies ran while one was open for 13% -> 0% of each run, Pallas kernels for 0% -> 9%
where the time goes in v1:
time: 402 us; the launch traced here: 400 us
  waiting for transfers between devices  245 us (61%)
  Pallas kernels  103 us (26%)
  starting transfers between devices  24.9 us (6%)
  blocking collectives  16.6 us (4%)
  local copies, waits for them, and re-layouts  10.3 us (3%)
    all_to_all x3, waiting for transfers between devices, exchange(): lax.all_to_all(values, ('tok', 'voc'), split_axis=0, concat_axis=0, tiled...  245 us
    all_to_all x3, starting transfers between devices, exchange(): lax.all_to_all(values, ('tok', 'voc'), split_axis=0, concat_axis=0, tiled...  24.9 us
    pallas_call x1, Pallas kernels, place(): pl.pallas_call(functools.partial(place_kernel, per_tile), grid_spec=pltpu...  21 us
    pallas_call x1, Pallas kernels, route(): pl.pallas_call(functools.partial(route_kernel, blocks, per_tile), grid_sp...  18.4 us
    pallas_call x1, Pallas kernels, score(): pl.pallas_call(score_kernel, grid=(width // block,), in_specs=[pl.BlockSp...  17.2 us
    all_to_all x1, blocking collectives, exchange(): lax.all_to_all(values, ('tok', 'voc'), split_axis=0, concat_axis=0, tiled...  16.6 us
    pallas_call x1, Pallas kernels, grad_parts(): pl.pallas_call(functools.partial(part_kernel, per_tile), grid=(width // b...  16.5 us
    pallas_call x1, Pallas kernels, grad_of_head(): pl.pallas_call(head_kernel, grid=(width // block,), in_specs=[pl.BlockSpe...  14.6 us
  transfers between devices with their start and end apart: 3, of which 3 were waited for; matrix products, arithmetic and copies ran while one was open for 0% of the time, Pallas kernels for 9%

profile of v1, /device:TPU:97, one launch (start us, length us, event | category | flops | bytes accessed | tf_op | source)
XLA Modules:
  0.0 400.3 jit_solution(14757806405206995895)
XLA Ops:
  0.6 0.8 reshape.35.owner_ref
  1.4 0.0 copy-start.3
  1.4 0.8 copy-done.3
  2.2 0.0 copy-start.4
  2.2 0.8 copy-done.4
  3.1 3.1 announce.1
  6.1 10.2 %all-to-all-start = ((f32[128,8,256]{2,1,0:T(8,128)}), f32[128,8,256]{2,1,0:T(8,128)S(1)}, u32[]{:S(2)}, u32[]{:S(2)}) async-start(f32[128,8,256]{2,1,0:T(8,128)} %get-tuple-element.14), calls=%async_computation | async-start | bytes 2097152 | tf_op jit(solution)/shard_map/all_to_all | solution.py:460
  16.3 16.6 %all-to-all-done.told_ref = f32[128,8,256]{2,1,0:T(8,128)S(1)} async-done(((f32[128,8,256]{2,1,0:T(8,128)}), f32[128,8,256]{2,1,0:T(8,128)S(1)}, u32[]{:S(2)}, u32[]{:S(2)}) %all-to-all-start) | async-done | bytes 1048608 | tf_op jit(solution)/shard_map/all_to_all | solution.py:460
  32.9 0.0 copy-start.2
  32.9 1.7 copy-done.2
  34.7 18.4 %route.1 = bf16[128,160,256]{2,1,0:T(8,128)(2,1)S(1)} custom-call(s32[1]{0:T(128)} %bitcast.1.tok_ref, f32[128,128]{1,0:T(8,128)S(1)} %bitcast.19, bf16[160,8192]{1,0:T(8,128)(2,1)S(1)} %bitcast.15), custom_call_target="tpu_custom_call" | custom-call | tf_op jit(solution)/shard_map/route/pallas_call | solution.py:133
  53.1 0.0 copy-start
  53.1 3.8 copy-done
  56.9 7.1 %all-to-all-start.1 = ((bf16[128,160,256]{2,1,0:T(8,128)(2,1)}), bf16[128,160,256]{2,1,0:T(8,128)(2,1)}, u32[]{:S(2)}, u32[]{:S(2)}) async-start(bf16[128,160,256]{2,1,0:T(8,128)(2,1)} %copy-done), calls=%async_computation.1 | async-start | bytes 20971520 | tf_op jit(solution)/shard_map/all_to_all | solution.py:460
  64.0 21.0 %place.1 = (f32[768,1024]{1,0:T(8,128)S(1)}, f32[8,1024]{1,0:T(8,128)S(1)}) custom-call(s32[1]{0:T(128)} %bitcast.owner_ref.me_ref, f32[128,8,256]{2,1,0:T(8,128)S(1)} %all-to-all-done.told_ref), custom_call_target="tpu_custom_call" | custom-call | flops 100663296 | bytes 6291456 | tf_op jit(solution)/shard_map/place/pallas_call | solution.py:189
  85.0 0.0 copy-start.1
  85.0 1.7 copy-done.1
  86.7 112.2 %all-to-all-done.1 = bf16[128,160,256]{2,1,0:T(8,128)(2,1)} async-done(((bf16[128,160,256]{2,1,0:T(8,128)(2,1)}), bf16[128,160,256]{2,1,0:T(8,128)(2,1)}, u32[]{:S(2)}, u32[]{:S(2)}) %all-to-all-start.1) | async-done | bytes 10485792 | tf_op jit(solution)/shard_map/all_to_all | solution.py:460
  198.8 17.2 %score.1 = (f32[768,1024]{1,0:T(8,128)S(1)}, f32[8,1024]{1,0:T(8,128)S(1)}, f32[128,1152]{1,0:T(8,128)S(1)}) custom-call(bf16[768,5120]{1,0:T(8,128)(2,1)} %head_ref.3, bf16[4,5120,256]{2,1,0:T(8,128)(2,1)} %bitcast.7.rows_ref, f32[768,1024]{1,0:T(8,128)} %copy-done.1, f32[8,1024]{1,0:T(8,128)S(1)} %get-tuple-element.16.facts_ref), custom_call_target="tpu_custom_call" | custom-call | tf_op jit(solution)/shard_map/score/pallas_call | solution.py:265
  216.1 0.6 copy.8
  216.7 16.6 %all_to_all.20 = f32[128,1,1152]{2,1,0:T(1,128)S(1)} all-to-all(f32[128,1,1152]{2,1,0:T(1,128)S(1)} %copy.8), channel_id=1, replica_groups=mesh['tok'=4,'voc'=32] {'tok','voc'}, dimensions={0} | all-to-all | bytes 1179648 | tf_op jit(solution)/shard_map/all_to_all | solution.py:460
  233.3 16.5 %grad_parts.1 = (bf16[1024,5120]{1,0:T(8,128)(2,1)}, bf16[768,1024]{1,0:T(8,128)(2,1)S(1)}) custom-call(f32[128,1152]{1,0:T(8,128)S(1)} %bitcast.16, f32[8,1024]{1,0:T(8,128)S(1)} %get-tuple-element.16.facts_ref, f32[8,1024]{1,0:T(8,128)S(1)} %get-tuple-element.21.own_ref, f32[768,1024]{1,0:T(8,128)S(1)} %get-tuple-element.22.part_ref, ...), custom_call_target="tpu_custom_call" | custom-call | tf_op jit(solution)/shard_map/grad_parts/pallas_call | solution.py:333
  249.8 0.0 copy-start.5
  249.8 7.7 %all-to-all-start.3 = ((bf16[128,8,5120]{2,1,0:T(8,128)(2,1)}), bf16[128,8,5120]{2,1,0:T(8,128)(2,1)}, u32[]{:S(2)}, u32[]{:S(2)}) async-start(bf16[128,8,5120]{2,1,0:T(8,128)(2,1)} %bitcast.23), calls=%async_computation.3 | async-start | bytes 20971520 | tf_op jit(solution)/shard_map/all_to_all | solution.py:460
  257.5 0.0 copy-done.5
  257.5 1.8 losses.1
  259.3 14.6 %grad_of_head.1 = bf16[768,5120]{1,0:T(8,128)(2,1)} custom-call(bf16[768,1024]{1,0:T(8,128)(2,1)S(1)} %get-tuple-element.24.weight_ref, bf16[4,5120,256]{2,1,0:T(8,128)(2,1)} %bitcast.7.rows_ref), custom_call_target="tpu_custom_call" | custom-call | flops 8053063680 | bytes 18350080 | tf_op jit(solution)/shard_map/grad_of_head/pallas_call | solution.py:370
  273.9 116.1 %all-to-all-done.3 = bf16[128,8,5120]{2,1,0:T(8,128)(2,1)} async-done(((bf16[128,8,5120]{2,1,0:T(8,128)(2,1)}), bf16[128,8,5120]{2,1,0:T(8,128)(2,1)}, u32[]{:S(2)}, u32[]{:S(2)}) %all-to-all-start.3) | async-done | bytes 10485792 | tf_op jit(solution)/shard_map/all_to_all | solution.py:460
  390.0 10.3 %combine.1 = bf16[256,5120]{1,0:T(8,128)(2,1)} custom-call(bf16[256,1024]{1,0:T(8,128)(2,1)S(1)} %get-tuple-element.20.table_ref, bf16[1024,5120]{1,0:T(8,128)(2,1)} %bitcast.11.parts_ref), custom_call_target="tpu_custom_call" | custom-call | tf_op jit(solution)/shard_map/combine/pallas_call | solution.py:445
  (2 shorter events, 0.1 us)
Async XLA Ops:
  1.4 0.8 copy-start.3
  2.2 0.8 copy-start.4
  6.1 26.7 %all-to-all-start = ((f32[128,8,256]{2,1,0:T(8,128)}), f32[128,8,256]{2,1,0:T(8,128)S(1)}, u32[]{:S(2)}, u32[]{:S(2)}) async-start(f32[128,8,256]{2,1,0:T(8,128)} %get-tuple-element.14), calls=%async_computation | async-start | bytes 2097152 | tf_op jit(solution)/shard_map/all_to_all | solution.py:460
  32.9 1.7 copy-start.2
  53.1 3.8 copy-start
  56.9 141.9 %all-to-all-start.1 = ((bf16[128,160,256]{2,1,0:T(8,128)(2,1)}), bf16[128,160,256]{2,1,0:T(8,128)(2,1)}, u32[]{:S(2)}, u32[]{:S(2)}) async-start(bf16[128,160,256]{2,1,0:T(8,128)(2,1)} %copy-done), calls=%async_computation.1 | async-start | bytes 20971520 | tf_op jit(solution)/shard_map/all_to_all | solution.py:460
  85.0 1.7 copy-start.1
  249.8 7.7 %copy-start.5 = (f32[256,64]{0,1:T(8,128)S(1)}, f32[256,64]{0,1:T(8,128)}, u32[]{:S(2)}) copy-start(f32[256,64]{0,1:T(8,128)} %param.9) | copy-start | bytes 196612
  249.8 140.2 %all-to-all-start.3 = ((bf16[128,8,5120]{2,1,0:T(8,128)(2,1)}), bf16[128,8,5120]{2,1,0:T(8,128)(2,1)}, u32[]{:S(2)}, u32[]{:S(2)}) async-start(bf16[128,8,5120]{2,1,0:T(8,128)(2,1)} %bitcast.23), calls=%async_computation.3 | async-start | bytes 20971520 | tf_op jit(solution)/shard_map/all_to_all | solution.py:460

commit v2 on v1

v2 whole, which is shorter than its diff:
```python
import functools

import jax
import jax.numpy as jnp
from jax import lax
from jax.experimental import pallas as pl
from jax.experimental.pallas import tpu as pltpu
from jax.sharding import PartitionSpec as P

loss_weight = 16.0
nothing = -1e30
f32, bf16, i32 = jnp.float32, jnp.bfloat16, jnp.int32
HIGHEST = lax.Precision.HIGHEST


near, far = pl.BlockSpec(memory_space=pltpu.VMEM), pl.BlockSpec(memory_space=pl.ANY)


def settings(mib=32):
    return pltpu.CompilerParams(vmem_limit_bytes=mib * 1024 * 1024)


def by_rows(a, b, precision=None):
    return lax.dot_general(
        a, b, (((1,), (1,)), ((), ())), preferred_element_type=f32, precision=precision
    )


def plain(a, b, precision=None):
    return lax.dot_general(
        a, b, (((1,), (0,)), ((), ())), preferred_element_type=f32, precision=precision
    )


def iota(shape, dim):
    return lax.broadcasted_iota(i32, shape, dim)


def rows_of(codes, per_tile):
    entries = codes.shape[1]
    wide = entries * per_tile
    spread = (iota((entries, wide), 0) == iota((entries, wide), 1) // per_tile).astype(bf16)
    expanded = plain(codes.astype(bf16), spread).astype(i32)
    return expanded * per_tile + iota(expanded.shape, 1) % per_tile


def announce_kernel(panel, per_tile, owner_ref, cand_ref, teacher_ref, out_ref, rows_ref):
    tiles = owner_ref.shape[1]
    entries = 2 * tiles
    tokens = tiles * per_tile
    slots = out_ref.shape[0]
    owner = jnp.concatenate([owner_ref[0:1, :], owner_ref[1:2, :]], axis=1).astype(f32)
    owners = jnp.broadcast_to(owner, (entries, entries))
    earlier = iota((entries, entries), 0) % tiles < iota((entries, entries), 1) % tiles
    same = (owners == owners.T) & earlier
    rank = jnp.sum(jnp.where(same, 1.0, 0.0), axis=0, keepdims=True)
    code = owner * 2.0 + rank
    rows = rows_of(jnp.broadcast_to(code, (8, entries)), per_tile)
    rows_ref[...] = rows
    cand = cand_ref[...]
    teacher = teacher_ref[...]
    columns = (
        jnp.where(cand < panel, cand + 1, 0).astype(f32),
        jnp.where(cand >= panel, cand - panel + 1, 0).astype(f32),
    )
    width = 2 * cand.shape[0]
    for which in range(8):
        row = iota((slots, tokens), 0) * 8 + which
        told = jnp.zeros((slots, width), f32)
        for group in range(2):
            hot = jnp.where(row == rows[0:1, group * tokens : (group + 1) * tokens], 1.0, 0.0)
            told = told + by_rows(
                hot, jnp.concatenate([columns[group], teacher], axis=0), HIGHEST
            )
        out_ref[:, which * width : (which + 1) * width] = told
    out_ref[:, 8 * width : 8 * width + entries] = jnp.broadcast_to(code, (slots, entries))


def announce(tile_owners, cand, teacher, panel, per_tile, owners):
    entries = 2 * tile_owners.shape[1]
    return pl.pallas_call(
        functools.partial(announce_kernel, panel, per_tile),
        out_shape=(
            jax.ShapeDtypeStruct((owners, 16 * cand.shape[0] + entries), f32),
            jax.ShapeDtypeStruct((8, entries * per_tile), i32),
        ),
        compiler_params=settings(58),
        name="announce",
    )(tile_owners, cand, teacher)


def route_kernel(per_tile, tok_ref, codes_ref, hidden_ref, out_ref, rows_ref, held_ref):
    step = pl.program_id(0)
    width = hidden_ref.shape[0]
    owners, lanes, _ = held_ref.shape
    blocks = lanes // 8
    tokens = rows_ref.shape[1] // 2
    pairs = hidden_ref.shape[1] // (2 * tokens)
    steps = blocks // (2 * pairs)

    @pl.when(step == 0)
    def _():
        rows_ref[...] = rows_of(codes_ref[...], per_tile)

    @pl.when(step < steps)
    def _():
        chunk = 32
        row = iota((chunk * 8, tokens), 0).astype(f32).astype(bf16)
        for pair in range(pairs):
            first = step * (2 * pairs) + 2 * pair
            rows = [rows_ref[pl.ds(first + w, 1), :] for w in range(2)]
            for at in range(0, owners, chunk):
                here = [(r - at * 8).astype(f32).astype(bf16) for r in rows]
                parts = []
                for which in range(2):
                    hot = jnp.where(
                        (row == here[which][:, 0:tokens])
                        | (row == here[which][:, tokens : 2 * tokens]),
                        jnp.ones_like(row),
                        jnp.zeros_like(row),
                    )
                    lane = (2 * pair + which) * tokens
                    part = by_rows(hot, hidden_ref[:, lane : lane + tokens])
                    parts.append(part.reshape(chunk, 8, width))
                held_ref[at : at + chunk, pl.ds(pl.multiple_of(first * 8, 16), 16), :] = (
                    jnp.concatenate(parts, axis=1).astype(bf16)
                )

    @pl.when(step >= steps)
    def _():
        count = out_ref.shape[0]
        for k in range(count):
            out_ref[k] = held_ref[(step - steps) * count + k].T


def route(tok, told, hidden, per_tile, blocks):
    width, total = hidden.shape
    owners = told.shape[0]
    tokens = total // blocks
    entries = 2 * tokens // per_tile
    pairs = 4
    steps = blocks // (2 * pairs)
    turn = 32
    return pl.pallas_call(
        functools.partial(route_kernel, per_tile),
        grid_spec=pltpu.PrefetchScalarGridSpec(
            num_scalar_prefetch=1,
            grid=(steps + owners // turn,),
            in_specs=[
                pl.BlockSpec((blocks, entries), lambda s, t: (t[0], told.shape[1] // entries - 1)),
                pl.BlockSpec(
                    (width, 2 * pairs * tokens), lambda s, t: (0, jnp.minimum(s, steps - 1))
                ),
            ],
            out_specs=pl.BlockSpec(
                (turn, width, blocks * 8), lambda s, t: (jnp.maximum(s - steps, 0), 0, 0)
            ),
            scratch_shapes=[
                pltpu.VMEM((blocks, 2 * tokens), i32),
                pltpu.VMEM((owners, blocks * 8, width), bf16),
            ],
        ),
        out_shape=jax.ShapeDtypeStruct((owners, width, blocks * 8), bf16),
        compiler_params=settings(58),
        name="route",
    )(tok, told, hidden)


def place_kernel(per_tile, owner_ref, told_ref, dense_ref, facts_ref):
    sources = told_ref.shape[0]
    lanes = sources * 8
    width = told_ref.shape[1] // 9
    turned = jnp.stack(
        [told_ref[:, k * width : (k + 1) * width] for k in range(8)], axis=1
    ).reshape(lanes, width).T
    codes = jnp.broadcast_to(
        told_ref[:, 8 * width :].reshape(sources, 1, width), (sources, 8, width)
    ).reshape(lanes, width).T
    picks = width // 2
    columns = turned[0:picks].astype(i32) - 1
    teacher = turned[picks:]
    target = jnp.exp(teacher)
    panel = dense_ref.shape[0]
    chunk = 128
    place = iota((chunk, lanes), 0)
    for at in range(0, panel, chunk):
        dense = jnp.zeros((chunk, lanes), f32)
        for k in range(picks):
            dense = jnp.where(place == columns[k : k + 1] - at, target[k : k + 1], dense)
        dense_ref[at : at + chunk, :] = dense
    half = codes.shape[0] // 2
    other = jnp.concatenate([codes[half:], codes[:half]], axis=0)
    slot = (iota((1, lanes), 1) // per_tile) % 2
    mine = (owner_ref[0] * 2 + slot).astype(f32)
    partner = jnp.sum(jnp.where(codes == mine, other + 1.0, 0.0), axis=0, keepdims=True)
    mass = jnp.sum(target, axis=0, keepdims=True)
    entropy = jnp.sum(jnp.where(columns >= 0, target * teacher, 0.0), axis=0, keepdims=True)
    facts_ref[...] = jnp.concatenate(
        [partner, mass, entropy, jnp.zeros((5, lanes), f32)], axis=0
    )


def place(owner, told, panel, per_tile):
    sources, width = told.shape
    rows = sources * 8
    block = 16
    return pl.pallas_call(
        functools.partial(place_kernel, per_tile),
        grid_spec=pltpu.PrefetchScalarGridSpec(
            num_scalar_prefetch=1,
            grid=(sources // block,),
            in_specs=[pl.BlockSpec((block, width), lambda s, o: (s, 0))],
            out_specs=[
                pl.BlockSpec((panel, block * 8), lambda s, o: (0, s)),
                pl.BlockSpec((8, block * 8), lambda s, o: (0, s)),
            ],
        ),
        out_shape=(
            jax.ShapeDtypeStruct((panel, rows), f32),
            jax.ShapeDtypeStruct((8, rows), f32),
        ),
        compiler_params=settings(),
        cost_estimate=pl.CostEstimate(
            flops=2 * 64 * panel * rows, bytes_accessed=8 * panel * rows, transcendentals=64 * rows
        ),
        name="place",
    )(owner, told)


def score_kernel(
    bounds, head_ref, rows_ref, dense_ref, facts_ref, part_ref, own_ref, told_ref, total_ref, held_ref, sems
):
    groups, _, lanes = rows_ref.shape
    copies = []
    for k, (low, high) in enumerate(bounds):
        copies.append(
            pltpu.make_async_copy(
                rows_ref.at[:, low:high, :], held_ref.at[:, low:high, :], sems.at[k]
            )
        )
    for copy in copies:
        copy.start()
    for k, (low, high) in enumerate(bounds):
        copies[k].wait()
        for t in range(groups):
            here = slice(t * lanes, (t + 1) * lanes)
            product = plain(head_ref[:, low:high], held_ref[t, low:high, :])
            total_ref[:, here] = product if k == 0 else total_ref[:, here] + product
    count = total_ref.shape[1]
    chunk = 128
    logs, largest, shares = [], [], []
    for at in range(0, count, chunk):
        here = slice(at, at + chunk)
        dense = dense_ref[:, here]
        score = total_ref[:, here]
        named = dense > 0.0
        most = jnp.max(jnp.where(named, score, nothing), axis=0, keepdims=True)
        part = jnp.where(named, jnp.exp(score - most), 0.0)
        part_ref[:, here] = part
        whole = jnp.sum(part, axis=0, keepdims=True)
        log = jnp.where(whole > 0.0, most + jnp.log(jnp.maximum(whole, 1.0)), nothing)
        shares.append(
            facts_ref[2:3, here] - jnp.sum(dense * score, axis=0, keepdims=True)
        )
        logs.append(log)
        largest.append(most)
    logs = jnp.concatenate(logs, axis=1)
    largest = jnp.concatenate(largest, axis=1)
    shares = jnp.concatenate(shares, axis=1)
    own_ref[...] = jnp.concatenate([largest, logs, jnp.zeros((6, count), f32)], axis=0)
    owners = told_ref.shape[0]
    told_ref[:, 0:count] = jnp.broadcast_to(logs, (owners, count))
    home = iota((owners, count), 1) // 8 == iota((owners, count), 0)
    which = (iota((count, 128), 0) % 8 == iota((count, 128), 1)).astype(f32)
    told_ref[:, count : count + 128] = plain(
        jnp.where(home, jnp.broadcast_to(shares, (owners, count)), 0.0), which, HIGHEST
    )


def score(head, rows, dense, facts, owners):
    panel, width = head.shape
    groups, _, lanes = rows.shape
    count = groups * lanes
    block = 1024
    cuts = [0, block // 4] + list(range(block, width, block)) + [width]
    bounds = list(zip(cuts[:-1], cuts[1:]))
    return pl.pallas_call(
        functools.partial(score_kernel, bounds),
        in_specs=[near, far, near, near],
        out_specs=[near, near, near],
        out_shape=(
            jax.ShapeDtypeStruct((panel, count), f32),
            jax.ShapeDtypeStruct((8, count), f32),
            jax.ShapeDtypeStruct((owners, count + 128), f32),
        ),
        scratch_shapes=[
            pltpu.VMEM((panel, count), f32),
            pltpu.VMEM((groups, width, lanes), bf16),
            pltpu.SemaphoreType.DMA((len(bounds),)),
        ],
        compiler_params=settings(24),
        name="score",
    )(head, rows, dense, facts)


def log_sum(a, b):
    most = jnp.maximum(a, b)
    return most + jnp.log(jnp.exp(a - most) + jnp.exp(b - most))


def turn_kernel(part_ref, dense_ref, part_out, dense_out):
    part_out[...] = part_ref[...].T
    dense_out[...] = (loss_weight * dense_ref[...]).T


def turn(part, dense):
    panel, count = part.shape
    block = 256
    columns = pl.BlockSpec((panel, block), lambda s: (0, s))
    rows = pl.BlockSpec((block, panel), lambda s: (s, 0))
    return pl.pallas_call(
        turn_kernel,
        grid=(count // block,),
        in_specs=[columns, columns],
        out_specs=[rows, rows],
        out_shape=[jax.ShapeDtypeStruct((count, panel), f32)] * 2,
        compiler_params=settings(24),
        cost_estimate=pl.CostEstimate(
            flops=4 * panel * count, bytes_accessed=16 * panel * count, transcendentals=0
        ),
        name="turn",
    )(part, dense)


def part_kernel(
    per_tile, logs_ref, facts_ref, own_ref, part_ref, dense_ref, head_ref, out_ref, weight_ref, held_ref, sems
):
    count, panel = part_ref.shape
    owners = logs_ref.shape[0]
    chunk = 128
    for at in range(0, count, chunk):
        here = slice(at, at + chunk)
        logs = logs_ref[:, here]
        partner = facts_ref[0:1, here].astype(i32) - 1
        slot = (iota((1, chunk), 1) // per_tile) % 2
        across = jnp.where(
            slot == 0, pltpu.roll(logs, chunk - per_tile, 1), pltpu.roll(logs, per_tile, 1)
        )
        picked = jnp.where(
            iota((owners, chunk), 0) == partner // 2,
            jnp.where(partner % 2 == slot, logs, across),
            0.0,
        )
        other = jnp.sum(picked, axis=0, keepdims=True)
        total = log_sum(own_ref[1:2, here], other)
        scale = loss_weight * facts_ref[1:2, here] * jnp.exp(own_ref[0:1, here] - total)
        scale = jnp.broadcast_to(scale, (chunk, chunk)).T
        for col in range(0, panel, chunk):
            there = slice(col, col + chunk)
            weight = part_ref[here, there] * scale - dense_ref[here, there]
            weight_ref[here, there] = weight.astype(bf16)
    slots, _, block = held_ref.shape

    def leave(k):
        place = pl.ds(pl.multiple_of(k * block, block), block)
        return pltpu.make_async_copy(
            held_ref.at[k % slots], out_ref.at[:, place], sems.at[k % slots]
        )

    def one(k, carry):
        @pl.when(k >= slots)
        def _():
            leave(k - slots).wait()

        place = pl.ds(pl.multiple_of(k * block, block), block)
        held_ref[k % slots] = plain(weight_ref[...], head_ref[:, place]).astype(bf16)
        leave(k).start()
        return carry

    blocks = out_ref.shape[1] // block
    lax.fori_loop(0, blocks, one, 0)
    for k in range(blocks - slots, blocks):
        leave(k).wait()


def grad_parts(logs, facts, own, part, dense, head, per_tile):
    panel, width = head.shape
    count = part.shape[0]
    block = 512
    return pl.pallas_call(
        functools.partial(part_kernel, per_tile),
        in_specs=[near] * 6,
        out_specs=[far, near],
        out_shape=(
            jax.ShapeDtypeStruct((count, width), bf16),
            jax.ShapeDtypeStruct((count, panel), bf16),
        ),
        scratch_shapes=[
            pltpu.VMEM((2, count, block), bf16),
            pltpu.SemaphoreType.DMA((2,)),
        ],
        compiler_params=settings(16),
        name="grad_parts",
    )(logs, facts, own, part, dense, head)


def head_kernel(weight_ref, rows_ref, out_ref, turned_ref):
    groups, _, lanes = rows_ref.shape

    @pl.when(pl.program_id(0) == 0)
    def _():
        for at in range(0, weight_ref.shape[0], 128):
            turned_ref[:, at : at + 128] = weight_ref[at : at + 128, :].T

    total = by_rows(turned_ref[:, 0:lanes], rows_ref[0])
    for t in range(1, groups):
        total = total + by_rows(turned_ref[:, t * lanes : (t + 1) * lanes], rows_ref[t])
    out_ref[...] = total.astype(bf16)


def grad_of_head(weight, rows):
    count, panel = weight.shape
    groups, width, lanes = rows.shape
    block = 512
    return pl.pallas_call(
        head_kernel,
        grid=(width // block,),
        in_specs=[
            pl.BlockSpec((count, panel), lambda s: (0, 0)),
            pl.BlockSpec((groups, block, lanes), lambda s: (0, s, 0)),
        ],
        out_specs=pl.BlockSpec((panel, block), lambda s: (0, s)),
        out_shape=jax.ShapeDtypeStruct((panel, width), bf16),
        scratch_shapes=[pltpu.VMEM((panel, count), bf16)],
        compiler_params=settings(),
        cost_estimate=pl.CostEstimate(
            flops=2 * panel * count * width,
            bytes_accessed=2 * (panel + count) * width,
            transcendentals=0,
        ),
        name="grad_of_head",
    )(weight, rows)


def loss_kernel(me_ref, logs_ref, rows_ref, teacher_ref, loss_ref, table_ref):
    owners = logs_ref.shape[0]
    tokens = teacher_ref.shape[1]
    count = table_ref.shape[1]
    mine = iota((count, 128), 0) == me_ref[0] * 8 + iota((count, 128), 1)
    mine = jnp.where(mine & (iota((count, 128), 1) < 8), 1.0, 0.0)
    logs = plain(logs_ref[:, 0:count], mine, HIGHEST).T
    shares = logs_ref[:, count : count + 128].T
    found = []
    total = jnp.zeros((1, tokens), f32)
    for group in range(2):
        row = rows_ref[0:1, group * tokens : (group + 1) * tokens]
        owner = jnp.where(iota((owners, tokens), 0) == row // 8, 1.0, 0.0)
        slot = iota((128, tokens), 0) == row % 8
        for table, kept in ((logs, True), (shares, False)):
            got = jnp.where(slot, plain(table, owner, HIGHEST), 0.0)
            got = jnp.sum(got, axis=0, keepdims=True)
            if kept:
                found.append(got)
            else:
                total = total + got
    teacher = teacher_ref[...]
    mass = jnp.sum(jnp.exp(teacher), axis=0, keepdims=True)
    loss_ref[...] = total + mass * log_sum(found[0], found[1])
    first, second = rows_ref[0:1, 0:tokens], rows_ref[0:1, tokens : 2 * tokens]
    for at in range(0, count, 128):
        row = iota((128, tokens), 0) + at
        hot = jnp.where((row == first) | (row == second), 1.0, 0.0)
        table_ref[:, at : at + 128] = hot.T.astype(bf16)


def losses(me, logs, rows, teacher, count):
    tokens = teacher.shape[1]
    return pl.pallas_call(
        loss_kernel,
        in_specs=[pl.BlockSpec(memory_space=pltpu.SMEM)] + [pl.BlockSpec(memory_space=pltpu.VMEM)] * 3,
        out_shape=(
            jax.ShapeDtypeStruct((1, tokens), f32),
            jax.ShapeDtypeStruct((tokens, count), bf16),
        ),
        compiler_params=settings(),
        cost_estimate=pl.CostEstimate(
            flops=12 * 2 * count * tokens * 128, bytes_accessed=4 * count * tokens, transcendentals=0
        ),
        name="losses",
    )(me, logs, rows, teacher)


def combine_kernel(table_ref, parts_ref, out_ref):
    out_ref[...] = plain(table_ref[...], parts_ref[...]).astype(bf16)


def combine(table, parts):
    tokens, count = table.shape
    width = parts.shape[1]
    block = width // 2
    return pl.pallas_call(
        combine_kernel,
        grid=(width // block,),
        in_specs=[
            pl.BlockSpec((tokens, count), lambda s: (0, 0)),
            pl.BlockSpec((count, block), lambda s: (0, s)),
        ],
        out_specs=pl.BlockSpec((tokens, block), lambda s: (0, s)),
        out_shape=jax.ShapeDtypeStruct((tokens, width), bf16),
        compiler_params=settings(58),
        name="combine",
    )(table, parts)


def exchange(values):
    owners, width = values.shape
    moved = lax.all_to_all(
        values.reshape(owners, 1, width), ("tok", "voc"), split_axis=0, concat_axis=0, tiled=True
    )
    return moved.reshape(owners, width)


def exchange_tiles(values):
    return lax.all_to_all(values, ("tok", "voc"), split_axis=0, concat_axis=0, tiled=True)


def body(hidden, head_weight, tile_owners, cand_pos, teacher_logp):
    panel, width = head_weight.shape
    tiles = tile_owners.shape[0]
    tokens = cand_pos.shape[0]
    per_tile = tokens // tiles
    tok_size, blocks = lax.axis_size("tok"), lax.axis_size("voc")
    owners = tok_size * blocks
    count = owners * 8
    tok = lax.axis_index("tok")
    me = (tok * blocks + lax.axis_index("voc")).astype(i32).reshape(1)
    teacher = teacher_logp.T
    told, home_rows = announce(tile_owners.T, cand_pos.T, teacher, panel, per_tile, owners)
    told = exchange(told)
    sent = route(tok.astype(i32).reshape(1), told, hidden.T, per_tile, blocks)
    rows = exchange_tiles(sent).reshape(tok_size, width, blocks * 8)
    dense, facts = place(me, told, panel, per_tile)
    part, own, logs = score(head_weight, rows, dense, facts, owners)
    logs = exchange(logs)
    part_rows, dense_rows = turn(part, dense)
    parts, weight = grad_parts(logs, facts, own, part_rows, dense_rows, head_weight, per_tile)
    home_parts = exchange_tiles(parts.reshape(owners, 8, width)).reshape(count, width)
    grad_head = grad_of_head(weight, rows)
    loss, table = losses(me, logs, home_rows, teacher, count)
    grad_hidden = combine(table, home_parts)
    return (loss.reshape(tokens), grad_hidden, grad_head)


def solution(mesh):
    placed = (
        P("tok", "voc"),
        P(("tok", "voc"), None),
        P(("tok", "voc"), None),
        P(("tok", "voc"), None),
        P(("tok", "voc"), None),
    )
    return jax.shard_map(
        body,
        mesh=mesh,
        in_specs=placed,
        out_specs=(P(("tok", "voc")), P(("tok", "voc"), None), P(("tok", "voc"), None)),
        check_vma=False,
    )
```

time: 402 us -> 394 us (0.980)
  local copies, waits for them, and re-layouts: 10.3 us -> 28.9 us
  blocking collectives: 16.6 us -> 0 us
  Pallas kernels: 103 us -> 88.6 us
  starting transfers between devices: 24.9 us -> 30.7 us
    all_to_all x1 -> x0, blocking collectives: 16.6 us -> none  [exchange(): lax.all_to_all(values, ('tok', 'voc'), split_axis=0, concat_axis=0, tiled...]
    unnamed x13 -> x28, local copies, waits for them, and re-layouts: 8.95 us -> 25 us
    pallas_call x3 -> x4, Pallas kernels: 52.1 us -> 39.6 us  [the longest x1 12.9 us: route(): pl.pallas_call(functools.partial(route_kernel, per_tile), grid_spec=pltpu...]
    all_to_all x3 -> x4, starting transfers between devices: 24.9 us -> 30.7 us  [the longest x2 15.5 us: exchange(): lax.all_to_all(values.reshape(owners, 1, width), ('tok', 'voc'), split_ax...]
    all_to_all x3 -> x4, waiting for transfers between devices: 245 us -> 244 us  [the longest x2 228 us: exchange_tiles(): lax.all_to_all(values, ('tok', 'voc'), split_axis=0, concat_axis=0, tiled...]
  transfers between devices with their start and end apart: 3 -> 4, of which waited for: 3 -> 4; matrix products, arithmetic and copies ran while one was open for 0% -> 0% of each run, Pallas kernels for 9% -> 10%
where the time goes in v2:
time: 394 us; the launch traced here: 393 us
  waiting for transfers between devices  244 us (62%)
  Pallas kernels  88.6 us (22%)
  starting transfers between devices  30.7 us (8%)
  local copies, waits for them, and re-layouts  28.9 us (7%)
    all_to_all x2, waiting for transfers between devices, exchange_tiles(): lax.all_to_all(values, ('tok', 'voc'), split_axis=0, concat_axis=0, tiled...  228 us
    unnamed x28, local copies, waits for them, and re-layouts  25 us
    pallas_call x1, Pallas kernels, place(): pl.pallas_call(functools.partial(place_kernel, per_tile), grid_spec=pltpu...  21.2 us
    all_to_all x2, starting transfers between devices, exchange(): lax.all_to_all(values.reshape(owners, 1, width), ('tok', 'voc'), split_ax...  15.5 us
    all_to_all x2, waiting for transfers between devices, exchange(): lax.all_to_all(values.reshape(owners, 1, width), ('tok', 'voc'), split_ax...  15.2 us
    all_to_all x2, starting transfers between devices, exchange_tiles(): lax.all_to_all(values, ('tok', 'voc'), split_axis=0, concat_axis=0, tiled...  15.2 us
    pallas_call x1, Pallas kernels, grad_of_head(): pl.pallas_call(head_kernel, grid=(width // block,), in_specs=[pl.BlockSpe...  15.1 us
    pallas_call x1, Pallas kernels, route(): pl.pallas_call(functools.partial(route_kernel, per_tile), grid_spec=pltpu...  12.9 us
  transfers between devices with their start and end apart: 4, of which 4 were waited for; matrix products, arithmetic and copies ran while one was open for 0% of the time, Pallas kernels for 10%

profile of v2, /device:TPU:97, one launch (start us, length us, event | category | flops | bytes accessed | tf_op | source)
XLA Modules:
  0.0 392.6 jit_solution(8920052286245216419)
XLA Ops:
  0.6 3.9 %announce.1 = (f32[128,1152]{1,0:T(8,128)}, s32[8,512]{1,0:T(8,128)}) custom-call(s32[2,64]{1,0:T(2,128)} %bitcast.29, s32[64,256]{1,0:T(8,128)} %bitcast.28, f32[64,256]{1,0:T(8,128)} %bitcast.24), custom_call_target="tpu_custom_call" | custom-call | tf_op jit(solution)/shard_map/announce/pallas_call | solution.py:81
  4.6 2.5 copy.8
  7.1 10.2 %all-to-all-start = ((f32[128,1,1152]{2,1,0:T(1,128)}), f32[128,1,1152]{2,1,0:T(1,128)S(1)}, u32[]{:S(2)}, u32[]{:S(2)}) async-start(f32[128,1,1152]{2,1,0:T(1,128)} %copy.8), calls=%async_computation | async-start | bytes 1179648 | tf_op jit(solution)/shard_map/all_to_all | solution.py:517
  17.2 11.6 %all-to-all-done = f32[128,1,1152]{2,1,0:T(1,128)S(1)} async-done(((f32[128,1,1152]{2,1,0:T(1,128)}), f32[128,1,1152]{2,1,0:T(1,128)S(1)}, u32[]{:S(2)}, u32[]{:S(2)}) %all-to-all-start) | async-done | bytes 589856 | tf_op jit(solution)/shard_map/all_to_all | solution.py:517
  28.9 0.9 copy.15
  29.7 12.9 %route.1 = bf16[128,160,256]{2,1,0:T(8,128)(2,1)} custom-call(s32[1]{0:T(128)} %bitcast.1.tok_ref, f32[128,1152]{1,0:T(8,128)} %bitcast.19, bf16[160,8192]{1,0:T(8,128)(2,1)} %bitcast.26), custom_call_target="tpu_custom_call" | custom-call | tf_op jit(solution)/shard_map/route/pallas_call | solution.py:144
  42.7 7.5 %all-to-all-start.1 = ((bf16[128,160,256]{2,1,0:T(8,128)(2,1)}), bf16[128,160,256]{2,1,0:T(8,128)(2,1)}, u32[]{:S(2)}, u32[]{:S(2)}) async-start(bf16[128,160,256]{2,1,0:T(8,128)(2,1)} %route.1), calls=%async_computation.1 | async-start | bytes 20971520 | tf_op jit(solution)/shard_map/all_to_all | solution.py:524
  50.3 1.1 copy-done.3
  51.3 21.2 %place.1 = (f32[768,1024]{1,0:T(8,128)S(1)}, f32[8,1024]{1,0:T(8,128)S(1)}) custom-call(s32[1]{0:T(128)} %bitcast.owner_ref.me_ref, f32[128,1152]{1,0:T(8,128)S(1)} %bitcast.20), custom_call_target="tpu_custom_call" | custom-call | flops 100663296 | bytes 6291456 | tf_op jit(solution)/shard_map/place/pallas_call | solution.py:207
  72.6 114.1 %all-to-all-done.1 = bf16[128,160,256]{2,1,0:T(8,128)(2,1)} async-done(((bf16[128,160,256]{2,1,0:T(8,128)(2,1)}), bf16[128,160,256]{2,1,0:T(8,128)(2,1)}, u32[]{:S(2)}, u32[]{:S(2)}) %all-to-all-start.1) | async-done | bytes 10485792 | tf_op jit(solution)/shard_map/all_to_all | solution.py:524
  186.7 3.2 copy-done
  189.9 12.1 %score.1 = (f32[768,1024]{1,0:T(8,128)S(1)}, f32[8,1024]{1,0:T(8,128)S(1)}, f32[128,1152]{1,0:T(8,128)S(1)}) custom-call(bf16[768,5120]{1,0:T(8,128)(2,1)S(1)} %copy-done, bf16[4,5120,256]{2,1,0:T(8,128)(2,1)} %bitcast.7.rows_ref, f32[768,1024]{1,0:T(8,128)S(1)} %get-tuple-element.17.dense_ref, f32[8,1024]{1,0:T(8,128)S(1)} %get-tuple-element.18.facts_ref), custom_call_target="tpu_custom_call" | custom-call | tf_op jit(solution)/shard_map/score/pallas_call | solution.py:287
  202.0 1.7 copy-done.8
  203.7 1.4 copy.9
  205.1 5.3 %all-to-all-start.2 = ((f32[128,1,1152]{2,1,0:T(1,128)}), f32[128,1,1152]{2,1,0:T(1,128)}, u32[]{:S(2)}, u32[]{:S(2)}) async-start(f32[128,1,1152]{2,1,0:T(1,128)} %copy.9), calls=%async_computation.2 | async-start | bytes 1179648 | tf_op jit(solution)/shard_map/all_to_all | solution.py:517
  210.4 1.9 copy-done.9
  212.3 2.4 turn.1
  214.7 1.7 copy-done.4
  216.4 1.8 copy-done.6
  218.1 3.6 all-to-all-done.2
  221.7 1.1 copy.14
  222.9 3.2 copy-done.1
  226.1 1.9 copy-done.5
  228.0 1.9 copy-done.7
  229.9 12.2 %grad_parts.1 = (bf16[1024,5120]{1,0:T(8,128)(2,1)S(1)}, bf16[1024,768]{1,0:T(8,128)(2,1)S(1)}) custom-call(f32[128,1152]{1,0:T(8,128)S(1)} %bitcast.21, f32[8,1024]{1,0:T(8,128)S(1)} %get-tuple-element.18.facts_ref, f32[8,1024]{1,0:T(8,128)S(1)} %get-tuple-element.23.own_ref, f32[1024,768]{1,0:T(8,128)S(1)} %copy-done.5, f32[1024,768]{1,0:T(8,128)S(1)} %copy-done.7, ...), custom_call_target="tpu_custom_call" | custom-call | tf_op jit(solution)/shard_map/grad_parts/pallas_call | solution.py:390
  242.1 4.0 %copy-done.2 = bf16[1024,5120]{1,0:T(8,128)(2,1)} copy-done((bf16[1024,5120]{1,0:T(8,128)(2,1)}, bf16[1024,5120]{1,0:T(8,128)(2,1)S(1)}, u32[]{:S(2)}) %copy-start.2) | copy-done | bytes 10485784
  246.1 7.7 %all-to-all-start.3 = ((bf16[128,8,5120]{2,1,0:T(8,128)(2,1)}), bf16[128,8,5120]{2,1,0:T(8,128)(2,1)}, u32[]{:S(2)}, u32[]{:S(2)}) async-start(bf16[128,8,5120]{2,1,0:T(8,128)(2,1)} %bitcast.18), calls=%async_computation.3 | async-start | bytes 20971520 | tf_op jit(solution)/shard_map/all_to_all | solution.py:524
  253.7 1.8 losses.1
  255.6 0.8 copy-done.10
  256.4 15.1 %grad_of_head.1 = bf16[768,5120]{1,0:T(8,128)(2,1)} custom-call(bf16[1024,768]{1,0:T(8,128)(2,1)S(1)} %get-tuple-element.28.weight_ref, bf16[4,5120,256]{2,1,0:T(8,128)(2,1)} %bitcast.7.rows_ref), custom_call_target="tpu_custom_call" | custom-call | flops 8053063680 | bytes 18350080 | tf_op jit(solution)/shard_map/grad_of_head/pallas_call | solution.py:425
  271.5 114.3 %all-to-all-done.3 = bf16[128,8,5120]{2,1,0:T(8,128)(2,1)} async-done(((bf16[128,8,5120]{2,1,0:T(8,128)(2,1)}), bf16[128,8,5120]{2,1,0:T(8,128)(2,1)}, u32[]{:S(2)}, u32[]{:S(2)}) %all-to-all-start.3) | async-done | bytes 10485792 | tf_op jit(solution)/shard_map/all_to_all | solution.py:524
  385.8 6.8 %combine.1 = bf16[256,5120]{1,0:T(8,128)(2,1)} custom-call(bf16[256,1024]{1,0:T(8,128)(2,1)} %copy-done.10, bf16[1024,5120]{1,0:T(8,128)(2,1)} %bitcast.11.parts_ref), custom_call_target="tpu_custom_call" | custom-call | tf_op jit(solution)/shard_map/combine/pallas_call | solution.py:501
  (15 shorter events, 0.0 us)
Async XLA Ops:
  7.1 21.8 %all-to-all-start = ((f32[128,1,1152]{2,1,0:T(1,128)}), f32[128,1,1152]{2,1,0:T(1,128)S(1)}, u32[]{:S(2)}, u32[]{:S(2)}) async-start(f32[128,1,1152]{2,1,0:T(1,128)} %copy.8), calls=%async_computation | async-start | bytes 1179648 | tf_op jit(solution)/shard_map/all_to_all | solution.py:517
  42.7 144.0 %all-to-all-start.1 = ((bf16[128,160,256]{2,1,0:T(8,128)(2,1)}), bf16[128,160,256]{2,1,0:T(8,128)(2,1)}, u32[]{:S(2)}, u32[]{:S(2)}) async-start(bf16[128,160,256]{2,1,0:T(8,128)(2,1)} %route.1), calls=%async_computation.1 | async-start | bytes 20971520 | tf_op jit(solution)/shard_map/all_to_all | solution.py:524
  50.2 1.1 copy-start.3
  186.7 3.2 copy-start
  202.0 1.7 copy-start.8
  205.1 16.7 %all-to-all-start.2 = ((f32[128,1,1152]{2,1,0:T(1,128)}), f32[128,1,1152]{2,1,0:T(1,128)}, u32[]{:S(2)}, u32[]{:S(2)}) async-start(f32[128,1,1152]{2,1,0:T(1,128)} %copy.9), calls=%async_computation.2 | async-start | bytes 1179648 | tf_op jit(solution)/shard_map/all_to_all | solution.py:517
  210.4 1.9 copy-start.9
  214.7 1.7 copy-start.4
  216.4 1.8 copy-start.6
  222.8 3.2 copy-start.1
  226.1 1.9 copy-start.5
  228.0 1.9 copy-start.7
  242.1 4.0 %copy-start.2 = (bf16[1024,5120]{1,0:T(8,128)(2,1)}, bf16[1024,5120]{1,0:T(8,128)(2,1)S(1)}, u32[]{:S(2)}) copy-start(bf16[1024,5120]{1,0:T(8,128)(2,1)S(1)} %get-tuple-element.27) | copy-start | bytes 31457284
  246.0 7.7 %copy-start.11 = (f32[256,64]{0,1:T(8,128)S(1)}, f32[256,64]{0,1:T(8,128)}, u32[]{:S(2)}) copy-start(f32[256,64]{0,1:T(8,128)} %param.9) | copy-start | bytes 196612
  246.1 7.7 %copy-start.12 = (s32[8,512]{1,0:T(8,128)S(1)}, s32[8,512]{1,0:T(8,128)}, u32[]{:S(2)}) copy-start(s32[8,512]{1,0:T(8,128)} %get-tuple-element.20.rows_ref) | copy-start | bytes 49156
  246.1 139.7 %all-to-all-start.3 = ((bf16[128,8,5120]{2,1,0:T(8,128)(2,1)}), bf16[128,8,5120]{2,1,0:T(8,128)(2,1)}, u32[]{:S(2)}, u32[]{:S(2)}) async-start(bf16[128,8,5120]{2,1,0:T(8,128)(2,1)} %bitcast.18), calls=%async_computation.3 | async-start | bytes 20971520 | tf_op jit(solution)/shard_map/all_to_all | solution.py:524
  255.6 0.8 copy-start.10

commit v3 on v2

--- a/solution.py
+++ b/solution.py
@@ -72,8 +72,8 @@
             told = told + by_rows(
                 hot, jnp.concatenate([columns[group], teacher], axis=0), HIGHEST
             )
-        out_ref[:, which * width : (which + 1) * width] = told
-    out_ref[:, 8 * width : 8 * width + entries] = jnp.broadcast_to(code, (slots, entries))
+        out_ref[:, 0, which * width : (which + 1) * width] = told
+    out_ref[:, 0, 8 * width : 8 * width + entries] = jnp.broadcast_to(code, (slots, entries))
 
 
 def announce(tile_owners, cand, teacher, panel, per_tile, owners):
@@ -81,7 +81,7 @@
     return pl.pallas_call(
         functools.partial(announce_kernel, panel, per_tile),
         out_shape=(
-            jax.ShapeDtypeStruct((owners, 16 * cand.shape[0] + entries), f32),
+            jax.ShapeDtypeStruct((owners, 1, 16 * cand.shape[0] + entries), f32),
             jax.ShapeDtypeStruct((8, entries * per_tile), i32),
         ),
         compiler_params=settings(58),
@@ -100,7 +100,7 @@
 
     @pl.when(step == 0)
     def _():
-        rows_ref[...] = rows_of(codes_ref[...], per_tile)
+        rows_ref[...] = rows_of(codes_ref[:, 0, :], per_tile)
 
     @pl.when(step < steps)
     def _():
@@ -147,7 +147,7 @@
             num_scalar_prefetch=1,
             grid=(steps + owners // turn,),
             in_specs=[
-                pl.BlockSpec((blocks, entries), lambda s, t: (t[0], told.shape[1] // entries - 1)),
+                pl.BlockSpec((blocks, 1, entries), lambda s, t: (t[0], 0, told.shape[2] // entries - 1)),
                 pl.BlockSpec(
                     (width, 2 * pairs * tokens), lambda s, t: (0, jnp.minimum(s, steps - 1))
                 ),
@@ -169,12 +169,12 @@
 def place_kernel(per_tile, owner_ref, told_ref, dense_ref, facts_ref):
     sources = told_ref.shape[0]
     lanes = sources * 8
-    width = told_ref.shape[1] // 9
+    width = told_ref.shape[2] // 9
     turned = jnp.stack(
-        [told_ref[:, k * width : (k + 1) * width] for k in range(8)], axis=1
+        [told_ref[:, 0, k * width : (k + 1) * width] for k in range(8)], axis=1
     ).reshape(lanes, width).T
     codes = jnp.broadcast_to(
-        told_ref[:, 8 * width :].reshape(sources, 1, width), (sources, 8, width)
+        told_ref[:, :, 8 * width :], (sources, 8, width)
     ).reshape(lanes, width).T
     picks = width // 2
     columns = turned[0:picks].astype(i32) - 1
@@ -201,7 +201,7 @@
 
 
 def place(owner, told, panel, per_tile):
-    sources, width = told.shape
+    sources, _, width = told.shape
     rows = sources * 8
     block = 16
     return pl.pallas_call(
@@ -209,7 +209,7 @@
         grid_spec=pltpu.PrefetchScalarGridSpec(
             num_scalar_prefetch=1,
             grid=(sources // block,),
-            in_specs=[pl.BlockSpec((block, width), lambda s, o: (s, 0))],
+            in_specs=[pl.BlockSpec((block, 1, width), lambda s, o: (s, 0, 0))],
             out_specs=[
                 pl.BlockSpec((panel, block * 8), lambda s, o: (0, s)),
                 pl.BlockSpec((8, block * 8), lambda s, o: (0, s)),
@@ -228,53 +228,74 @@
 
 
 def score_kernel(
-    bounds, head_ref, rows_ref, dense_ref, facts_ref, part_ref, own_ref, told_ref, total_ref, held_ref, sems
+    bounds, head_ref, rows_ref, dense_ref, facts_ref, part_ref, own_ref, told_ref,
+    total_ref, head_held, rows_held, dense_held, part_held, sems, last_sem, out_sems
 ):
     groups, _, lanes = rows_ref.shape
+    panel, count = total_ref.shape
     copies = []
     for k, (low, high) in enumerate(bounds):
         copies.append(
-            pltpu.make_async_copy(
-                rows_ref.at[:, low:high, :], held_ref.at[:, low:high, :], sems.at[k]
+            (
+                pltpu.make_async_copy(
+                    head_ref.at[:, low:high], head_held.at[:, low:high], sems.at[0, k]
+                ),
+                pltpu.make_async_copy(
+                    rows_ref.at[:, low:high, :], rows_held.at[:, low:high, :], sems.at[1, k]
+                ),
             )
         )
-    for copy in copies:
-        copy.start()
+    last = pltpu.make_async_copy(dense_ref, dense_held, last_sem)
+    ahead = 3
+    for pair in copies[:ahead]:
+        pair[0].start()
+        pair[1].start()
     for k, (low, high) in enumerate(bounds):
-        copies[k].wait()
+        if k + ahead < len(bounds):
+            copies[k + ahead][0].start()
+            copies[k + ahead][1].start()
+        if k + ahead == len(bounds):
+            last.start()
+        copies[k][0].wait()
+        copies[k][1].wait()
         for t in range(groups):
             here = slice(t * lanes, (t + 1) * lanes)
-            product = plain(head_ref[:, low:high], held_ref[t, low:high, :])
+            product = plain(head_held[:, low:high], rows_held[t, low:high, :])
             total_ref[:, here] = product if k == 0 else total_ref[:, here] + product
-    count = total_ref.shape[1]
+    last.wait()
     chunk = 128
-    logs, largest, shares = [], [], []
-    for at in range(0, count, chunk):
+    logs, largest, shares, leave = [], [], [], []
+    for k, at in enumerate(range(0, count, chunk)):
         here = slice(at, at + chunk)
-        dense = dense_ref[:, here]
+        dense = dense_held[:, here]
         score = total_ref[:, here]
         named = dense > 0.0
         most = jnp.max(jnp.where(named, score, nothing), axis=0, keepdims=True)
         part = jnp.where(named, jnp.exp(score - most), 0.0)
-        part_ref[:, here] = part
+        part_held[:, here] = part
+        leave.append(
+            pltpu.make_async_copy(part_held.at[:, here], part_ref.at[:, here], out_sems.at[k])
+        )
+        leave[-1].start()
         whole = jnp.sum(part, axis=0, keepdims=True)
         log = jnp.where(whole > 0.0, most + jnp.log(jnp.maximum(whole, 1.0)), nothing)
-        shares.append(
-            facts_ref[2:3, here] - jnp.sum(dense * score, axis=0, keepdims=True)
-        )
+        shares.append(facts_ref[2:3, here] - jnp.sum(dense * score, axis=0, keepdims=True))
         logs.append(log)
         largest.append(most)
     logs = jnp.concatenate(logs, axis=1)
     largest = jnp.concatenate(largest, axis=1)
-    shares = jnp.concatenate(shares, axis=1)
     own_ref[...] = jnp.concatenate([largest, logs, jnp.zeros((6, count), f32)], axis=0)
     owners = told_ref.shape[0]
-    told_ref[:, 0:count] = jnp.broadcast_to(logs, (owners, count))
-    home = iota((owners, count), 1) // 8 == iota((owners, count), 0)
-    which = (iota((count, 128), 0) % 8 == iota((count, 128), 1)).astype(f32)
-    told_ref[:, count : count + 128] = plain(
-        jnp.where(home, jnp.broadcast_to(shares, (owners, count)), 0.0), which, HIGHEST
+    told_ref[:, 0, 0:count] = jnp.broadcast_to(logs, (owners, count))
+    group = chunk // 8
+    home = iota((group, chunk), 1) // 8 == iota((group, chunk), 0)
+    which = (iota((chunk, chunk), 0) % 8 == iota((chunk, chunk), 1)).astype(f32)
+    spread = [jnp.where(home, jnp.broadcast_to(share, (group, chunk)), 0.0) for share in shares]
+    told_ref[:, 0, count : count + chunk] = plain(
+        jnp.concatenate(spread, axis=0), which, HIGHEST
     )
+    for copy in leave:
+        copy.wait()
 
 
 def score(head, rows, dense, facts, owners):
@@ -286,19 +307,24 @@
     bounds = list(zip(cuts[:-1], cuts[1:]))
     return pl.pallas_call(
         functools.partial(score_kernel, bounds),
-        in_specs=[near, far, near, near],
-        out_specs=[near, near, near],
+        in_specs=[far, far, far, near],
+        out_specs=[far, near, near],
         out_shape=(
             jax.ShapeDtypeStruct((panel, count), f32),
             jax.ShapeDtypeStruct((8, count), f32),
-            jax.ShapeDtypeStruct((owners, count + 128), f32),
+            jax.ShapeDtypeStruct((owners, 1, count + 128), f32),
         ),
         scratch_shapes=[
             pltpu.VMEM((panel, count), f32),
+            pltpu.VMEM((panel, width), bf16),
             pltpu.VMEM((groups, width, lanes), bf16),
-            pltpu.SemaphoreType.DMA((len(bounds),)),
+            pltpu.VMEM((panel, count), f32),
+            pltpu.VMEM((panel, count), f32),
+            pltpu.SemaphoreType.DMA((2, len(bounds))),
+            pltpu.SemaphoreType.DMA,
+            pltpu.SemaphoreType.DMA((count // 128,)),
         ],
-        compiler_params=settings(24),
+        compiler_params=settings(56),
         name="score",
     )(head, rows, dense, facts)
 
@@ -324,7 +350,7 @@
         in_specs=[columns, columns],
         out_specs=[rows, rows],
         out_shape=[jax.ShapeDtypeStruct((count, panel), f32)] * 2,
-        compiler_params=settings(24),
+        compiler_params=settings(56),
         cost_estimate=pl.CostEstimate(
             flops=4 * panel * count, bytes_accessed=16 * panel * count, transcendentals=0
         ),
@@ -333,14 +359,33 @@
 
 
 def part_kernel(
-    per_tile, logs_ref, facts_ref, own_ref, part_ref, dense_ref, head_ref, out_ref, weight_ref, held_ref, sems
+    per_tile, logs_ref, facts_ref, own_ref, part_ref, dense_ref, head_ref, out_ref, weight_ref,
+    part_held, dense_held, head_held, out_held, sems, head_sems, out_sems
 ):
     count, panel = part_ref.shape
     owners = logs_ref.shape[0]
     chunk = 128
-    for at in range(0, count, chunk):
+    slots, _, block = out_held.shape
+    blocks = out_ref.shape[1] // block
+    tables, heads = [], []
+    for k in range(count // chunk):
+        here = slice(k * chunk, (k + 1) * chunk)
+        tables.append(
+            (
+                pltpu.make_async_copy(part_ref.at[here], part_held.at[here], sems.at[0, k]),
+                pltpu.make_async_copy(dense_ref.at[here], dense_held.at[here], sems.at[1, k]),
+            )
+        )
+        tables[-1][0].start()
+        tables[-1][1].start()
+    for k in range(blocks):
+        here = slice(k * block, (k + 1) * block)
+        heads.append(
+            pltpu.make_async_copy(head_ref.at[:, here], head_held.at[:, here], head_sems.at[k])
+        )
+    for k, at in enumerate(range(0, count, chunk)):
         here = slice(at, at + chunk)
-        logs = logs_ref[:, here]
+        logs = logs_ref[:, 0, here]
         partner = facts_ref[0:1, here].astype(i32) - 1
         slot = (iota((1, chunk), 1) // per_tile) % 2
         across = jnp.where(
@@ -355,32 +400,30 @@
         total = log_sum(own_ref[1:2, here], other)
         scale = loss_weight * facts_ref[1:2, here] * jnp.exp(own_ref[0:1, here] - total)
         scale = jnp.broadcast_to(scale, (chunk, chunk)).T
+        tables[k][0].wait()
+        tables[k][1].wait()
+        if k == 2:
+            for copy in heads[:2]:
+                copy.start()
         for col in range(0, panel, chunk):
             there = slice(col, col + chunk)
-            weight = part_ref[here, there] * scale - dense_ref[here, there]
+            weight = part_held[here, there] * scale - dense_held[here, there]
             weight_ref[here, there] = weight.astype(bf16)
-    slots, _, block = held_ref.shape
-
-    def leave(k):
-        place = pl.ds(pl.multiple_of(k * block, block), block)
-        return pltpu.make_async_copy(
-            held_ref.at[k % slots], out_ref.at[:, place], sems.at[k % slots]
+    leave = []
+    for k in range(blocks):
+        here = slice(k * block, (k + 1) * block)
+        if k >= slots:
+            leave[k - slots].wait()
+        if k + 2 < blocks:
+            heads[k + 2].start()
+        heads[k].wait()
+        out_held[k % slots] = plain(weight_ref[...], head_held[:, here]).astype(bf16)
+        leave.append(
+            pltpu.make_async_copy(out_held.at[k % slots], out_ref.at[:, here], out_sems.at[k % slots])
         )
-
-    def one(k, carry):
-        @pl.when(k >= slots)
-        def _():
-            leave(k - slots).wait()
-
-        place = pl.ds(pl.multiple_of(k * block, block), block)
-        held_ref[k % slots] = plain(weight_ref[...], head_ref[:, place]).astype(bf16)
-        leave(k).start()
-        return carry
-
-    blocks = out_ref.shape[1] // block
-    lax.fori_loop(0, blocks, one, 0)
-    for k in range(blocks - slots, blocks):
-        leave(k).wait()
+        leave[-1].start()
+    for copy in leave[blocks - slots :]:
+        copy.wait()
 
 
 def grad_parts(logs, facts, own, part, dense, head, per_tile):
@@ -389,17 +432,22 @@
     block = 512
     return pl.pallas_call(
         functools.partial(part_kernel, per_tile),
-        in_specs=[near] * 6,
+        in_specs=[near, near, near, far, far, far],
         out_specs=[far, near],
         out_shape=(
             jax.ShapeDtypeStruct((count, width), bf16),
             jax.ShapeDtypeStruct((count, panel), bf16),
         ),
         scratch_shapes=[
+            pltpu.VMEM((count, panel), f32),
+            pltpu.VMEM((count, panel), f32),
+            pltpu.VMEM((panel, width), bf16),
             pltpu.VMEM((2, count, block), bf16),
+            pltpu.SemaphoreType.DMA((2, count // 128)),
+            pltpu.SemaphoreType.DMA((width // block,)),
             pltpu.SemaphoreType.DMA((2,)),
         ],
-        compiler_params=settings(16),
+        compiler_params=settings(56),
         name="grad_parts",
     )(logs, facts, own, part, dense, head)
 
@@ -448,8 +496,8 @@
     count = table_ref.shape[1]
     mine = iota((count, 128), 0) == me_ref[0] * 8 + iota((count, 128), 1)
     mine = jnp.where(mine & (iota((count, 128), 1) < 8), 1.0, 0.0)
-    logs = plain(logs_ref[:, 0:count], mine, HIGHEST).T
-    shares = logs_ref[:, count : count + 128].T
+    logs = plain(logs_ref[:, 0, 0:count], mine, HIGHEST).T
+    shares = logs_ref[:, 0, count : count + 128].T
     found = []
     total = jnp.zeros((1, tokens), f32)
     for group in range(2):
@@ -513,14 +561,6 @@
 
 
 def exchange(values):
-    owners, width = values.shape
-    moved = lax.all_to_all(
-        values.reshape(owners, 1, width), ("tok", "voc"), split_axis=0, concat_axis=0, tiled=True
-    )
-    return moved.reshape(owners, width)
-
-
-def exchange_tiles(values):
     return lax.all_to_all(values, ("tok", "voc"), split_axis=0, concat_axis=0, tiled=True)
 
 
@@ -538,13 +578,13 @@
     told, home_rows = announce(tile_owners.T, cand_pos.T, teacher, panel, per_tile, owners)
     told = exchange(told)
     sent = route(tok.astype(i32).reshape(1), told, hidden.T, per_tile, blocks)
-    rows = exchange_tiles(sent).reshape(tok_size, width, blocks * 8)
+    rows = exchange(sent).reshape(tok_size, width, blocks * 8)
     dense, facts = place(me, told, panel, per_tile)
     part, own, logs = score(head_weight, rows, dense, facts, owners)
     logs = exchange(logs)
     part_rows, dense_rows = turn(part, dense)
     parts, weight = grad_parts(logs, facts, own, part_rows, dense_rows, head_weight, per_tile)
-    home_parts = exchange_tiles(parts.reshape(owners, 8, width)).reshape(count, width)
+    home_parts = exchange(parts.reshape(owners, 8, width)).reshape(count, width)
     grad_head = grad_of_head(weight, rows)
     loss, table = losses(me, logs, home_rows, teacher, count)
     grad_hidden = combine(table, home_parts)

time: 394 us -> 383 us (0.972)
  local copies, waits for them, and re-layouts: 28.9 us -> 4.71 us
  Pallas kernels: 88.6 us -> 101 us
    unnamed x28 -> x20, local copies, waits for them, and re-layouts: 25 us -> 4.71 us
    pallas_call x2, Pallas kernels: 24.3 us -> 32.8 us  [the longest x1 16.9 us: grad_parts(): pl.pallas_call(functools.partial(part_kernel, per_tile), in_specs=[near,...]
  transfers between devices with their start and end apart: 4 -> 4, of which waited for: 4 -> 4; matrix products, arithmetic and copies ran while one was open for 0% -> 0% of each run, Pallas kernels for 10% -> 12%
where the time goes in v3:
time: 383 us; the launch traced here: 382 us
  waiting for transfers between devices  245 us (64%)
  Pallas kernels  101 us (26%)
  starting transfers between devices  30.8 us (8%)
  local copies, waits for them, and re-layouts  4.71 us (1%)
    all_to_all x4, waiting for transfers between devices, exchange(): lax.all_to_all(values, ('tok', 'voc'), split_axis=0, concat_axis=0, tiled...  245 us
    all_to_all x4, starting transfers between devices, exchange(): lax.all_to_all(values, ('tok', 'voc'), split_axis=0, concat_axis=0, tiled...  30.8 us
    pallas_call x1, Pallas kernels, place(): pl.pallas_call(functools.partial(place_kernel, per_tile), grid_spec=pltpu...  21 us
    pallas_call x1, Pallas kernels, grad_parts(): pl.pallas_call(functools.partial(part_kernel, per_tile), in_specs=[near,...  16.9 us
    pallas_call x1, Pallas kernels, score(): pl.pallas_call(functools.partial(score_kernel, bounds), in_specs=[far, fa...  15.9 us
    pallas_call x1, Pallas kernels, grad_of_head(): pl.pallas_call(head_kernel, grid=(width // block,), in_specs=[pl.BlockSpe...  15.1 us
    pallas_call x1, Pallas kernels, route(): pl.pallas_call(functools.partial(route_kernel, per_tile), grid_spec=pltpu...  13 us
  transfers between devices with their start and end apart: 4, of which 4 were waited for; matrix products, arithmetic and copies ran while one was open for 0% of the time, Pallas kernels for 12%

profile of v3, /device:TPU:97, one launch (start us, length us, event | category | flops | bytes accessed | tf_op | source)
XLA Modules:
  0.0 381.8 jit_solution(17506073351117728149)
XLA Ops:
  0.6 4.1 %announce.1 = (f32[128,1,1152]{2,1,0:T(1,128)}, s32[8,512]{1,0:T(8,128)}) custom-call(s32[2,64]{1,0:T(2,128)} %bitcast.15, s32[64,256]{1,0:T(8,128)} %bitcast.14, f32[64,256]{1,0:T(8,128)} %bitcast.10), custom_call_target="tpu_custom_call" | custom-call | tf_op jit(solution)/shard_map/announce/pallas_call | solution.py:81
  4.7 10.2 %all-to-all-start = ((f32[128,1,1152]{2,1,0:T(1,128)}), f32[128,1,1152]{2,1,0:T(1,128)S(1)}, u32[]{:S(2)}, u32[]{:S(2)}) async-start(f32[128,1,1152]{2,1,0:T(1,128)} %get-tuple-element.16), calls=%async_computation | async-start | bytes 1179648 | tf_op jit(solution)/shard_map/all_to_all | solution.py:564
  14.9 11.6 %all-to-all-done.codes_ref.told_ref = f32[128,1,1152]{2,1,0:T(1,128)S(1)} async-done(((f32[128,1,1152]{2,1,0:T(1,128)}), f32[128,1,1152]{2,1,0:T(1,128)S(1)}, u32[]{:S(2)}, u32[]{:S(2)}) %all-to-all-start) | async-done | bytes 589856 | tf_op jit(solution)/shard_map/all_to_all | solution.py:564
  26.5 0.8 copy-done.1
  27.4 13.0 %route.1 = bf16[128,160,256]{2,1,0:T(8,128)(2,1)} custom-call(s32[1]{0:T(128)} %bitcast.1.tok_ref, f32[128,1,1152]{2,1,0:T(1,128)} %copy-done.1, bf16[160,8192]{1,0:T(8,128)(2,1)} %bitcast.13), custom_call_target="tpu_custom_call" | custom-call | tf_op jit(solution)/shard_map/route/pallas_call | solution.py:144
  40.3 7.7 %all-to-all-start.1 = ((bf16[128,160,256]{2,1,0:T(8,128)(2,1)}), bf16[128,160,256]{2,1,0:T(8,128)(2,1)}, u32[]{:S(2)}, u32[]{:S(2)}) async-start(bf16[128,160,256]{2,1,0:T(8,128)(2,1)} %route.1), calls=%async_computation.1 | async-start | bytes 20971520 | tf_op jit(solution)/shard_map/all_to_all | solution.py:564
  48.0 0.0 copy-done.2
  48.0 21.0 %place.1 = (f32[768,1024]{1,0:T(8,128)S(1)}, f32[8,1024]{1,0:T(8,128)S(1)}) custom-call(s32[1]{0:T(128)} %bitcast.owner_ref.me_ref, f32[128,1,1152]{2,1,0:T(1,128)S(1)} %copy-done.2), custom_call_target="tpu_custom_call" | custom-call | flops 100663296 | bytes 6291456 | tf_op jit(solution)/shard_map/place/pallas_call | solution.py:207
  69.1 0.0 copy-start
  69.1 1.7 copy-done
  70.7 0.6 copy-done.6
  71.3 113.1 %all-to-all-done.1 = bf16[128,160,256]{2,1,0:T(8,128)(2,1)} async-done(((bf16[128,160,256]{2,1,0:T(8,128)(2,1)}), bf16[128,160,256]{2,1,0:T(8,128)(2,1)}, u32[]{:S(2)}, u32[]{:S(2)}) %all-to-all-start.1) | async-done | bytes 10485792 | tf_op jit(solution)/shard_map/all_to_all | solution.py:564
  184.4 15.9 %score.1 = (f32[768,1024]{1,0:T(8,128)}, f32[8,1024]{1,0:T(8,128)}, f32[128,1,1152]{2,1,0:T(1,128)}) custom-call(bf16[768,5120]{1,0:T(8,128)(2,1)} %head_ref.3, bf16[4,5120,256]{2,1,0:T(8,128)(2,1)} %bitcast.6.rows_ref, f32[768,1024]{1,0:T(8,128)} %copy-done, f32[8,1024]{1,0:T(8,128)} %copy-done.6), custom_call_target="tpu_custom_call" | custom-call | tf_op jit(solution)/shard_map/score/pallas_call | solution.py:308
  200.3 5.3 %all-to-all-start.2 = ((f32[128,1,1152]{2,1,0:T(1,128)}), f32[128,1,1152]{2,1,0:T(1,128)S(1)}, u32[]{:S(2)}, u32[]{:S(2)}) async-start(f32[128,1,1152]{2,1,0:T(1,128)} %get-tuple-element.19), calls=%async_computation.2 | async-start | bytes 1179648 | tf_op jit(solution)/shard_map/all_to_all | solution.py:564
  205.5 6.2 %turn.1 = (f32[1024,768]{1,0:T(8,128)}, f32[1024,768]{1,0:T(8,128)}) custom-call(f32[768,1024]{1,0:T(8,128)} %get-tuple-element.24.part_ref, f32[768,1024]{1,0:T(8,128)} %copy-done), custom_call_target="tpu_custom_call" | custom-call | flops 3145728 | bytes 12582912 | tf_op jit(solution)/shard_map/turn/pallas_call | solution.py:347
  211.7 5.5 %all-to-all-done.2.logs_ref = f32[128,1,1152]{2,1,0:T(1,128)S(1)} async-done(((f32[128,1,1152]{2,1,0:T(1,128)}), f32[128,1,1152]{2,1,0:T(1,128)S(1)}, u32[]{:S(2)}, u32[]{:S(2)}) %all-to-all-start.2) | async-done | bytes 589856 | tf_op jit(solution)/shard_map/all_to_all | solution.py:564
  217.2 0.8 copy-done.3
  218.0 16.9 %grad_parts.1 = (bf16[1024,5120]{1,0:T(8,128)(2,1)}, bf16[1024,768]{1,0:T(8,128)(2,1)}) custom-call(f32[128,1,1152]{2,1,0:T(1,128)} %copy-done.3, f32[8,1024]{1,0:T(8,128)} %copy-done.6, f32[8,1024]{1,0:T(8,128)} %get-tuple-element.23.own_ref, f32[1024,768]{1,0:T(8,128)} %get-tuple-element.25.part_ref, f32[1024,768]{1,0:T(8,128)} %get-tuple-element.26.dense_ref, ...), custom_call_target="tpu_custom_call" | custom-call | tf_op jit(solution)/shard_map/grad_parts/pallas_call | solution.py:433
  234.9 0.0 copy-start.4
  234.9 0.0 copy-start.7
  234.9 0.0 copy-start.9
  234.9 0.0 copy-start.8
  235.0 7.7 %all-to-all-start.3 = ((bf16[128,8,5120]{2,1,0:T(8,128)(2,1)}), bf16[128,8,5120]{2,1,0:T(8,128)(2,1)}, u32[]{:S(2)}, u32[]{:S(2)}) async-start(bf16[128,8,5120]{2,1,0:T(8,128)(2,1)} %bitcast.12), calls=%async_computation.3 | async-start | bytes 20971520 | tf_op jit(solution)/shard_map/all_to_all | solution.py:564
  242.6 0.0 copy-done.4
  242.6 0.0 copy-done.7
  242.7 0.0 copy-done.9
  242.7 1.8 losses.1
  244.5 0.8 copy-done.5
  245.3 0.0 copy-done.8
  245.3 15.1 %grad_of_head.1 = bf16[768,5120]{1,0:T(8,128)(2,1)} custom-call(bf16[1024,768]{1,0:T(8,128)(2,1)S(1)} %copy-done.8, bf16[4,5120,256]{2,1,0:T(8,128)(2,1)} %bitcast.6.rows_ref), custom_call_target="tpu_custom_call" | custom-call | flops 8053063680 | bytes 18350080 | tf_op jit(solution)/shard_map/grad_of_head/pallas_call | solution.py:473
  260.4 114.6 %all-to-all-done.3 = bf16[128,8,5120]{2,1,0:T(8,128)(2,1)} async-done(((bf16[128,8,5120]{2,1,0:T(8,128)(2,1)}), bf16[128,8,5120]{2,1,0:T(8,128)(2,1)}, u32[]{:S(2)}, u32[]{:S(2)}) %all-to-all-start.3) | async-done | bytes 10485792 | tf_op jit(solution)/shard_map/all_to_all | solution.py:564
  375.0 6.8 %combine.1 = bf16[256,5120]{1,0:T(8,128)(2,1)} custom-call(bf16[256,1024]{1,0:T(8,128)(2,1)} %copy-done.5, bf16[1024,5120]{1,0:T(8,128)(2,1)} %bitcast.9.parts_ref), custom_call_target="tpu_custom_call" | custom-call | tf_op jit(solution)/shard_map/combine/pallas_call | solution.py:549
  (5 shorter events, 0.0 us)
Async XLA Ops:
  4.7 21.8 %all-to-all-start = ((f32[128,1,1152]{2,1,0:T(1,128)}), f32[128,1,1152]{2,1,0:T(1,128)S(1)}, u32[]{:S(2)}, u32[]{:S(2)}) async-start(f32[128,1,1152]{2,1,0:T(1,128)} %get-tuple-element.16), calls=%async_computation | async-start | bytes 1179648 | tf_op jit(solution)/shard_map/all_to_all | solution.py:564
  26.5 0.8 copy-start.1
  40.3 7.7 %copy-start.2 = (f32[128,1,1152]{2,1,0:T(1,128)S(1)}, f32[128,1,1152]{2,1,0:T(1,128)}, u32[]{:S(2)}) copy-start(f32[128,1,1152]{2,1,0:T(1,128)} %copy-done.1) | copy-start | bytes 1769476
  40.3 144.1 %all-to-all-start.1 = ((bf16[128,160,256]{2,1,0:T(8,128)(2,1)}), bf16[128,160,256]{2,1,0:T(8,128)(2,1)}, u32[]{:S(2)}, u32[]{:S(2)}) async-start(bf16[128,160,256]{2,1,0:T(8,128)(2,1)} %route.1), calls=%async_computation.1 | async-start | bytes 20971520 | tf_op jit(solution)/shard_map/all_to_all | solution.py:564
  69.1 1.7 copy-start
  70.7 0.6 copy-start.6
  200.3 16.9 %all-to-all-start.2 = ((f32[128,1,1152]{2,1,0:T(1,128)}), f32[128,1,1152]{2,1,0:T(1,128)S(1)}, u32[]{:S(2)}, u32[]{:S(2)}) async-start(f32[128,1,1152]{2,1,0:T(1,128)} %get-tuple-element.19), calls=%async_computation.2 | async-start | bytes 1179648 | tf_op jit(solution)/shard_map/all_to_all | solution.py:564
  217.2 0.8 copy-start.3
  234.9 7.7 %copy-start.4 = (f32[128,1,1152]{2,1,0:T(1,128)S(1)}, f32[128,1,1152]{2,1,0:T(1,128)}, u32[]{:S(2)}) copy-start(f32[128,1,1152]{2,1,0:T(1,128)} %copy-done.3) | copy-start | bytes 1769476
  234.9 7.7 %copy-start.7 = (f32[256,64]{0,1:T(8,128)S(1)}, f32[256,64]{0,1:T(8,128)}, u32[]{:S(2)}) copy-start(f32[256,64]{0,1:T(8,128)} %param.9) | copy-start | bytes 196612
  234.9 7.7 %copy-start.9 = (s32[8,512]{1,0:T(8,128)S(1)}, s32[8,512]{1,0:T(8,128)}, u32[]{:S(2)}) copy-start(s32[8,512]{1,0:T(8,128)} %get-tuple-element.20.rows_ref) | copy-start | bytes 49156
  234.9 10.4 %copy-start.8 = (bf16[1024,768]{1,0:T(8,128)(2,1)S(1)}, bf16[1024,768]{1,0:T(8,128)(2,1)}, u32[]{:S(2)}) copy-start(bf16[1024,768]{1,0:T(8,128)(2,1)} %get-tuple-element.28.weight_ref) | copy-start | bytes 4718596
  235.0 140.1 %all-to-all-start.3 = ((bf16[128,8,5120]{2,1,0:T(8,128)(2,1)}), bf16[128,8,5120]{2,1,0:T(8,128)(2,1)}, u32[]{:S(2)}, u32[]{:S(2)}) async-start(bf16[128,8,5120]{2,1,0:T(8,128)(2,1)} %bitcast.12), calls=%async_computation.3 | async-start | bytes 20971520 | tf_op jit(solution)/shard_map/all_to_all | solution.py:564
  244.5 0.8 copy-start.5

commit v4 on v3

--- a/solution.py
+++ b/solution.py
@@ -58,21 +58,39 @@
     rows = rows_of(jnp.broadcast_to(code, (8, entries)), per_tile)
     rows_ref[...] = rows
     cand = cand_ref[...]
-    teacher = teacher_ref[...]
-    columns = (
-        jnp.where(cand < panel, cand + 1, 0).astype(f32),
-        jnp.where(cand >= panel, cand - panel + 1, 0).astype(f32),
-    )
+    first = teacher_ref[...].astype(bf16)
+    rest = teacher_ref[...] - first.astype(f32)
+    second = rest.astype(bf16)
+    third = (rest - second.astype(f32)).astype(bf16)
+    sides = []
+    for column in (
+        jnp.where(cand < panel, cand + 1, 0),
+        jnp.where(cand >= panel, cand - panel + 1, 0),
+    ):
+        high, low = column // 32, column % 32
+        sides.append(
+            jnp.concatenate(
+                [
+                    high.astype(f32).astype(bf16),
+                    first,
+                    low.astype(f32).astype(bf16),
+                    second,
+                    jnp.zeros_like(first),
+                    third,
+                ],
+                axis=0,
+            )
+        )
+    sides = jnp.concatenate(sides, axis=1)
     width = 2 * cand.shape[0]
+    times = jnp.where(iota((slots, width), 1) < cand.shape[0], 32.0, 1.0)
     for which in range(8):
-        row = iota((slots, tokens), 0) * 8 + which
-        told = jnp.zeros((slots, width), f32)
-        for group in range(2):
-            hot = jnp.where(row == rows[0:1, group * tokens : (group + 1) * tokens], 1.0, 0.0)
-            told = told + by_rows(
-                hot, jnp.concatenate([columns[group], teacher], axis=0), HIGHEST
-            )
-        out_ref[:, 0, which * width : (which + 1) * width] = told
+        row = iota((slots, 2 * tokens), 0) * 8 + which
+        hot = jnp.where(row == rows[0:1, :], 1.0, 0.0).astype(bf16)
+        told = by_rows(hot, sides)
+        out_ref[:, 0, which * width : (which + 1) * width] = (
+            told[:, 0:width] * times + told[:, width : 2 * width] + told[:, 2 * width :]
+        )
     out_ref[:, 0, 8 * width : 8 * width + entries] = jnp.broadcast_to(code, (slots, entries))
 
 
@@ -219,7 +237,7 @@
             jax.ShapeDtypeStruct((panel, rows), f32),
             jax.ShapeDtypeStruct((8, rows), f32),
         ),
-        compiler_params=settings(),
+        compiler_params=settings(58),
         cost_estimate=pl.CostEstimate(
             flops=2 * 64 * panel * rows, bytes_accessed=8 * panel * rows, transcendentals=64 * rows
         ),
@@ -246,7 +264,7 @@
             )
         )
     last = pltpu.make_async_copy(dense_ref, dense_held, last_sem)
-    ahead = 3
+    ahead = 4
     for pair in copies[:ahead]:
         pair[0].start()
         pair[1].start()
@@ -303,7 +321,7 @@
     groups, _, lanes = rows.shape
     count = groups * lanes
     block = 1024
-    cuts = [0, block // 4] + list(range(block, width, block)) + [width]
+    cuts = [0, 512, 1280, 2560, 3840, 5120]
     bounds = list(zip(cuts[:-1], cuts[1:]))
     return pl.pallas_call(
         functools.partial(score_kernel, bounds),
@@ -360,11 +378,19 @@
 
 def part_kernel(
     per_tile, logs_ref, facts_ref, own_ref, part_ref, dense_ref, head_ref, out_ref, weight_ref,
-    part_held, dense_held, head_held, out_held, sems, head_sems, out_sems
+    logs_held, facts_held, own_held, part_held, dense_held, head_held, out_held,
+    small_sems, sems, head_sems, out_sems
 ):
     count, panel = part_ref.shape
     owners = logs_ref.shape[0]
     chunk = 128
+    small = [
+        pltpu.make_async_copy(facts_ref, facts_held, small_sems.at[0]),
+        pltpu.make_async_copy(own_ref, own_held, small_sems.at[1]),
+        pltpu.make_async_copy(logs_ref, logs_held, small_sems.at[2]),
+    ]
+    for copy in small:
+        copy.start()
     slots, _, block = out_held.shape
     blocks = out_ref.shape[1] // block
     tables, heads = [], []
@@ -383,10 +409,12 @@
         heads.append(
             pltpu.make_async_copy(head_ref.at[:, here], head_held.at[:, here], head_sems.at[k])
         )
+    for copy in small:
+        copy.wait()
     for k, at in enumerate(range(0, count, chunk)):
         here = slice(at, at + chunk)
-        logs = logs_ref[:, 0, here]
-        partner = facts_ref[0:1, here].astype(i32) - 1
+        logs = logs_held[:, 0, here]
+        partner = facts_held[0:1, here].astype(i32) - 1
         slot = (iota((1, chunk), 1) // per_tile) % 2
         across = jnp.where(
             slot == 0, pltpu.roll(logs, chunk - per_tile, 1), pltpu.roll(logs, per_tile, 1)
@@ -397,8 +425,8 @@
             0.0,
         )
         other = jnp.sum(picked, axis=0, keepdims=True)
-        total = log_sum(own_ref[1:2, here], other)
-        scale = loss_weight * facts_ref[1:2, here] * jnp.exp(own_ref[0:1, here] - total)
+        total = log_sum(own_held[1:2, here], other)
+        scale = loss_weight * facts_held[1:2, here] * jnp.exp(own_held[0:1, here] - total)
         scale = jnp.broadcast_to(scale, (chunk, chunk)).T
         tables[k][0].wait()
         tables[k][1].wait()
@@ -432,17 +460,21 @@
     block = 512
     return pl.pallas_call(
         functools.partial(part_kernel, per_tile),
-        in_specs=[near, near, near, far, far, far],
+        in_specs=[far] * 6,
         out_specs=[far, near],
         out_shape=(
             jax.ShapeDtypeStruct((count, width), bf16),
             jax.ShapeDtypeStruct((count, panel), bf16),
         ),
         scratch_shapes=[
+            pltpu.VMEM(logs.shape, f32),
+            pltpu.VMEM(facts.shape, f32),
+            pltpu.VMEM(own.shape, f32),
             pltpu.VMEM((count, panel), f32),
             pltpu.VMEM((count, panel), f32),
             pltpu.VMEM((panel, width), bf16),
             pltpu.VMEM((2, count, block), bf16),
+            pltpu.SemaphoreType.DMA((3,)),
             pltpu.SemaphoreType.DMA((2, count // 128)),
             pltpu.SemaphoreType.DMA((width // block,)),
             pltpu.SemaphoreType.DMA((2,)),
@@ -530,7 +562,7 @@
             jax.ShapeDtypeStruct((1, tokens), f32),
             jax.ShapeDtypeStruct((tokens, count), bf16),
         ),
-        compiler_params=settings(),
+        compiler_params=settings(58),
         cost_estimate=pl.CostEstimate(
             flops=12 * 2 * count * tokens * 128, bytes_accessed=4 * count * tokens, transcendentals=0
         ),

time: 383 us -> 382 us (level)
  no operation moved by 1% of the time
where the time goes in v4:
time: 382 us; the launch traced here: 381 us
  waiting for transfers between devices  243 us (64%)
  Pallas kernels  103 us (27%)
  starting transfers between devices  32.7 us (9%)
    all_to_all x4, waiting for transfers between devices, exchange(): lax.all_to_all(values, ('tok', 'voc'), split_axis=0, concat_axis=0, tiled...  243 us
    all_to_all x4, starting transfers between devices, exchange(): lax.all_to_all(values, ('tok', 'voc'), split_axis=0, concat_axis=0, tiled...  32.7 us
    pallas_call x1, Pallas kernels, place(): pl.pallas_call(functools.partial(place_kernel, per_tile), grid_spec=pltpu...  22.4 us
    pallas_call x1, Pallas kernels, grad_parts(): pl.pallas_call(functools.partial(part_kernel, per_tile), in_specs=[far] *...  17.8 us
    pallas_call x1, Pallas kernels, score(): pl.pallas_call(functools.partial(score_kernel, bounds), in_specs=[far, fa...  15.6 us
    pallas_call x1, Pallas kernels, grad_of_head(): pl.pallas_call(head_kernel, grid=(width // block,), in_specs=[pl.BlockSpe...  15.1 us
    pallas_call x1, Pallas kernels, route(): pl.pallas_call(functools.partial(route_kernel, per_tile), grid_spec=pltpu...  13 us
  transfers between devices with their start and end apart: 4, of which 4 were waited for; matrix products, arithmetic and copies ran while one was open for 0% of the time, Pallas kernels for 12%

profile of v4, /device:TPU:97, one launch (start us, length us, event | category | flops | bytes accessed | tf_op | source)
XLA Modules:
  0.0 381.1 jit_solution(15098198522303812647)
XLA Ops:
  0.6 3.0 announce.1
  3.7 10.2 %all-to-all-start = ((f32[128,1,1152]{2,1,0:T(1,128)}), f32[128,1,1152]{2,1,0:T(1,128)S(1)}, u32[]{:S(2)}, u32[]{:S(2)}) async-start(f32[128,1,1152]{2,1,0:T(1,128)} %get-tuple-element.16), calls=%async_computation | async-start | bytes 1179648 | tf_op jit(solution)/shard_map/all_to_all | solution.py:596
  13.9 11.6 %all-to-all-done.codes_ref.told_ref = f32[128,1,1152]{2,1,0:T(1,128)S(1)} async-done(((f32[128,1,1152]{2,1,0:T(1,128)}), f32[128,1,1152]{2,1,0:T(1,128)S(1)}, u32[]{:S(2)}, u32[]{:S(2)}) %all-to-all-start) | async-done | bytes 589856 | tf_op jit(solution)/shard_map/all_to_all | solution.py:596
  25.5 0.0 copy-start.1
  25.5 0.8 copy-done.1
  26.3 13.0 %route.1 = bf16[128,160,256]{2,1,0:T(8,128)(2,1)} custom-call(s32[1]{0:T(128)} %bitcast.1.tok_ref, f32[128,1,1152]{2,1,0:T(1,128)} %copy-done.1, bf16[160,8192]{1,0:T(8,128)(2,1)} %bitcast.11), custom_call_target="tpu_custom_call" | custom-call | tf_op jit(solution)/shard_map/route/pallas_call | solution.py:162
  39.3 7.6 %all-to-all-start.1 = ((bf16[128,160,256]{2,1,0:T(8,128)(2,1)}), bf16[128,160,256]{2,1,0:T(8,128)(2,1)}, u32[]{:S(2)}, u32[]{:S(2)}) async-start(bf16[128,160,256]{2,1,0:T(8,128)(2,1)} %route.1), calls=%async_computation.1 | async-start | bytes 20971520 | tf_op jit(solution)/shard_map/all_to_all | solution.py:596
  46.9 22.4 %place.1 = (f32[768,1024]{1,0:T(8,128)}, f32[8,1024]{1,0:T(8,128)}) custom-call(s32[1]{0:T(128)} %bitcast.owner_ref.me_ref, f32[128,1,1152]{2,1,0:T(1,128)} %copy-done.1), custom_call_target="tpu_custom_call" | custom-call | flops 100663296 | bytes 6291456 | tf_op jit(solution)/shard_map/place/pallas_call | solution.py:225
  69.3 111.2 %all-to-all-done.1 = bf16[128,160,256]{2,1,0:T(8,128)(2,1)} async-done(((bf16[128,160,256]{2,1,0:T(8,128)(2,1)}), bf16[128,160,256]{2,1,0:T(8,128)(2,1)}, u32[]{:S(2)}, u32[]{:S(2)}) %all-to-all-start.1) | async-done | bytes 10485792 | tf_op jit(solution)/shard_map/all_to_all | solution.py:596
  180.5 15.6 %score.1 = (f32[768,1024]{1,0:T(8,128)}, f32[8,1024]{1,0:T(8,128)}, f32[128,1,1152]{2,1,0:T(1,128)}) custom-call(bf16[768,5120]{1,0:T(8,128)(2,1)} %head_ref.3, bf16[4,5120,256]{2,1,0:T(8,128)(2,1)} %bitcast.6.rows_ref, f32[768,1024]{1,0:T(8,128)} %get-tuple-element.17.dense_ref, f32[8,1024]{1,0:T(8,128)} %get-tuple-element.18.facts_ref), custom_call_target="tpu_custom_call" | custom-call | tf_op jit(solution)/shard_map/score/pallas_call | solution.py:326
  196.1 7.3 %all-to-all-start.2 = ((f32[128,1,1152]{2,1,0:T(1,128)}), f32[128,1,1152]{2,1,0:T(1,128)S(1)}, u32[]{:S(2)}, u32[]{:S(2)}) async-start(f32[128,1,1152]{2,1,0:T(1,128)} %get-tuple-element.19), calls=%async_computation.2 | async-start | bytes 1179648 | tf_op jit(solution)/shard_map/all_to_all | solution.py:596
  203.4 6.2 %turn.1 = (f32[1024,768]{1,0:T(8,128)}, f32[1024,768]{1,0:T(8,128)}) custom-call(f32[768,1024]{1,0:T(8,128)} %get-tuple-element.24.part_ref, f32[768,1024]{1,0:T(8,128)} %get-tuple-element.17.dense_ref), custom_call_target="tpu_custom_call" | custom-call | flops 3145728 | bytes 12582912 | tf_op jit(solution)/shard_map/turn/pallas_call | solution.py:365
  209.6 5.5 %all-to-all-done.2.logs_ref = f32[128,1,1152]{2,1,0:T(1,128)S(1)} async-done(((f32[128,1,1152]{2,1,0:T(1,128)}), f32[128,1,1152]{2,1,0:T(1,128)S(1)}, u32[]{:S(2)}, u32[]{:S(2)}) %all-to-all-start.2) | async-done | bytes 589856 | tf_op jit(solution)/shard_map/all_to_all | solution.py:596
  215.0 0.0 copy-start.2
  215.0 0.8 copy-done.2
  215.9 17.8 %grad_parts.1 = (bf16[1024,5120]{1,0:T(8,128)(2,1)}, bf16[1024,768]{1,0:T(8,128)(2,1)}) custom-call(f32[128,1,1152]{2,1,0:T(1,128)} %copy-done.2, f32[8,1024]{1,0:T(8,128)} %get-tuple-element.18.facts_ref, f32[8,1024]{1,0:T(8,128)} %get-tuple-element.23.own_ref, f32[1024,768]{1,0:T(8,128)} %get-tuple-element.25.part_ref, ...), custom_call_target="tpu_custom_call" | custom-call | tf_op jit(solution)/shard_map/grad_parts/pallas_call | solution.py:461
  233.7 0.0 copy-start
  233.7 7.7 %all-to-all-start.3 = ((bf16[128,8,5120]{2,1,0:T(8,128)(2,1)}), bf16[128,8,5120]{2,1,0:T(8,128)(2,1)}, u32[]{:S(2)}, u32[]{:S(2)}) async-start(bf16[128,8,5120]{2,1,0:T(8,128)(2,1)} %bitcast.10), calls=%async_computation.3 | async-start | bytes 20971520 | tf_op jit(solution)/shard_map/all_to_all | solution.py:596
  241.3 3.2 losses.1
  244.5 0.0 copy-done
  244.5 15.1 %grad_of_head.1 = bf16[768,5120]{1,0:T(8,128)(2,1)} custom-call(bf16[1024,768]{1,0:T(8,128)(2,1)S(1)} %copy-done, bf16[4,5120,256]{2,1,0:T(8,128)(2,1)} %bitcast.6.rows_ref), custom_call_target="tpu_custom_call" | custom-call | flops 8053063680 | bytes 18350080 | tf_op jit(solution)/shard_map/grad_of_head/pallas_call | solution.py:505
  259.6 114.7 %all-to-all-done.3 = bf16[128,8,5120]{2,1,0:T(8,128)(2,1)} async-done(((bf16[128,8,5120]{2,1,0:T(8,128)(2,1)}), bf16[128,8,5120]{2,1,0:T(8,128)(2,1)}, u32[]{:S(2)}, u32[]{:S(2)}) %all-to-all-start.3) | async-done | bytes 10485792 | tf_op jit(solution)/shard_map/all_to_all | solution.py:596
  374.3 6.8 %combine.1 = bf16[256,5120]{1,0:T(8,128)(2,1)} custom-call(bf16[256,1024]{1,0:T(8,128)(2,1)} %get-tuple-element.22.table_ref, bf16[1024,5120]{1,0:T(8,128)(2,1)} %bitcast.9.parts_ref), custom_call_target="tpu_custom_call" | custom-call | tf_op jit(solution)/shard_map/combine/pallas_call | solution.py:581
Async XLA Ops:
  3.7 21.8 %all-to-all-start = ((f32[128,1,1152]{2,1,0:T(1,128)}), f32[128,1,1152]{2,1,0:T(1,128)S(1)}, u32[]{:S(2)}, u32[]{:S(2)}) async-start(f32[128,1,1152]{2,1,0:T(1,128)} %get-tuple-element.16), calls=%async_computation | async-start | bytes 1179648 | tf_op jit(solution)/shard_map/all_to_all | solution.py:596
  25.5 0.8 copy-start.1
  39.3 141.2 %all-to-all-start.1 = ((bf16[128,160,256]{2,1,0:T(8,128)(2,1)}), bf16[128,160,256]{2,1,0:T(8,128)(2,1)}, u32[]{:S(2)}, u32[]{:S(2)}) async-start(bf16[128,160,256]{2,1,0:T(8,128)(2,1)} %route.1), calls=%async_computation.1 | async-start | bytes 20971520 | tf_op jit(solution)/shard_map/all_to_all | solution.py:596
  196.1 18.9 %all-to-all-start.2 = ((f32[128,1,1152]{2,1,0:T(1,128)}), f32[128,1,1152]{2,1,0:T(1,128)S(1)}, u32[]{:S(2)}, u32[]{:S(2)}) async-start(f32[128,1,1152]{2,1,0:T(1,128)} %get-tuple-element.19), calls=%async_computation.2 | async-start | bytes 1179648 | tf_op jit(solution)/shard_map/all_to_all | solution.py:596
  215.0 0.8 copy-start.2
  233.7 10.9 %copy-start = (bf16[1024,768]{1,0:T(8,128)(2,1)S(1)}, bf16[1024,768]{1,0:T(8,128)(2,1)}, u32[]{:S(2)}) copy-start(bf16[1024,768]{1,0:T(8,128)(2,1)} %get-tuple-element.28.weight_ref) | copy-start | bytes 4718596
  233.7 140.6 %all-to-all-start.3 = ((bf16[128,8,5120]{2,1,0:T(8,128)(2,1)}), bf16[128,8,5120]{2,1,0:T(8,128)(2,1)}, u32[]{:S(2)}, u32[]{:S(2)}) async-start(bf16[128,8,5120]{2,1,0:T(8,128)(2,1)} %bitcast.10), calls=%async_computation.3 | async-start | bytes 20971520 | tf_op jit(solution)/shard_map/all_to_all | solution.py:596

commit v5 on v4

--- a/solution.py
+++ b/solution.py
@@ -102,7 +102,7 @@
             jax.ShapeDtypeStruct((owners, 1, 16 * cand.shape[0] + entries), f32),
             jax.ShapeDtypeStruct((8, entries * per_tile), i32),
         ),
-        compiler_params=settings(58),
+        compiler_params=settings(59),
         name="announce",
     )(tile_owners, cand, teacher)
 
@@ -179,7 +179,7 @@
             ],
         ),
         out_shape=jax.ShapeDtypeStruct((owners, width, blocks * 8), bf16),
-        compiler_params=settings(58),
+        compiler_params=settings(59),
         name="route",
     )(tok, told, hidden)
 
@@ -237,7 +237,7 @@
             jax.ShapeDtypeStruct((panel, rows), f32),
             jax.ShapeDtypeStruct((8, rows), f32),
         ),
-        compiler_params=settings(58),
+        compiler_params=settings(59),
         cost_estimate=pl.CostEstimate(
             flops=2 * 64 * panel * rows, bytes_accessed=8 * panel * rows, transcendentals=64 * rows
         ),
@@ -342,7 +342,7 @@
             pltpu.SemaphoreType.DMA,
             pltpu.SemaphoreType.DMA((count // 128,)),
         ],
-        compiler_params=settings(56),
+        compiler_params=settings(59),
         name="score",
     )(head, rows, dense, facts)
 
@@ -368,7 +368,7 @@
         in_specs=[columns, columns],
         out_specs=[rows, rows],
         out_shape=[jax.ShapeDtypeStruct((count, panel), f32)] * 2,
-        compiler_params=settings(56),
+        compiler_params=settings(59),
         cost_estimate=pl.CostEstimate(
             flops=4 * panel * count, bytes_accessed=16 * panel * count, transcendentals=0
         ),
@@ -430,7 +430,7 @@
         scale = jnp.broadcast_to(scale, (chunk, chunk)).T
         tables[k][0].wait()
         tables[k][1].wait()
-        if k == 2:
+        if k == 0:
             for copy in heads[:2]:
                 copy.start()
         for col in range(0, panel, chunk):
@@ -457,7 +457,7 @@
 def grad_parts(logs, facts, own, part, dense, head, per_tile):
     panel, width = head.shape
     count = part.shape[0]
-    block = 512
+    block = 1024
     return pl.pallas_call(
         functools.partial(part_kernel, per_tile),
         in_specs=[far] * 6,
@@ -479,7 +479,7 @@
             pltpu.SemaphoreType.DMA((width // block,)),
             pltpu.SemaphoreType.DMA((2,)),
         ],
-        compiler_params=settings(56),
+        compiler_params=settings(59),
         name="grad_parts",
     )(logs, facts, own, part, dense, head)
 
@@ -562,7 +562,7 @@
             jax.ShapeDtypeStruct((1, tokens), f32),
             jax.ShapeDtypeStruct((tokens, count), bf16),
         ),
-        compiler_params=settings(58),
+        compiler_params=settings(59),
         cost_estimate=pl.CostEstimate(
             flops=12 * 2 * count * tokens * 128, bytes_accessed=4 * count * tokens, transcendentals=0
         ),
@@ -587,7 +587,7 @@
         ],
         out_specs=pl.BlockSpec((tokens, block), lambda s: (0, s)),
         out_shape=jax.ShapeDtypeStruct((tokens, width), bf16),
-        compiler_params=settings(58),
+        compiler_params=settings(59),
         name="combine",
     )(table, parts)
 

time: 382 us -> 381 us (level)
  no operation moved by 1% of the time
where the time goes in v5:
time: 381 us; the launch traced here: 380 us
  waiting for transfers between devices  242 us (64%)
  Pallas kernels  102 us (27%)
  starting transfers between devices  32.7 us (9%)
    all_to_all x4, waiting for transfers between devices, exchange(): lax.all_to_all(values, ('tok', 'voc'), split_axis=0, concat_axis=0, tiled...  242 us
    all_to_all x4, starting transfers between devices, exchange(): lax.all_to_all(values, ('tok', 'voc'), split_axis=0, concat_axis=0, tiled...  32.7 us
    pallas_call x1, Pallas kernels, place(): pl.pallas_call(functools.partial(place_kernel, per_tile), grid_spec=pltpu...  22.4 us
    pallas_call x1, Pallas kernels, grad_parts(): pl.pallas_call(functools.partial(part_kernel, per_tile), in_specs=[far] *...  17 us
    pallas_call x1, Pallas kernels, score(): pl.pallas_call(functools.partial(score_kernel, bounds), in_specs=[far, fa...  15.6 us
    pallas_call x1, Pallas kernels, grad_of_head(): pl.pallas_call(head_kernel, grid=(width // block,), in_specs=[pl.BlockSpe...  15.1 us
    pallas_call x1, Pallas kernels, route(): pl.pallas_call(functools.partial(route_kernel, per_tile), grid_spec=pltpu...  13 us
  transfers between devices with their start and end apart: 4, of which 4 were waited for; matrix products, arithmetic and copies ran while one was open for 0% of the time, Pallas kernels for 12%

profile of v5, /device:TPU:97, one launch (start us, length us, event | category | flops | bytes accessed | tf_op | source)
XLA Modules:
  0.0 379.7 jit_solution(8280616382068825970)
XLA Ops:
  0.6 3.0 announce.1
  3.7 10.2 %all-to-all-start = ((f32[128,1,1152]{2,1,0:T(1,128)}), f32[128,1,1152]{2,1,0:T(1,128)S(1)}, u32[]{:S(2)}, u32[]{:S(2)}) async-start(f32[128,1,1152]{2,1,0:T(1,128)} %get-tuple-element.16), calls=%async_computation | async-start | bytes 1179648 | tf_op jit(solution)/shard_map/all_to_all | solution.py:596
  13.9 11.6 %all-to-all-done.codes_ref.told_ref = f32[128,1,1152]{2,1,0:T(1,128)S(1)} async-done(((f32[128,1,1152]{2,1,0:T(1,128)}), f32[128,1,1152]{2,1,0:T(1,128)S(1)}, u32[]{:S(2)}, u32[]{:S(2)}) %all-to-all-start) | async-done | bytes 589856 | tf_op jit(solution)/shard_map/all_to_all | solution.py:596
  25.5 0.0 copy-start.1
  25.5 0.8 copy-done.1
  26.3 13.0 %route.1 = bf16[128,160,256]{2,1,0:T(8,128)(2,1)} custom-call(s32[1]{0:T(128)} %bitcast.1.tok_ref, f32[128,1,1152]{2,1,0:T(1,128)} %copy-done.1, bf16[160,8192]{1,0:T(8,128)(2,1)} %bitcast.11), custom_call_target="tpu_custom_call" | custom-call | tf_op jit(solution)/shard_map/route/pallas_call | solution.py:162
  39.3 7.6 %all-to-all-start.1 = ((bf16[128,160,256]{2,1,0:T(8,128)(2,1)}), bf16[128,160,256]{2,1,0:T(8,128)(2,1)}, u32[]{:S(2)}, u32[]{:S(2)}) async-start(bf16[128,160,256]{2,1,0:T(8,128)(2,1)} %route.1), calls=%async_computation.1 | async-start | bytes 20971520 | tf_op jit(solution)/shard_map/all_to_all | solution.py:596
  46.9 22.4 %place.1 = (f32[768,1024]{1,0:T(8,128)}, f32[8,1024]{1,0:T(8,128)}) custom-call(s32[1]{0:T(128)} %bitcast.owner_ref.me_ref, f32[128,1,1152]{2,1,0:T(1,128)} %copy-done.1), custom_call_target="tpu_custom_call" | custom-call | flops 100663296 | bytes 6291456 | tf_op jit(solution)/shard_map/place/pallas_call | solution.py:225
  69.3 111.2 %all-to-all-done.1 = bf16[128,160,256]{2,1,0:T(8,128)(2,1)} async-done(((bf16[128,160,256]{2,1,0:T(8,128)(2,1)}), bf16[128,160,256]{2,1,0:T(8,128)(2,1)}, u32[]{:S(2)}, u32[]{:S(2)}) %all-to-all-start.1) | async-done | bytes 10485792 | tf_op jit(solution)/shard_map/all_to_all | solution.py:596
  180.5 15.6 %score.1 = (f32[768,1024]{1,0:T(8,128)}, f32[8,1024]{1,0:T(8,128)}, f32[128,1,1152]{2,1,0:T(1,128)}) custom-call(bf16[768,5120]{1,0:T(8,128)(2,1)} %head_ref.3, bf16[4,5120,256]{2,1,0:T(8,128)(2,1)} %bitcast.6.rows_ref, f32[768,1024]{1,0:T(8,128)} %get-tuple-element.17.dense_ref, f32[8,1024]{1,0:T(8,128)} %get-tuple-element.18.facts_ref), custom_call_target="tpu_custom_call" | custom-call | tf_op jit(solution)/shard_map/score/pallas_call | solution.py:326
  196.1 7.3 %all-to-all-start.2 = ((f32[128,1,1152]{2,1,0:T(1,128)}), f32[128,1,1152]{2,1,0:T(1,128)S(1)}, u32[]{:S(2)}, u32[]{:S(2)}) async-start(f32[128,1,1152]{2,1,0:T(1,128)} %get-tuple-element.19), calls=%async_computation.2 | async-start | bytes 1179648 | tf_op jit(solution)/shard_map/all_to_all | solution.py:596
  203.4 6.2 %turn.1 = (f32[1024,768]{1,0:T(8,128)}, f32[1024,768]{1,0:T(8,128)}) custom-call(f32[768,1024]{1,0:T(8,128)} %get-tuple-element.24.part_ref, f32[768,1024]{1,0:T(8,128)} %get-tuple-element.17.dense_ref), custom_call_target="tpu_custom_call" | custom-call | flops 3145728 | bytes 12582912 | tf_op jit(solution)/shard_map/turn/pallas_call | solution.py:365
  209.6 5.5 %all-to-all-done.2.logs_ref = f32[128,1,1152]{2,1,0:T(1,128)S(1)} async-done(((f32[128,1,1152]{2,1,0:T(1,128)}), f32[128,1,1152]{2,1,0:T(1,128)S(1)}, u32[]{:S(2)}, u32[]{:S(2)}) %all-to-all-start.2) | async-done | bytes 589856 | tf_op jit(solution)/shard_map/all_to_all | solution.py:596
  215.0 0.0 copy-start.2
  215.0 0.8 copy-done.2
  215.9 17.0 %grad_parts.1 = (bf16[1024,5120]{1,0:T(8,128)(2,1)}, bf16[1024,768]{1,0:T(8,128)(2,1)}) custom-call(f32[128,1,1152]{2,1,0:T(1,128)} %copy-done.2, f32[8,1024]{1,0:T(8,128)} %get-tuple-element.18.facts_ref, f32[8,1024]{1,0:T(8,128)} %get-tuple-element.23.own_ref, f32[1024,768]{1,0:T(8,128)} %get-tuple-element.25.part_ref, ...), custom_call_target="tpu_custom_call" | custom-call | tf_op jit(solution)/shard_map/grad_parts/pallas_call | solution.py:461
  232.8 0.0 copy-start
  232.8 7.7 %all-to-all-start.3 = ((bf16[128,8,5120]{2,1,0:T(8,128)(2,1)}), bf16[128,8,5120]{2,1,0:T(8,128)(2,1)}, u32[]{:S(2)}, u32[]{:S(2)}) async-start(bf16[128,8,5120]{2,1,0:T(8,128)(2,1)} %bitcast.10), calls=%async_computation.3 | async-start | bytes 20971520 | tf_op jit(solution)/shard_map/all_to_all | solution.py:596
  240.5 3.2 losses.1
  243.7 0.0 copy-done
  243.7 15.1 %grad_of_head.1 = bf16[768,5120]{1,0:T(8,128)(2,1)} custom-call(bf16[1024,768]{1,0:T(8,128)(2,1)S(1)} %copy-done, bf16[4,5120,256]{2,1,0:T(8,128)(2,1)} %bitcast.6.rows_ref), custom_call_target="tpu_custom_call" | custom-call | flops 8053063680 | bytes 18350080 | tf_op jit(solution)/shard_map/grad_of_head/pallas_call | solution.py:505
  258.8 114.1 %all-to-all-done.3 = bf16[128,8,5120]{2,1,0:T(8,128)(2,1)} async-done(((bf16[128,8,5120]{2,1,0:T(8,128)(2,1)}), bf16[128,8,5120]{2,1,0:T(8,128)(2,1)}, u32[]{:S(2)}, u32[]{:S(2)}) %all-to-all-start.3) | async-done | bytes 10485792 | tf_op jit(solution)/shard_map/all_to_all | solution.py:596
  372.9 6.8 %combine.1 = bf16[256,5120]{1,0:T(8,128)(2,1)} custom-call(bf16[256,1024]{1,0:T(8,128)(2,1)} %get-tuple-element.22.table_ref, bf16[1024,5120]{1,0:T(8,128)(2,1)} %bitcast.9.parts_ref), custom_call_target="tpu_custom_call" | custom-call | tf_op jit(solution)/shard_map/combine/pallas_call | solution.py:581
Async XLA Ops:
  3.7 21.8 %all-to-all-start = ((f32[128,1,1152]{2,1,0:T(1,128)}), f32[128,1,1152]{2,1,0:T(1,128)S(1)}, u32[]{:S(2)}, u32[]{:S(2)}) async-start(f32[128,1,1152]{2,1,0:T(1,128)} %get-tuple-element.16), calls=%async_computation | async-start | bytes 1179648 | tf_op jit(solution)/shard_map/all_to_all | solution.py:596
  25.5 0.8 copy-start.1
  39.3 141.2 %all-to-all-start.1 = ((bf16[128,160,256]{2,1,0:T(8,128)(2,1)}), bf16[128,160,256]{2,1,0:T(8,128)(2,1)}, u32[]{:S(2)}, u32[]{:S(2)}) async-start(bf16[128,160,256]{2,1,0:T(8,128)(2,1)} %route.1), calls=%async_computation.1 | async-start | bytes 20971520 | tf_op jit(solution)/shard_map/all_to_all | solution.py:596
  196.1 18.9 %all-to-all-start.2 = ((f32[128,1,1152]{2,1,0:T(1,128)}), f32[128,1,1152]{2,1,0:T(1,128)S(1)}, u32[]{:S(2)}, u32[]{:S(2)}) async-start(f32[128,1,1152]{2,1,0:T(1,128)} %get-tuple-element.19), calls=%async_computation.2 | async-start | bytes 1179648 | tf_op jit(solution)/shard_map/all_to_all | solution.py:596
  215.0 0.8 copy-start.2
  232.8 10.9 %copy-start = (bf16[1024,768]{1,0:T(8,128)(2,1)S(1)}, bf16[1024,768]{1,0:T(8,128)(2,1)}, u32[]{:S(2)}) copy-start(bf16[1024,768]{1,0:T(8,128)(2,1)} %get-tuple-element.28.weight_ref) | copy-start | bytes 4718596
  232.8 140.1 %all-to-all-start.3 = ((bf16[128,8,5120]{2,1,0:T(8,128)(2,1)}), bf16[128,8,5120]{2,1,0:T(8,128)(2,1)}, u32[]{:S(2)}, u32[]{:S(2)}) async-start(bf16[128,8,5120]{2,1,0:T(8,128)(2,1)} %bitcast.10), calls=%async_computation.3 | async-start | bytes 20971520 | tf_op jit(solution)/shard_map/all_to_all | solution.py:596

commit v6 on v5

--- a/solution.py
+++ b/solution.py
@@ -107,7 +107,9 @@
     )(tile_owners, cand, teacher)
 
 
-def route_kernel(per_tile, tok_ref, codes_ref, hidden_ref, out_ref, rows_ref, held_ref):
+def route_kernel(
+    per_tile, tok_ref, codes_ref, hidden_ref, told_ref, out_ref, kept_ref, rows_ref, held_ref, pass_ref, sems
+):
     step = pl.program_id(0)
     width = hidden_ref.shape[0]
     owners, lanes, _ = held_ref.shape
@@ -119,6 +121,7 @@
     @pl.when(step == 0)
     def _():
         rows_ref[...] = rows_of(codes_ref[:, 0, :], per_tile)
+        pltpu.make_async_copy(told_ref, pass_ref, sems.at[0]).start()
 
     @pl.when(step < steps)
     def _():
@@ -150,6 +153,15 @@
         for k in range(count):
             out_ref[k] = held_ref[(step - steps) * count + k].T
 
+    @pl.when(step == 1)
+    def _():
+        pltpu.make_async_copy(told_ref, pass_ref, sems.at[0]).wait()
+        pltpu.make_async_copy(pass_ref, kept_ref, sems.at[1]).start()
+
+    @pl.when(step == pl.num_programs(0) - 1)
+    def _():
+        pltpu.make_async_copy(pass_ref, kept_ref, sems.at[1]).wait()
+
 
 def route(tok, told, hidden, per_tile, blocks):
     width, total = hidden.shape
@@ -169,19 +181,28 @@
                 pl.BlockSpec(
                     (width, 2 * pairs * tokens), lambda s, t: (0, jnp.minimum(s, steps - 1))
                 ),
+                far,
             ],
-            out_specs=pl.BlockSpec(
-                (turn, width, blocks * 8), lambda s, t: (jnp.maximum(s - steps, 0), 0, 0)
-            ),
+            out_specs=[
+                pl.BlockSpec(
+                    (turn, width, blocks * 8), lambda s, t: (jnp.maximum(s - steps, 0), 0, 0)
+                ),
+                far,
+            ],
             scratch_shapes=[
                 pltpu.VMEM((blocks, 2 * tokens), i32),
                 pltpu.VMEM((owners, blocks * 8, width), bf16),
+                pltpu.VMEM(told.shape, f32),
+                pltpu.SemaphoreType.DMA((2,)),
             ],
         ),
-        out_shape=jax.ShapeDtypeStruct((owners, width, blocks * 8), bf16),
+        out_shape=(
+            jax.ShapeDtypeStruct((owners, width, blocks * 8), bf16),
+            jax.ShapeDtypeStruct(told.shape, f32),
+        ),
         compiler_params=settings(59),
         name="route",
-    )(tok, told, hidden)
+    )(tok, told, hidden, told)
 
 
 def place_kernel(per_tile, owner_ref, told_ref, dense_ref, facts_ref):
@@ -377,9 +398,9 @@
 
 
 def part_kernel(
-    per_tile, logs_ref, facts_ref, own_ref, part_ref, dense_ref, head_ref, out_ref, weight_ref,
+    per_tile, logs_ref, facts_ref, own_ref, part_ref, dense_ref, head_ref, out_ref, weight_ref, kept_ref,
     logs_held, facts_held, own_held, part_held, dense_held, head_held, out_held,
-    small_sems, sems, head_sems, out_sems
+    small_sems, kept_sem, sems, head_sems, out_sems
 ):
     count, panel = part_ref.shape
     owners = logs_ref.shape[0]
@@ -403,7 +424,7 @@
             )
         )
         tables[-1][0].start()
-        tables[-1][1].start()
+        tables[-1][1].start(priority=1)
     for k in range(blocks):
         here = slice(k * block, (k + 1) * block)
         heads.append(
@@ -411,6 +432,8 @@
         )
     for copy in small:
         copy.wait()
+    keep = pltpu.make_async_copy(logs_held, kept_ref, kept_sem)
+    keep.start(priority=1)
     for k, at in enumerate(range(0, count, chunk)):
         here = slice(at, at + chunk)
         logs = logs_held[:, 0, here]
@@ -449,9 +472,10 @@
         leave.append(
             pltpu.make_async_copy(out_held.at[k % slots], out_ref.at[:, here], out_sems.at[k % slots])
         )
-        leave[-1].start()
+        leave[-1].start(priority=1)
     for copy in leave[blocks - slots :]:
         copy.wait()
+    keep.wait()
 
 
 def grad_parts(logs, facts, own, part, dense, head, per_tile):
@@ -461,10 +485,11 @@
     return pl.pallas_call(
         functools.partial(part_kernel, per_tile),
         in_specs=[far] * 6,
-        out_specs=[far, near],
+        out_specs=[far, near, far],
         out_shape=(
             jax.ShapeDtypeStruct((count, width), bf16),
             jax.ShapeDtypeStruct((count, panel), bf16),
+            jax.ShapeDtypeStruct(logs.shape, f32),
         ),
         scratch_shapes=[
             pltpu.VMEM(logs.shape, f32),
@@ -475,6 +500,7 @@
             pltpu.VMEM((panel, width), bf16),
             pltpu.VMEM((2, count, block), bf16),
             pltpu.SemaphoreType.DMA((3,)),
+            pltpu.SemaphoreType.DMA,
             pltpu.SemaphoreType.DMA((2, count // 128)),
             pltpu.SemaphoreType.DMA((width // block,)),
             pltpu.SemaphoreType.DMA((2,)),
@@ -609,13 +635,13 @@
     teacher = teacher_logp.T
     told, home_rows = announce(tile_owners.T, cand_pos.T, teacher, panel, per_tile, owners)
     told = exchange(told)
-    sent = route(tok.astype(i32).reshape(1), told, hidden.T, per_tile, blocks)
+    sent, told = route(tok.astype(i32).reshape(1), told, hidden.T, per_tile, blocks)
     rows = exchange(sent).reshape(tok_size, width, blocks * 8)
     dense, facts = place(me, told, panel, per_tile)
     part, own, logs = score(head_weight, rows, dense, facts, owners)
     logs = exchange(logs)
     part_rows, dense_rows = turn(part, dense)
-    parts, weight = grad_parts(logs, facts, own, part_rows, dense_rows, head_weight, per_tile)
+    parts, weight, logs = grad_parts(logs, facts, own, part_rows, dense_rows, head_weight, per_tile)
     home_parts = exchange(parts.reshape(owners, 8, width)).reshape(count, width)
     grad_head = grad_of_head(weight, rows)
     loss, table = losses(me, logs, home_rows, teacher, count)

time: 381 us -> 380 us (level)
  no operation moved by 1% of the time
where the time goes in v6:
time: 380 us; the launch traced here: 379 us
  waiting for transfers between devices  244 us (64%)
  Pallas kernels  101 us (27%)
  starting transfers between devices  30.3 us (8%)
    all_to_all x4, waiting for transfers between devices, exchange(): lax.all_to_all(values, ('tok', 'voc'), split_axis=0, concat_axis=0, tiled...  244 us
    all_to_all x4, starting transfers between devices, exchange(): lax.all_to_all(values, ('tok', 'voc'), split_axis=0, concat_axis=0, tiled...  30.3 us
    pallas_call x1, Pallas kernels, place(): pl.pallas_call(functools.partial(place_kernel, per_tile), grid_spec=pltpu...  22.4 us
    pallas_call x1, Pallas kernels, grad_parts(): pl.pallas_call(functools.partial(part_kernel, per_tile), in_specs=[far] *...  16.1 us
    pallas_call x1, Pallas kernels, score(): pl.pallas_call(functools.partial(score_kernel, bounds), in_specs=[far, fa...  15.6 us
    pallas_call x1, Pallas kernels, grad_of_head(): pl.pallas_call(head_kernel, grid=(width // block,), in_specs=[pl.BlockSpe...  15.1 us
    pallas_call x1, Pallas kernels, route(): pl.pallas_call(functools.partial(route_kernel, per_tile), grid_spec=pltpu...  13 us
  transfers between devices with their start and end apart: 4, of which 4 were waited for; matrix products, arithmetic and copies ran while one was open for 0% of the time, Pallas kernels for 12%

profile of v6, /device:TPU:97, one launch (start us, length us, event | category | flops | bytes accessed | tf_op | source)
XLA Modules:
  0.0 378.6 jit_solution(3103162180473925963)
XLA Ops:
  0.6 3.0 announce.1
  3.7 10.2 %all-to-all-start = ((f32[128,1,1152]{2,1,0:T(1,128)}), f32[128,1,1152]{2,1,0:T(1,128)S(1)}, u32[]{:S(2)}, u32[]{:S(2)}) async-start(f32[128,1,1152]{2,1,0:T(1,128)} %get-tuple-element.19), calls=%async_computation | async-start | bytes 1179648 | tf_op jit(solution)/shard_map/all_to_all | solution.py:622
  13.9 11.6 %all-to-all-done.codes_ref.told_ref = f32[128,1,1152]{2,1,0:T(1,128)S(1)} async-done(((f32[128,1,1152]{2,1,0:T(1,128)}), f32[128,1,1152]{2,1,0:T(1,128)S(1)}, u32[]{:S(2)}, u32[]{:S(2)}) %all-to-all-start) | async-done | bytes 589856 | tf_op jit(solution)/shard_map/all_to_all | solution.py:622
  25.5 0.0 copy-start.1
  25.5 0.8 copy-done.1
  26.3 13.0 %route.1 = (bf16[128,160,256]{2,1,0:T(8,128)(2,1)}, f32[128,1,1152]{2,1,0:T(1,128)}) custom-call(s32[1]{0:T(128)} %bitcast.1.tok_ref, f32[128,1,1152]{2,1,0:T(1,128)} %copy-done.1, bf16[160,8192]{1,0:T(8,128)(2,1)} %bitcast.11, f32[128,1,1152]{2,1,0:T(1,128)} %copy-done.1), custom_call_target="tpu_custom_call" | custom-call | tf_op jit(solution)/shard_map/route/pallas_call | solution.py:174
  39.3 7.6 %all-to-all-start.1 = ((bf16[128,160,256]{2,1,0:T(8,128)(2,1)}), bf16[128,160,256]{2,1,0:T(8,128)(2,1)}, u32[]{:S(2)}, u32[]{:S(2)}) async-start(bf16[128,160,256]{2,1,0:T(8,128)(2,1)} %get-tuple-element.20), calls=%async_computation.1 | async-start | bytes 20971520 | tf_op jit(solution)/shard_map/all_to_all | solution.py:622
  46.9 22.4 %place.1 = (f32[768,1024]{1,0:T(8,128)}, f32[8,1024]{1,0:T(8,128)}) custom-call(s32[1]{0:T(128)} %bitcast.owner_ref.me_ref, f32[128,1,1152]{2,1,0:T(1,128)} %get-tuple-element.21.told_ref), custom_call_target="tpu_custom_call" | custom-call | flops 100663296 | bytes 6291456 | tf_op jit(solution)/shard_map/place/pallas_call | solution.py:246
  69.3 113.5 %all-to-all-done.1 = bf16[128,160,256]{2,1,0:T(8,128)(2,1)} async-done(((bf16[128,160,256]{2,1,0:T(8,128)(2,1)}), bf16[128,160,256]{2,1,0:T(8,128)(2,1)}, u32[]{:S(2)}, u32[]{:S(2)}) %all-to-all-start.1) | async-done | bytes 10485792 | tf_op jit(solution)/shard_map/all_to_all | solution.py:622
  182.9 15.6 %score.1 = (f32[768,1024]{1,0:T(8,128)}, f32[8,1024]{1,0:T(8,128)}, f32[128,1,1152]{2,1,0:T(1,128)}) custom-call(bf16[768,5120]{1,0:T(8,128)(2,1)} %head_ref.3, bf16[4,5120,256]{2,1,0:T(8,128)(2,1)} %bitcast.6.rows_ref, f32[768,1024]{1,0:T(8,128)} %get-tuple-element.22.dense_ref, f32[8,1024]{1,0:T(8,128)} %get-tuple-element.23.facts_ref), custom_call_target="tpu_custom_call" | custom-call | tf_op jit(solution)/shard_map/score/pallas_call | solution.py:347
  198.5 4.9 %all-to-all-start.2 = ((f32[128,1,1152]{2,1,0:T(1,128)}), f32[128,1,1152]{2,1,0:T(1,128)S(1)}, u32[]{:S(2)}, u32[]{:S(2)}) async-start(f32[128,1,1152]{2,1,0:T(1,128)} %get-tuple-element.24), calls=%async_computation.2 | async-start | bytes 1179648 | tf_op jit(solution)/shard_map/all_to_all | solution.py:622
  203.4 6.2 %turn.1 = (f32[1024,768]{1,0:T(8,128)}, f32[1024,768]{1,0:T(8,128)}) custom-call(f32[768,1024]{1,0:T(8,128)} %get-tuple-element.26.part_ref, f32[768,1024]{1,0:T(8,128)} %get-tuple-element.22.dense_ref), custom_call_target="tpu_custom_call" | custom-call | flops 3145728 | bytes 12582912 | tf_op jit(solution)/shard_map/turn/pallas_call | solution.py:386
  209.6 5.5 %all-to-all-done.2.logs_ref = f32[128,1,1152]{2,1,0:T(1,128)S(1)} async-done(((f32[128,1,1152]{2,1,0:T(1,128)}), f32[128,1,1152]{2,1,0:T(1,128)S(1)}, u32[]{:S(2)}, u32[]{:S(2)}) %all-to-all-start.2) | async-done | bytes 589856 | tf_op jit(solution)/shard_map/all_to_all | solution.py:622
  215.1 0.0 copy-start.2
  215.1 0.8 copy-done.2
  215.9 16.1 %grad_parts.1 = (bf16[1024,5120]{1,0:T(8,128)(2,1)}, bf16[1024,768]{1,0:T(8,128)(2,1)}, f32[128,1,1152]{2,1,0:T(1,128)}) custom-call(f32[128,1,1152]{2,1,0:T(1,128)} %copy-done.2, f32[8,1024]{1,0:T(8,128)} %get-tuple-element.23.facts_ref, f32[8,1024]{1,0:T(8,128)} %get-tuple-element.25.own_ref, f32[1024,768]{1,0:T(8,128)} %get-tuple-element.27.part_ref, ...), custom_call_target="tpu_custom_call" | custom-call | tf_op jit(solution)/shard_map/grad_parts/pallas_call | solution.py:485
  232.0 0.0 copy-start
  232.0 7.7 %all-to-all-start.3 = ((bf16[128,8,5120]{2,1,0:T(8,128)(2,1)}), bf16[128,8,5120]{2,1,0:T(8,128)(2,1)}, u32[]{:S(2)}, u32[]{:S(2)}) async-start(bf16[128,8,5120]{2,1,0:T(8,128)(2,1)} %bitcast.10), calls=%async_computation.3 | async-start | bytes 20971520 | tf_op jit(solution)/shard_map/all_to_all | solution.py:622
  239.7 3.2 losses.1
  242.9 0.0 copy-done
  242.9 15.1 %grad_of_head.1 = bf16[768,5120]{1,0:T(8,128)(2,1)} custom-call(bf16[1024,768]{1,0:T(8,128)(2,1)S(1)} %copy-done, bf16[4,5120,256]{2,1,0:T(8,128)(2,1)} %bitcast.6.rows_ref), custom_call_target="tpu_custom_call" | custom-call | flops 8053063680 | bytes 18350080 | tf_op jit(solution)/shard_map/grad_of_head/pallas_call | solution.py:531
  258.0 113.8 %all-to-all-done.3 = bf16[128,8,5120]{2,1,0:T(8,128)(2,1)} async-done(((bf16[128,8,5120]{2,1,0:T(8,128)(2,1)}), bf16[128,8,5120]{2,1,0:T(8,128)(2,1)}, u32[]{:S(2)}, u32[]{:S(2)}) %all-to-all-start.3) | async-done | bytes 10485792 | tf_op jit(solution)/shard_map/all_to_all | solution.py:622
  371.8 6.8 %combine.1 = bf16[256,5120]{1,0:T(8,128)(2,1)} custom-call(bf16[256,1024]{1,0:T(8,128)(2,1)} %get-tuple-element.32.table_ref, bf16[1024,5120]{1,0:T(8,128)(2,1)} %bitcast.9.parts_ref), custom_call_target="tpu_custom_call" | custom-call | tf_op jit(solution)/shard_map/combine/pallas_call | solution.py:607
Async XLA Ops:
  3.7 21.8 %all-to-all-start = ((f32[128,1,1152]{2,1,0:T(1,128)}), f32[128,1,1152]{2,1,0:T(1,128)S(1)}, u32[]{:S(2)}, u32[]{:S(2)}) async-start(f32[128,1,1152]{2,1,0:T(1,128)} %get-tuple-element.19), calls=%async_computation | async-start | bytes 1179648 | tf_op jit(solution)/shard_map/all_to_all | solution.py:622
  25.5 0.8 copy-start.1
  39.3 143.5 %all-to-all-start.1 = ((bf16[128,160,256]{2,1,0:T(8,128)(2,1)}), bf16[128,160,256]{2,1,0:T(8,128)(2,1)}, u32[]{:S(2)}, u32[]{:S(2)}) async-start(bf16[128,160,256]{2,1,0:T(8,128)(2,1)} %get-tuple-element.20), calls=%async_computation.1 | async-start | bytes 20971520 | tf_op jit(solution)/shard_map/all_to_all | solution.py:622
  198.5 16.6 %all-to-all-start.2 = ((f32[128,1,1152]{2,1,0:T(1,128)}), f32[128,1,1152]{2,1,0:T(1,128)S(1)}, u32[]{:S(2)}, u32[]{:S(2)}) async-start(f32[128,1,1152]{2,1,0:T(1,128)} %get-tuple-element.24), calls=%async_computation.2 | async-start | bytes 1179648 | tf_op jit(solution)/shard_map/all_to_all | solution.py:622
  215.1 0.8 copy-start.2
  232.0 10.9 %copy-start = (bf16[1024,768]{1,0:T(8,128)(2,1)S(1)}, bf16[1024,768]{1,0:T(8,128)(2,1)}, u32[]{:S(2)}) copy-start(bf16[1024,768]{1,0:T(8,128)(2,1)} %get-tuple-element.34.weight_ref) | copy-start | bytes 4718596
  232.0 139.8 %all-to-all-start.3 = ((bf16[128,8,5120]{2,1,0:T(8,128)(2,1)}), bf16[128,8,5120]{2,1,0:T(8,128)(2,1)}, u32[]{:S(2)}, u32[]{:S(2)}) async-start(bf16[128,8,5120]{2,1,0:T(8,128)(2,1)} %bitcast.10), calls=%async_computation.3 | async-start | bytes 20971520 | tf_op jit(solution)/shard_map/all_to_all | solution.py:622

commit v7 on v6

--- a/solution.py
+++ b/solution.py
@@ -318,7 +318,9 @@
         leave[-1].start()
         whole = jnp.sum(part, axis=0, keepdims=True)
         log = jnp.where(whole > 0.0, most + jnp.log(jnp.maximum(whole, 1.0)), nothing)
-        shares.append(facts_ref[2:3, here] - jnp.sum(dense * score, axis=0, keepdims=True))
+        shares.append(
+            facts_ref[2:3, here] - jnp.sum(dense * (score - log), axis=0, keepdims=True)
+        )
         logs.append(log)
         largest.append(most)
     logs = jnp.concatenate(logs, axis=1)
@@ -548,7 +550,7 @@
     )(weight, rows)
 
 
-def loss_kernel(me_ref, logs_ref, rows_ref, teacher_ref, loss_ref, table_ref):
+def loss_kernel(panel, me_ref, logs_ref, rows_ref, cand_ref, teacher_ref, loss_ref, table_ref):
     owners = logs_ref.shape[0]
     tokens = teacher_ref.shape[1]
     count = table_ref.shape[1]
@@ -569,9 +571,14 @@
                 found.append(got)
             else:
                 total = total + got
-    teacher = teacher_ref[...]
-    mass = jnp.sum(jnp.exp(teacher), axis=0, keepdims=True)
-    loss_ref[...] = total + mass * log_sum(found[0], found[1])
+    target = jnp.exp(teacher_ref[...])
+    whole = log_sum(found[0], found[1])
+    first = cand_ref[...] < panel
+    for group in range(2):
+        named = first if group == 0 else ~first
+        mass = jnp.sum(jnp.where(named, target, 0.0), axis=0, keepdims=True)
+        total = total + mass * (whole - found[group])
+    loss_ref[...] = total
     first, second = rows_ref[0:1, 0:tokens], rows_ref[0:1, tokens : 2 * tokens]
     for at in range(0, count, 128):
         row = iota((128, tokens), 0) + at
@@ -579,11 +586,11 @@
         table_ref[:, at : at + 128] = hot.T.astype(bf16)
 
 
-def losses(me, logs, rows, teacher, count):
+def losses(me, logs, rows, cand, teacher, panel, count):
     tokens = teacher.shape[1]
     return pl.pallas_call(
-        loss_kernel,
-        in_specs=[pl.BlockSpec(memory_space=pltpu.SMEM)] + [pl.BlockSpec(memory_space=pltpu.VMEM)] * 3,
+        functools.partial(loss_kernel, panel),
+        in_specs=[pl.BlockSpec(memory_space=pltpu.SMEM), near, near, near, near],
         out_shape=(
             jax.ShapeDtypeStruct((1, tokens), f32),
             jax.ShapeDtypeStruct((tokens, count), bf16),
@@ -593,7 +600,7 @@
             flops=12 * 2 * count * tokens * 128, bytes_accessed=4 * count * tokens, transcendentals=0
         ),
         name="losses",
-    )(me, logs, rows, teacher)
+    )(me, logs, rows, cand, teacher)
 
 
 def combine_kernel(table_ref, parts_ref, out_ref):
@@ -644,7 +651,7 @@
     parts, weight, logs = grad_parts(logs, facts, own, part_rows, dense_rows, head_weight, per_tile)
     home_parts = exchange(parts.reshape(owners, 8, width)).reshape(count, width)
     grad_head = grad_of_head(weight, rows)
-    loss, table = losses(me, logs, home_rows, teacher, count)
+    loss, table = losses(me, logs, home_rows, cand_pos.T, teacher, panel, count)
     grad_hidden = combine(table, home_parts)
     return (loss.reshape(tokens), grad_hidden, grad_head)
 

time: 380 us -> 380 us (level)
  no operation moved by 1% of the time
where the time goes in v7:
time: 380 us
  waiting for transfers between devices  245 us (64%)
  Pallas kernels  102 us (27%)
  starting transfers between devices  30.3 us (8%)
    all_to_all x4, waiting for transfers between devices, exchange(): lax.all_to_all(values, ('tok', 'voc'), split_axis=0, concat_axis=0, tiled...  245 us
    all_to_all x4, starting transfers between devices, exchange(): lax.all_to_all(values, ('tok', 'voc'), split_axis=0, concat_axis=0, tiled...  30.3 us
    pallas_call x1, Pallas kernels, place(): pl.pallas_call(functools.partial(place_kernel, per_tile), grid_spec=pltpu...  22.4 us
    pallas_call x1, Pallas kernels, grad_parts(): pl.pallas_call(functools.partial(part_kernel, per_tile), in_specs=[far] *...  16.1 us
    pallas_call x1, Pallas kernels, score(): pl.pallas_call(functools.partial(score_kernel, bounds), in_specs=[far, fa...  15.6 us
    pallas_call x1, Pallas kernels, grad_of_head(): pl.pallas_call(head_kernel, grid=(width // block,), in_specs=[pl.BlockSpe...  15.1 us
    pallas_call x1, Pallas kernels, route(): pl.pallas_call(functools.partial(route_kernel, per_tile), grid_spec=pltpu...  13 us
  transfers between devices with their start and end apart: 4, of which 4 were waited for; matrix products, arithmetic and copies ran while one was open for 0% of the time, Pallas kernels for 12%

profile of v7, /device:TPU:97, one launch (start us, length us, event | category | flops | bytes accessed | tf_op | source)
XLA Modules:
  0.0 379.5 jit_solution(2212011368735281506)
XLA Ops:
  0.6 3.1 announce.1
  3.7 10.2 %all-to-all-start = ((f32[128,1,1152]{2,1,0:T(1,128)}), f32[128,1,1152]{2,1,0:T(1,128)S(1)}, u32[]{:S(2)}, u32[]{:S(2)}) async-start(f32[128,1,1152]{2,1,0:T(1,128)} %get-tuple-element.19), calls=%async_computation | async-start | bytes 1179648 | tf_op jit(solution)/shard_map/all_to_all | solution.py:629
  13.9 11.6 %all-to-all-done.codes_ref.told_ref = f32[128,1,1152]{2,1,0:T(1,128)S(1)} async-done(((f32[128,1,1152]{2,1,0:T(1,128)}), f32[128,1,1152]{2,1,0:T(1,128)S(1)}, u32[]{:S(2)}, u32[]{:S(2)}) %all-to-all-start) | async-done | bytes 589856 | tf_op jit(solution)/shard_map/all_to_all | solution.py:629
  25.5 0.0 copy-start.1
  25.5 0.8 copy-done.1
  26.3 13.0 %route.1 = (bf16[128,160,256]{2,1,0:T(8,128)(2,1)}, f32[128,1,1152]{2,1,0:T(1,128)}) custom-call(s32[1]{0:T(128)} %bitcast.1.tok_ref, f32[128,1,1152]{2,1,0:T(1,128)} %copy-done.1, bf16[160,8192]{1,0:T(8,128)(2,1)} %bitcast.11, f32[128,1,1152]{2,1,0:T(1,128)} %copy-done.1), custom_call_target="tpu_custom_call" | custom-call | tf_op jit(solution)/shard_map/route/pallas_call | solution.py:174
  39.3 7.6 %all-to-all-start.1 = ((bf16[128,160,256]{2,1,0:T(8,128)(2,1)}), bf16[128,160,256]{2,1,0:T(8,128)(2,1)}, u32[]{:S(2)}, u32[]{:S(2)}) async-start(bf16[128,160,256]{2,1,0:T(8,128)(2,1)} %get-tuple-element.20), calls=%async_computation.1 | async-start | bytes 20971520 | tf_op jit(solution)/shard_map/all_to_all | solution.py:629
  46.9 22.4 %place.1 = (f32[768,1024]{1,0:T(8,128)}, f32[8,1024]{1,0:T(8,128)}) custom-call(s32[1]{0:T(128)} %bitcast.owner_ref.me_ref, f32[128,1,1152]{2,1,0:T(1,128)} %get-tuple-element.21.told_ref), custom_call_target="tpu_custom_call" | custom-call | flops 100663296 | bytes 6291456 | tf_op jit(solution)/shard_map/place/pallas_call | solution.py:246
  69.3 113.5 %all-to-all-done.1 = bf16[128,160,256]{2,1,0:T(8,128)(2,1)} async-done(((bf16[128,160,256]{2,1,0:T(8,128)(2,1)}), bf16[128,160,256]{2,1,0:T(8,128)(2,1)}, u32[]{:S(2)}, u32[]{:S(2)}) %all-to-all-start.1) | async-done | bytes 10485792 | tf_op jit(solution)/shard_map/all_to_all | solution.py:629
  182.9 15.6 %score.1 = (f32[768,1024]{1,0:T(8,128)}, f32[8,1024]{1,0:T(8,128)}, f32[128,1,1152]{2,1,0:T(1,128)}) custom-call(bf16[768,5120]{1,0:T(8,128)(2,1)} %head_ref.3, bf16[4,5120,256]{2,1,0:T(8,128)(2,1)} %bitcast.6.rows_ref, f32[768,1024]{1,0:T(8,128)} %get-tuple-element.22.dense_ref, f32[8,1024]{1,0:T(8,128)} %get-tuple-element.23.facts_ref), custom_call_target="tpu_custom_call" | custom-call | tf_op jit(solution)/shard_map/score/pallas_call | solution.py:349
  198.5 4.9 %all-to-all-start.2 = ((f32[128,1,1152]{2,1,0:T(1,128)}), f32[128,1,1152]{2,1,0:T(1,128)S(1)}, u32[]{:S(2)}, u32[]{:S(2)}) async-start(f32[128,1,1152]{2,1,0:T(1,128)} %get-tuple-element.24), calls=%async_computation.2 | async-start | bytes 1179648 | tf_op jit(solution)/shard_map/all_to_all | solution.py:629
  203.4 6.2 %turn.1 = (f32[1024,768]{1,0:T(8,128)}, f32[1024,768]{1,0:T(8,128)}) custom-call(f32[768,1024]{1,0:T(8,128)} %get-tuple-element.26.part_ref, f32[768,1024]{1,0:T(8,128)} %get-tuple-element.22.dense_ref), custom_call_target="tpu_custom_call" | custom-call | flops 3145728 | bytes 12582912 | tf_op jit(solution)/shard_map/turn/pallas_call | solution.py:388
  209.6 5.5 %all-to-all-done.2.logs_ref = f32[128,1,1152]{2,1,0:T(1,128)S(1)} async-done(((f32[128,1,1152]{2,1,0:T(1,128)}), f32[128,1,1152]{2,1,0:T(1,128)S(1)}, u32[]{:S(2)}, u32[]{:S(2)}) %all-to-all-start.2) | async-done | bytes 589856 | tf_op jit(solution)/shard_map/all_to_all | solution.py:629
  215.1 0.0 copy-start.2
  215.1 0.8 copy-done.2
  215.9 16.1 %grad_parts.1 = (bf16[1024,5120]{1,0:T(8,128)(2,1)}, bf16[1024,768]{1,0:T(8,128)(2,1)}, f32[128,1,1152]{2,1,0:T(1,128)}) custom-call(f32[128,1,1152]{2,1,0:T(1,128)} %copy-done.2, f32[8,1024]{1,0:T(8,128)} %get-tuple-element.23.facts_ref, f32[8,1024]{1,0:T(8,128)} %get-tuple-element.25.own_ref, f32[1024,768]{1,0:T(8,128)} %get-tuple-element.27.part_ref, ...), custom_call_target="tpu_custom_call" | custom-call | tf_op jit(solution)/shard_map/grad_parts/pallas_call | solution.py:487
  232.0 0.0 copy-start
  232.0 7.7 %all-to-all-start.3 = ((bf16[128,8,5120]{2,1,0:T(8,128)(2,1)}), bf16[128,8,5120]{2,1,0:T(8,128)(2,1)}, u32[]{:S(2)}, u32[]{:S(2)}) async-start(bf16[128,8,5120]{2,1,0:T(8,128)(2,1)} %bitcast.10), calls=%async_computation.3 | async-start | bytes 20971520 | tf_op jit(solution)/shard_map/all_to_all | solution.py:629
  239.7 3.2 losses.1
  242.9 0.0 copy-done
  242.9 15.1 %grad_of_head.1 = bf16[768,5120]{1,0:T(8,128)(2,1)} custom-call(bf16[1024,768]{1,0:T(8,128)(2,1)S(1)} %copy-done, bf16[4,5120,256]{2,1,0:T(8,128)(2,1)} %bitcast.6.rows_ref), custom_call_target="tpu_custom_call" | custom-call | flops 8053063680 | bytes 18350080 | tf_op jit(solution)/shard_map/grad_of_head/pallas_call | solution.py:533
  258.0 114.7 %all-to-all-done.3 = bf16[128,8,5120]{2,1,0:T(8,128)(2,1)} async-done(((bf16[128,8,5120]{2,1,0:T(8,128)(2,1)}), bf16[128,8,5120]{2,1,0:T(8,128)(2,1)}, u32[]{:S(2)}, u32[]{:S(2)}) %all-to-all-start.3) | async-done | bytes 10485792 | tf_op jit(solution)/shard_map/all_to_all | solution.py:629
  372.7 6.8 %combine.1 = bf16[256,5120]{1,0:T(8,128)(2,1)} custom-call(bf16[256,1024]{1,0:T(8,128)(2,1)} %get-tuple-element.32.table_ref, bf16[1024,5120]{1,0:T(8,128)(2,1)} %bitcast.9.parts_ref), custom_call_target="tpu_custom_call" | custom-call | tf_op jit(solution)/shard_map/combine/pallas_call | solution.py:614
Async XLA Ops:
  3.7 21.8 %all-to-all-start = ((f32[128,1,1152]{2,1,0:T(1,128)}), f32[128,1,1152]{2,1,0:T(1,128)S(1)}, u32[]{:S(2)}, u32[]{:S(2)}) async-start(f32[128,1,1152]{2,1,0:T(1,128)} %get-tuple-element.19), calls=%async_computation | async-start | bytes 1179648 | tf_op jit(solution)/shard_map/all_to_all | solution.py:629
  25.5 0.8 copy-start.1
  39.3 143.5 %all-to-all-start.1 = ((bf16[128,160,256]{2,1,0:T(8,128)(2,1)}), bf16[128,160,256]{2,1,0:T(8,128)(2,1)}, u32[]{:S(2)}, u32[]{:S(2)}) async-start(bf16[128,160,256]{2,1,0:T(8,128)(2,1)} %get-tuple-element.20), calls=%async_computation.1 | async-start | bytes 20971520 | tf_op jit(solution)/shard_map/all_to_all | solution.py:629
  198.5 16.6 %all-to-all-start.2 = ((f32[128,1,1152]{2,1,0:T(1,128)}), f32[128,1,1152]{2,1,0:T(1,128)S(1)}, u32[]{:S(2)}, u32[]{:S(2)}) async-start(f32[128,1,1152]{2,1,0:T(1,128)} %get-tuple-element.24), calls=%async_computation.2 | async-start | bytes 1179648 | tf_op jit(solution)/shard_map/all_to_all | solution.py:629
  215.1 0.8 copy-start.2
  232.0 10.9 %copy-start = (bf16[1024,768]{1,0:T(8,128)(2,1)S(1)}, bf16[1024,768]{1,0:T(8,128)(2,1)}, u32[]{:S(2)}) copy-start(bf16[1024,768]{1,0:T(8,128)(2,1)} %get-tuple-element.34.weight_ref) | copy-start | bytes 4718596
  232.0 140.7 %all-to-all-start.3 = ((bf16[128,8,5120]{2,1,0:T(8,128)(2,1)}), bf16[128,8,5120]{2,1,0:T(8,128)(2,1)}, u32[]{:S(2)}, u32[]{:S(2)}) async-start(bf16[128,8,5120]{2,1,0:T(8,128)(2,1)} %bitcast.10), calls=%async_computation.3 | async-start | bytes 20971520 | tf_op jit(solution)/shard_map/all_to_all | solution.py:629

commit v8 on v7

--- a/solution.py
+++ b/solution.py
@@ -168,7 +168,7 @@
     owners = told.shape[0]
     tokens = total // blocks
     entries = 2 * tokens // per_tile
-    pairs = 4
+    pairs = 8
     steps = blocks // (2 * pairs)
     turn = 32
     return pl.pallas_call(

time: 380 us -> 381 us (level)
  no operation moved by 1% of the time
where the time goes in v8:
time: 381 us; the launch traced here: 380 us
  waiting for transfers between devices  245 us (64%)
  Pallas kernels  101 us (27%)
  starting transfers between devices  31 us (8%)
    all_to_all x4, waiting for transfers between devices, exchange(): lax.all_to_all(values, ('tok', 'voc'), split_axis=0, concat_axis=0, tiled...  245 us
    all_to_all x4, starting transfers between devices, exchange(): lax.all_to_all(values, ('tok', 'voc'), split_axis=0, concat_axis=0, tiled...  31 us
    pallas_call x1, Pallas kernels, place(): pl.pallas_call(functools.partial(place_kernel, per_tile), grid_spec=pltpu...  22.4 us
    pallas_call x1, Pallas kernels, grad_parts(): pl.pallas_call(functools.partial(part_kernel, per_tile), in_specs=[far] *...  16.1 us
    pallas_call x1, Pallas kernels, score(): pl.pallas_call(functools.partial(score_kernel, bounds), in_specs=[far, fa...  15.6 us
    pallas_call x1, Pallas kernels, grad_of_head(): pl.pallas_call(head_kernel, grid=(width // block,), in_specs=[pl.BlockSpe...  15.1 us
    pallas_call x1, Pallas kernels, route(): pl.pallas_call(functools.partial(route_kernel, per_tile), grid_spec=pltpu...  12.8 us
  transfers between devices with their start and end apart: 4, of which 4 were waited for; matrix products, arithmetic and copies ran while one was open for 0% of the time, Pallas kernels for 12%

profile of v8, /device:TPU:97, one launch (start us, length us, event | category | flops | bytes accessed | tf_op | source)
XLA Modules:
  0.0 379.9 jit_solution(14464460575359887141)
XLA Ops:
  0.6 3.1 announce.1
  3.7 10.2 %all-to-all-start = ((f32[128,1,1152]{2,1,0:T(1,128)}), f32[128,1,1152]{2,1,0:T(1,128)S(1)}, u32[]{:S(2)}, u32[]{:S(2)}) async-start(f32[128,1,1152]{2,1,0:T(1,128)} %get-tuple-element.19), calls=%async_computation | async-start | bytes 1179648 | tf_op jit(solution)/shard_map/all_to_all | solution.py:629
  13.9 11.6 %all-to-all-done.codes_ref.told_ref = f32[128,1,1152]{2,1,0:T(1,128)S(1)} async-done(((f32[128,1,1152]{2,1,0:T(1,128)}), f32[128,1,1152]{2,1,0:T(1,128)S(1)}, u32[]{:S(2)}, u32[]{:S(2)}) %all-to-all-start) | async-done | bytes 589856 | tf_op jit(solution)/shard_map/all_to_all | solution.py:629
  25.5 0.0 copy-start.1
  25.5 0.8 copy-done.1
  26.3 12.8 %route.1 = (bf16[128,160,256]{2,1,0:T(8,128)(2,1)}, f32[128,1,1152]{2,1,0:T(1,128)}) custom-call(s32[1]{0:T(128)} %bitcast.1.tok_ref, f32[128,1,1152]{2,1,0:T(1,128)} %copy-done.1, bf16[160,8192]{1,0:T(8,128)(2,1)} %bitcast.11, f32[128,1,1152]{2,1,0:T(1,128)} %copy-done.1), custom_call_target="tpu_custom_call" | custom-call | tf_op jit(solution)/shard_map/route/pallas_call | solution.py:174
  39.1 7.6 %all-to-all-start.1 = ((bf16[128,160,256]{2,1,0:T(8,128)(2,1)}), bf16[128,160,256]{2,1,0:T(8,128)(2,1)}, u32[]{:S(2)}, u32[]{:S(2)}) async-start(bf16[128,160,256]{2,1,0:T(8,128)(2,1)} %get-tuple-element.20), calls=%async_computation.1 | async-start | bytes 20971520 | tf_op jit(solution)/shard_map/all_to_all | solution.py:629
  46.7 22.4 %place.1 = (f32[768,1024]{1,0:T(8,128)}, f32[8,1024]{1,0:T(8,128)}) custom-call(s32[1]{0:T(128)} %bitcast.owner_ref.me_ref, f32[128,1,1152]{2,1,0:T(1,128)} %get-tuple-element.21.told_ref), custom_call_target="tpu_custom_call" | custom-call | flops 100663296 | bytes 6291456 | tf_op jit(solution)/shard_map/place/pallas_call | solution.py:246
  69.1 113.5 %all-to-all-done.1 = bf16[128,160,256]{2,1,0:T(8,128)(2,1)} async-done(((bf16[128,160,256]{2,1,0:T(8,128)(2,1)}), bf16[128,160,256]{2,1,0:T(8,128)(2,1)}, u32[]{:S(2)}, u32[]{:S(2)}) %all-to-all-start.1) | async-done | bytes 10485792 | tf_op jit(solution)/shard_map/all_to_all | solution.py:629
  182.6 15.6 %score.1 = (f32[768,1024]{1,0:T(8,128)}, f32[8,1024]{1,0:T(8,128)}, f32[128,1,1152]{2,1,0:T(1,128)}) custom-call(bf16[768,5120]{1,0:T(8,128)(2,1)} %head_ref.3, bf16[4,5120,256]{2,1,0:T(8,128)(2,1)} %bitcast.6.rows_ref, f32[768,1024]{1,0:T(8,128)} %get-tuple-element.22.dense_ref, f32[8,1024]{1,0:T(8,128)} %get-tuple-element.23.facts_ref), custom_call_target="tpu_custom_call" | custom-call | tf_op jit(solution)/shard_map/score/pallas_call | solution.py:349
  198.3 5.6 %all-to-all-start.2 = ((f32[128,1,1152]{2,1,0:T(1,128)}), f32[128,1,1152]{2,1,0:T(1,128)S(1)}, u32[]{:S(2)}, u32[]{:S(2)}) async-start(f32[128,1,1152]{2,1,0:T(1,128)} %get-tuple-element.24), calls=%async_computation.2 | async-start | bytes 1179648 | tf_op jit(solution)/shard_map/all_to_all | solution.py:629
  203.8 6.2 %turn.1 = (f32[1024,768]{1,0:T(8,128)}, f32[1024,768]{1,0:T(8,128)}) custom-call(f32[768,1024]{1,0:T(8,128)} %get-tuple-element.26.part_ref, f32[768,1024]{1,0:T(8,128)} %get-tuple-element.22.dense_ref), custom_call_target="tpu_custom_call" | custom-call | flops 3145728 | bytes 12582912 | tf_op jit(solution)/shard_map/turn/pallas_call | solution.py:388
  210.0 5.5 %all-to-all-done.2.logs_ref = f32[128,1,1152]{2,1,0:T(1,128)S(1)} async-done(((f32[128,1,1152]{2,1,0:T(1,128)}), f32[128,1,1152]{2,1,0:T(1,128)S(1)}, u32[]{:S(2)}, u32[]{:S(2)}) %all-to-all-start.2) | async-done | bytes 589856 | tf_op jit(solution)/shard_map/all_to_all | solution.py:629
  215.5 0.0 copy-start.2
  215.5 0.8 copy-done.2
  216.3 16.1 %grad_parts.1 = (bf16[1024,5120]{1,0:T(8,128)(2,1)}, bf16[1024,768]{1,0:T(8,128)(2,1)}, f32[128,1,1152]{2,1,0:T(1,128)}) custom-call(f32[128,1,1152]{2,1,0:T(1,128)} %copy-done.2, f32[8,1024]{1,0:T(8,128)} %get-tuple-element.23.facts_ref, f32[8,1024]{1,0:T(8,128)} %get-tuple-element.25.own_ref, f32[1024,768]{1,0:T(8,128)} %get-tuple-element.27.part_ref, ...), custom_call_target="tpu_custom_call" | custom-call | tf_op jit(solution)/shard_map/grad_parts/pallas_call | solution.py:487
  232.4 0.0 copy-start
  232.5 7.7 %all-to-all-start.3 = ((bf16[128,8,5120]{2,1,0:T(8,128)(2,1)}), bf16[128,8,5120]{2,1,0:T(8,128)(2,1)}, u32[]{:S(2)}, u32[]{:S(2)}) async-start(bf16[128,8,5120]{2,1,0:T(8,128)(2,1)} %bitcast.10), calls=%async_computation.3 | async-start | bytes 20971520 | tf_op jit(solution)/shard_map/all_to_all | solution.py:629
  240.1 3.2 losses.1
  243.3 0.0 copy-done
  243.3 15.1 %grad_of_head.1 = bf16[768,5120]{1,0:T(8,128)(2,1)} custom-call(bf16[1024,768]{1,0:T(8,128)(2,1)S(1)} %copy-done, bf16[4,5120,256]{2,1,0:T(8,128)(2,1)} %bitcast.6.rows_ref), custom_call_target="tpu_custom_call" | custom-call | flops 8053063680 | bytes 18350080 | tf_op jit(solution)/shard_map/grad_of_head/pallas_call | solution.py:533
  258.4 114.7 %all-to-all-done.3 = bf16[128,8,5120]{2,1,0:T(8,128)(2,1)} async-done(((bf16[128,8,5120]{2,1,0:T(8,128)(2,1)}), bf16[128,8,5120]{2,1,0:T(8,128)(2,1)}, u32[]{:S(2)}, u32[]{:S(2)}) %all-to-all-start.3) | async-done | bytes 10485792 | tf_op jit(solution)/shard_map/all_to_all | solution.py:629
  373.1 6.8 %combine.1 = bf16[256,5120]{1,0:T(8,128)(2,1)} custom-call(bf16[256,1024]{1,0:T(8,128)(2,1)} %get-tuple-element.32.table_ref, bf16[1024,5120]{1,0:T(8,128)(2,1)} %bitcast.9.parts_ref), custom_call_target="tpu_custom_call" | custom-call | tf_op jit(solution)/shard_map/combine/pallas_call | solution.py:614
Async XLA Ops:
  3.7 21.8 %all-to-all-start = ((f32[128,1,1152]{2,1,0:T(1,128)}), f32[128,1,1152]{2,1,0:T(1,128)S(1)}, u32[]{:S(2)}, u32[]{:S(2)}) async-start(f32[128,1,1152]{2,1,0:T(1,128)} %get-tuple-element.19), calls=%async_computation | async-start | bytes 1179648 | tf_op jit(solution)/shard_map/all_to_all | solution.py:629
  25.5 0.8 copy-start.1
  39.1 143.5 %all-to-all-start.1 = ((bf16[128,160,256]{2,1,0:T(8,128)(2,1)}), bf16[128,160,256]{2,1,0:T(8,128)(2,1)}, u32[]{:S(2)}, u32[]{:S(2)}) async-start(bf16[128,160,256]{2,1,0:T(8,128)(2,1)} %get-tuple-element.20), calls=%async_computation.1 | async-start | bytes 20971520 | tf_op jit(solution)/shard_map/all_to_all | solution.py:629
  198.3 17.2 %all-to-all-start.2 = ((f32[128,1,1152]{2,1,0:T(1,128)}), f32[128,1,1152]{2,1,0:T(1,128)S(1)}, u32[]{:S(2)}, u32[]{:S(2)}) async-start(f32[128,1,1152]{2,1,0:T(1,128)} %get-tuple-element.24), calls=%async_computation.2 | async-start | bytes 1179648 | tf_op jit(solution)/shard_map/all_to_all | solution.py:629
  215.5 0.8 copy-start.2
  232.4 10.9 %copy-start = (bf16[1024,768]{1,0:T(8,128)(2,1)S(1)}, bf16[1024,768]{1,0:T(8,128)(2,1)}, u32[]{:S(2)}) copy-start(bf16[1024,768]{1,0:T(8,128)(2,1)} %get-tuple-element.34.weight_ref) | copy-start | bytes 4718596
  232.5 140.7 %all-to-all-start.3 = ((bf16[128,8,5120]{2,1,0:T(8,128)(2,1)}), bf16[128,8,5120]{2,1,0:T(8,128)(2,1)}, u32[]{:S(2)}, u32[]{:S(2)}) async-start(bf16[128,8,5120]{2,1,0:T(8,128)(2,1)} %bitcast.10), calls=%async_computation.3 | async-start | bytes 20971520 | tf_op jit(solution)/shard_map/all_to_all | solution.py:629
